TPU v7x, 32 devices: a whole 2x2x4 slice. The times are simulated.
32 devices in a mesh: grp: 4 (over y, core), tile: 8 (over z, x).
Axes of the slice: x: 2, y: 2, z: 4, core: 2. Of those that a mesh axis runs over, the one named last changes fastest.
Arguments:
- amplitudes: bfloat16 [256, 4, 9216], P(('grp', 'tile')), may hold values from -6 to 6
- kept: int32 [256, 4], P(('grp', 'tile')), may hold values from 0 to 7, all different within a row; in each aligned block of 8 rows (0 to 7, 8 to 15, ...) at most 8 rows name the same one
- coef: bfloat16 [256], P(('grp', 'tile')), may hold values from -0.125 to 0.125
- ladder_factor: bfloat16 [8, 16, 96, 96], P('tile'), may hold values from -0.375 to 0.375
- cycle_integral_tiles: bfloat16 [8, 96, 96], P('tile'), may hold values from -0.625 to 0.625
Outputs:
- residual: bfloat16 [256, 4, 9216], P(('grp', 'tile'))
Inputs may be any that keep to these rules, and one draw needn't show every extreme that they name: `kept`: each row names 4 different tiles; in each aligned block of 8 rows (the pairs of one device) no tile is named by more than 8 rows, a bound that some block reaches.
All inputs are finite; a program needn't handle non-finite values.
Results may differ from a plain program's by a relative error of at most 0.0056.
Values may be sent and summed in bfloat16 or wider, within the bound.
No kernel may reach another device: no remote copies, remote signals or barrier semaphores. Data moves between devices by JAX's collectives and lax.ppermute only.
A program may use at most 128 MiB of HBM per device.

v0:
```python
import functools

import jax
import jax.numpy as jnp
from jax import lax
from jax.experimental import pallas as pl
from jax.experimental.pallas import tpu as pltpu
from jax.sharding import PartitionSpec as P

LANES = 128
ALL = ("grp", "tile")


def pack_factors(factors):
    count, width, _ = factors.shape
    quads = factors.reshape(count // 4, 4, width, width)
    spare = LANES - width
    pieces = [quads[:, 3, :, i * spare:(i + 1) * spare] for i in range(3)]
    packed = jnp.concatenate([quads[:, :3], jnp.stack(pieces, axis=1)], axis=-1)
    return packed.reshape(2, count // 8 * 3, width, LANES)


def unpack(refs, stacked, beside, width):
    spare = LANES - width
    lane = lax.broadcasted_iota(jnp.int32, (width, LANES), 1)
    number = 0
    for ref in refs:
        for quad in range(ref.shape[0] // 3):
            parts = [ref[quad * 3 + i] for i in range(3)]
            wide = [part.astype(jnp.float32) for part in parts]
            moved = [pltpu.roll(wide[i], spare * (i + 1), 1) for i in range(3)]
            fourth = jnp.where(lane < spare, moved[0], jnp.where(lane < 2 * spare, moved[1], moved[2]))
            parts.append(fourth.astype(jnp.bfloat16))
            for part in parts:
                stacked[number * width:(number + 1) * width, :] = part
                beside[:, number * LANES:(number + 1) * LANES] = part
                number += 1


def ladder_kernel(near, tiles, width, first_stage, kept_ref, me_ref, blocks_ref, *rest):
    if not first_stage:
        rest = rest[1:]
    factor_refs, total_ref = rest[:2 * len(near)], rest[2 * len(near)]
    table, counts, stacked, beside, grown = rest[2 * len(near) + 1:]
    rows = blocks_ref.shape[0]
    most = table.shape[0] // tiles
    me = me_ref[0]

    def clear(j, _):
        counts[j] = 0
        return 0

    lax.fori_loop(0, tiles, clear, 0)

    def fill(r, _):
        slot = kept_ref[r] ^ me
        n = counts[slot]
        table[slot * most + n] = r
        counts[slot] = n + 1
        return 0

    lax.fori_loop(0, rows, fill, 0)

    factor_count = stacked.shape[0] // width
    for number, slot in enumerate(near):
        count = counts[slot]

        @pl.when(count > 0)
        def _(number=number, slot=slot, count=count):
            unpack(factor_refs[2 * number:2 * number + 2], stacked, beside, width)

            def job(i, _):
                first = table[slot * most + 2 * i]
                second = table[slot * most + jnp.minimum(2 * i + 1, count - 1)]
                pair = jnp.concatenate([blocks_ref[first], blocks_ref[second]], axis=1)
                inner = jnp.dot(stacked[...], pair, preferred_element_type=jnp.float32)
                for f in range(factor_count):
                    part = inner[f * width:(f + 1) * width].astype(jnp.bfloat16)
                    grown[0:width, f * LANES:(f + 1) * LANES] = part[:, :LANES]
                    grown[width:2 * width, f * LANES:(f + 1) * LANES] = part[:, LANES:]
                total = lax.dot_general(
                    grown[...], beside[...], (((1,), (1,)), ((), ())), preferred_element_type=jnp.float32
                )
                total_ref[first] = total[:width]
                total_ref[second] = total[width:]
                return 0

            lax.fori_loop(0, (count + 1) // 2, job, 0)


SMEM, VMEM = pl.BlockSpec(memory_space=pltpu.SMEM), pl.BlockSpec(memory_space=pltpu.VMEM)


def ladder(near, kept, me, blocks, total, parts, tiles, width, most):
    rows = blocks.shape[0]
    factor_count = parts[0].shape[0] // 3 * 4 * 2
    carried = [] if total is None else [total]
    return pl.pallas_call(
        functools.partial(ladder_kernel, near, tiles, width, total is None),
        out_shape=jax.ShapeDtypeStruct((rows, width, width), jnp.float32),
        in_specs=[SMEM, SMEM] + [VMEM] * (1 + len(carried) + len(parts)),
        out_specs=VMEM,
        input_output_aliases={} if total is None else {3: 0},
        scratch_shapes=[
            pltpu.SMEM((tiles * most,), jnp.int32),
            pltpu.SMEM((tiles,), jnp.int32),
            pltpu.VMEM((factor_count * width, LANES), jnp.bfloat16),
            pltpu.VMEM((width, factor_count * LANES), jnp.bfloat16),
            pltpu.VMEM((2 * width, factor_count * LANES), jnp.bfloat16),
        ],
        compiler_params=pltpu.CompilerParams(vmem_limit_bytes=12 << 20),
        cost_estimate=pl.CostEstimate(
            flops=rows, bytes_accessed=rows, transcendentals=0
        ),
    )(kept, me, blocks, *carried, *parts)


def close_kernel(tiles, width, kept_ref, blocks_ref, total_ref, spread_ref, out_ref, hidden):
    groups = spread_ref.shape[0] // tiles
    hidden[:, width:, :] = jnp.zeros((tiles, LANES - width, LANES), jnp.bfloat16)
    for tile in range(tiles):
        pieces = [spread_ref[g * tiles + tile].astype(jnp.float32) for g in range(groups)]
        hidden[tile, :width, :] = jnp.concatenate(pieces, axis=0).astype(jnp.bfloat16)
    for r in range(blocks_ref.shape[0]):
        term = jnp.dot(blocks_ref[r, :width, :], hidden[kept_ref[r]], preferred_element_type=jnp.float32)
        out_ref[r] = (total_ref[r] + term[:, :width]).astype(jnp.bfloat16)


def close(kept, blocks, total, spread, tiles, width):
    rows = blocks.shape[0]
    return pl.pallas_call(
        functools.partial(close_kernel, tiles, width),
        out_shape=jax.ShapeDtypeStruct((rows, width, width), jnp.bfloat16),
        in_specs=[SMEM] + [VMEM] * 3,
        out_specs=VMEM,
        scratch_shapes=[pltpu.VMEM((tiles, LANES, LANES), jnp.bfloat16)],
        compiler_params=pltpu.CompilerParams(vmem_limit_bytes=16 << 20),
        cost_estimate=pl.CostEstimate(flops=rows * 2 * width**3, bytes_accessed=1 << 20, transcendentals=0),
    )(kept, blocks, total, spread)


def on_device(amplitudes, kept, coef, ladder_factor, cycle_integral_tiles):
    pairs, slots, flat = amplitudes.shape
    width = ladder_factor.shape[-1]
    tiles, groups = lax.axis_size("tile"), lax.axis_size("grp")
    across = 1 << ((tiles.bit_length() - 1) // 2)
    rows = pairs * slots
    me = lax.axis_index("tile")
    core = lax.axis_index("grp") % 2

    def to_tile(array, flip):
        return lax.ppermute(array, "tile", [(i, i ^ flip) for i in range(tiles)])

    def to_core(array):
        return lax.ppermute(array, "grp", [(i, i ^ 1) for i in range(groups)])

    block_list = amplitudes.reshape(rows, flat)
    names = kept.reshape(rows)
    weights = jnp.where(
        jnp.arange(tiles, dtype=jnp.int32)[:, None] == names[None, :], jnp.repeat(coef, slots)[None, :], jnp.zeros((), coef.dtype)
    )
    part_sum = jnp.dot(weights, block_list, preferred_element_type=jnp.float32)
    share = flat // groups
    shares = part_sum.reshape(tiles, groups, share).transpose(1, 0, 2).reshape(groups * tiles, share)
    arrived = lax.all_to_all(shares, ALL, split_axis=0, concat_axis=0, tiled=True)
    running = jnp.sum(arrived, axis=0).astype(jnp.bfloat16).reshape(width // groups, width)
    hidden = jnp.dot(running, cycle_integral_tiles[0], preferred_element_type=jnp.float32).astype(jnp.bfloat16)
    hidden = jnp.pad(hidden, ((0, 0), (0, LANES - width)))
    spread = lax.all_to_all(
        jnp.broadcast_to(hidden[None], (groups * tiles,) + hidden.shape), ALL, split_axis=0, concat_axis=0, tiled=True
    )

    packed = pack_factors(ladder_factor[0])
    mine = lax.dynamic_index_in_dim(packed, core, 0, keepdims=False)
    halves = {0: mine}
    for up in range(1, tiles // across):
        halves[up * across] = to_tile(mine, up * across)
    for up in range(tiles // across):
        source = halves[up * across]
        if up * across >= tiles // 2:
            source, _ = lax.optimization_barrier((source, hidden))
            halves[up * across] = source
        for side in range(1, across):
            halves[up * across + side] = to_tile(source, side)

    blocks = jnp.pad(block_list.reshape(rows, width, width), ((0, 0), (0, LANES - width), (0, LANES - width)))
    place = me.reshape(1)
    total = ladder((0,), names, place, blocks, None, [packed[0], packed[1]], tiles, width, pairs)
    for near in (tuple(range(1, tiles // 2)), tuple(range(tiles // 2, tiles))):
        parts = []
        for slot in near:
            parts += [halves[slot], to_core(halves[slot])]
        total, *parts = lax.optimization_barrier((total, *parts))
        total = ladder(near, names, place, blocks, total, parts, tiles, width, pairs)
    residual = close(names, blocks, total, spread, tiles, width)
    return residual.reshape(pairs, slots, flat)


def solution(mesh):
    in_specs = (
        P(("grp", "tile"), None, None),
        P(("grp", "tile"), None),
        P(("grp", "tile")),
        P("tile", None, None, None),
        P("tile", None, None),
    )
    out_specs = P(("grp", "tile"), None, None)
    return jax.shard_map(
        on_device, mesh=mesh, in_specs=in_specs, out_specs=out_specs, check_vma=False
    )
```

profile of v0, /device:TPU:0, one launch (start us, length us, event | category | flops | bytes accessed | tf_op | source)
XLA Modules:
  0.0 70.1 jit_solution(10396635359391482871)
XLA Ops:
  0.0 0.8 %copy.11 = s32[8,4]{1,0:T(8,128)S(1)} copy(s32[8,4]{0,1:T(4,128)} %param.6) | data formatting | bytes 256 | tf_op args[1]
  0.8 0.1 reshape.37.kept_ref
  0.8 1.2 %reshape.40 = bf16[32,9216]{1,0:T(8,128)(2,1)S(1)} reshape(bf16[8,4,9216]{2,1,0:T(4,128)(2,1)} %param.5) | data formatting | bytes 1179648 | tf_op jit(solution)/shard_map/reshape | solution.py:157
  2.1 0.7 %broadcast_in_dim.24 = bf16[8,4]{1,0:T(8,128)(2,1)S(1)} broadcast(bf16[8]{0:T(256)(128)(2,1)} %param.7), dimensions={0} | broadcast | bytes 80 | tf_op jit(solution)/shard_map/broadcast_in_dim | solution.py:160
  2.8 0.1 broadcast_in_dim.25
  2.9 0.2 convolution_bitcast_fusion
  3.1 1.0 %copy.17 = f32[32,1,2304]{2,1,0:T(1,128)} copy(f32[32,1,2304]{2,0,1:T(8,128)S(1)} %convolution_bitcast_fusion) | data formatting | bytes 589824 | tf_op jit(solution)/shard_map/all_to_all | solution.py:165
  4.1 7.3 %all-to-all-start = ((f32[32,1,2304]{2,1,0:T(1,128)}), f32[32,1,2304]{2,1,0:T(1,128)S(1)}, u32[]{:S(2)}, u32[]{:S(2)}) async-start(f32[32,1,2304]{2,1,0:T(1,128)} %copy.17), calls=%async_computation | async-start | bytes 589824 | tf_op jit(solution)/shard_map/all_to_all | solution.py:165
  11.5 0.2 copy.12
  11.8 0.1 maximum_maximum_fusion
  11.9 0.2 copy.18
  12.0 1.8 %collective-permute-start.2 = (bf16[6,96,128]{2,1,0:T(8,128)(2,1)S(1)}, bf16[6,96,128]{2,1,0:T(8,128)(2,1)S(1)}, u32[]{:S(2)}, u32[]{:S(2)}) collective-permute-start(bf16[6,96,128]{2,1,0:T(8,128)(2,1)S(1)} %bitcast.28), channel_id=1, source_target_pairs={{0,2},{1,3},{2,0},{3,1},{4,6},{5,7},{6,4},{7,5},{8,10},{9,11},{10,... | collective-permute-start | bytes 442376 | tf_op jit(solution)/shard_map/ppermute | solution.py:152
  13.9 1.5 %collective-permute-start = (bf16[6,96,128]{2,1,0:T(8,128)(2,1)S(1)}, bf16[6,96,128]{2,1,0:T(8,128)(2,1)S(1)}, u32[]{:S(2)}, u32[]{:S(2)}) collective-permute-start(bf16[6,96,128]{2,1,0:T(8,128)(2,1)S(1)} %bitcast.29), channel_id=1, source_target_pairs={{0,1},{1,0},{2,3},{3,2},{4,5},{5,4},{6,7},{7,6},{8,9},{9,8},{10,11... | collective-permute-start | bytes 442376 | tf_op jit(solution)/shard_map/ppermute | solution.py:152
  15.3 2.4 %collective-permute-start.10 = (bf16[6,96,128]{2,1,0:T(8,128)(2,1)S(1)}, bf16[6,96,128]{2,1,0:T(8,128)(2,1)S(1)}, u32[]{:S(2)}, u32[]{:S(2)}) collective-permute-start(bf16[6,96,128]{2,1,0:T(8,128)(2,1)S(1)} %bitcast.30), channel_id=1, source_target_pairs={{0,6},{1,7},{2,4},{3,5},{4,2},{5,3},{6,0},{7,1},{8,14},{9,15},{10,... | collective-permute-start | bytes 442376 | tf_op jit(solution)/shard_map/ppermute | solution.py:152
  17.7 0.1 collective-permute-start.6
  17.8 4.4 %collective-permute-done.2.rest_3_ = bf16[6,96,128]{2,1,0:T(8,128)(2,1)S(1)} collective-permute-done((bf16[6,96,128]{2,1,0:T(8,128)(2,1)S(1)}, bf16[6,96,128]{2,1,0:T(8,128)(2,1)S(1)}, u32[]{:S(2)}, u32[]{:S(2)}) %collective-permute-start.2) | collective-permute-done | bytes 147488 | tf_op jit(solution)/shard_map/ppermute | solution.py:152
  22.2 1.5 %collective-permute-start.4 = (bf16[6,96,128]{2,1,0:T(8,128)(2,1)S(1)}, bf16[6,96,128]{2,1,0:T(8,128)(2,1)}, u32[]{:S(2)}, u32[]{:S(2)}) collective-permute-start(bf16[6,96,128]{2,1,0:T(8,128)(2,1)S(1)} %collective-permute-done.2.rest_3_), channel_id=1, source_target_pairs={{0,1},{1,0},{2,3},{3,2},{4,5},{5,4},{6,7},{7,6},{8,9},{9,8},{10,11... | collective-permute-start | bytes 442376 | tf_op jit(solution)/shard_map/ppermute | solution.py:152
  23.7 0.5 collective-permute-start.1
  24.2 0.2 reduce_sum.9
  24.4 0.1 convert_element_type.21
  24.5 0.1 convolution_convert_fusion
  24.6 3.2 %collective-permute-done.10.rest_5_ = bf16[6,96,128]{2,1,0:T(8,128)(2,1)S(1)} collective-permute-done((bf16[6,96,128]{2,1,0:T(8,128)(2,1)S(1)}, bf16[6,96,128]{2,1,0:T(8,128)(2,1)S(1)}, u32[]{:S(2)}, u32[]{:S(2)}) %collective-permute-start.10) | collective-permute-done | bytes 147488 | tf_op jit(solution)/shard_map/ppermute | solution.py:152
  27.8 1.5 %collective-permute-start.12 = (bf16[6,96,128]{2,1,0:T(8,128)(2,1)S(1)}, bf16[6,96,128]{2,1,0:T(8,128)(2,1)}, u32[]{:S(2)}, u32[]{:S(2)}) collective-permute-start(bf16[6,96,128]{2,1,0:T(8,128)(2,1)S(1)} %collective-permute-done.10.rest_5_), channel_id=1, source_target_pairs={{0,1},{1,0},{2,3},{3,2},{4,5},{5,4},{6,7},{7,6},{8,9},{9,8},{10,11... | collective-permute-start | bytes 442376 | tf_op jit(solution)/shard_map/ppermute | solution.py:152
  29.3 4.9 %collective-permute-done.6.rest_1_ = bf16[6,96,128]{2,1,0:T(8,128)(2,1)S(1)} collective-permute-done((bf16[6,96,128]{2,1,0:T(8,128)(2,1)S(1)}, bf16[6,96,128]{2,1,0:T(8,128)(2,1)S(1)}, u32[]{:S(2)}, u32[]{:S(2)}) %collective-permute-start.6) | collective-permute-done | bytes 147488 | tf_op jit(solution)/shard_map/ppermute | solution.py:152
  34.2 1.5 %collective-permute-start.8 = (bf16[6,96,128]{2,1,0:T(8,128)(2,1)S(1)}, bf16[6,96,128]{2,1,0:T(8,128)(2,1)}, u32[]{:S(2)}, u32[]{:S(2)}) collective-permute-start(bf16[6,96,128]{2,1,0:T(8,128)(2,1)S(1)} %collective-permute-done.6.rest_1_), channel_id=1, source_target_pairs={{0,1},{1,0},{2,3},{3,2},{4,5},{5,4},{6,7},{7,6},{8,9},{9,8},{10,11... | collective-permute-start | bytes 442376 | tf_op jit(solution)/shard_map/ppermute | solution.py:152
  35.6 0.7 %broadcast_in_dim.28 = bf16[32,24,128]{2,1,0:T(8,128)(2,1)} broadcast(bf16[24,128]{1,0:T(8,128)(2,1)S(1)} %pad.9), dimensions={1,2} | broadcast | bytes 202752 | tf_op jit(solution)/shard_map/broadcast_in_dim | solution.py:170
  36.3 2.7 %all-to-all-start.1 = ((bf16[32,24,128]{2,1,0:T(8,128)(2,1)}), bf16[32,24,128]{2,1,0:T(8,128)(2,1)S(1)}, u32[]{:S(2)}, u32[]{:S(2)}) async-start(bf16[32,24,128]{2,1,0:T(8,128)(2,1)} %broadcast_in_dim.28), calls=%async_computation.1 | async-start | bytes 393216 | tf_op jit(solution)/shard_map/all_to_all | solution.py:169
  39.1 0.6 reshape_reshape.3
  39.7 0.3 collective-permute-start.5
  40.0 0.3 collective-permute-start.11
  40.3 0.3 collective-permute-start.7
  40.5 0.3 collective-permute-start.13
  40.8 0.3 collective-permute-start.9
  41.1 0.2 copy.13
  41.3 0.2 copy.14
  41.4 0.3 pad.8.blocks_ref
  41.7 2.8 %shard_map.55.rest_0_ = f32[32,96,96]{2,1,0:T(8,128)S(1)} custom-call(s32[32]{0:T(128)S(1)} %reshape.37.kept_ref, s32[1]{0:T(128)} %bitcast.me_ref, bf16[32,128,128]{2,1,0:T(8,128)(2,1)S(1)} %pad.8.blocks_ref, bf16[6,96,128]{2,1,0:T(8,128)(2,1)S(1)} %bitcast.22, bf16[6,96,128]{2,1,0:T(8,128)(2,1)S(1)} %bitcast.23), custom_call_target="tpu_custom_call" | custom-call | flops 32 | bytes 32 | tf_op jit(solution)/shard_map/pallas_call | solution.py:98
  44.6 0.9 %copy-done.4 = bf16[6,96,128]{2,1,0:T(8,128)(2,1)S(1)} copy-done((bf16[6,96,128]{2,1,0:T(8,128)(2,1)S(1)}, bf16[6,96,128]{2,1,0:T(8,128)(2,1)}, u32[]{:S(2)}) %copy-start.4) | copy-done | bytes 147480
  45.5 0.9 %copy-done.6 = bf16[6,96,128]{2,1,0:T(8,128)(2,1)S(1)} copy-done((bf16[6,96,128]{2,1,0:T(8,128)(2,1)S(1)}, bf16[6,96,128]{2,1,0:T(8,128)(2,1)}, u32[]{:S(2)}) %copy-start.6) | copy-done | bytes 147480
  46.4 0.9 %copy-done.8 = bf16[6,96,128]{2,1,0:T(8,128)(2,1)S(1)} copy-done((bf16[6,96,128]{2,1,0:T(8,128)(2,1)S(1)}, bf16[6,96,128]{2,1,0:T(8,128)(2,1)}, u32[]{:S(2)}) %copy-start.8) | copy-done | bytes 147480
  47.3 0.9 %copy-done.10 = bf16[6,96,128]{2,1,0:T(8,128)(2,1)S(1)} copy-done((bf16[6,96,128]{2,1,0:T(8,128)(2,1)S(1)}, bf16[6,96,128]{2,1,0:T(8,128)(2,1)}, u32[]{:S(2)}) %copy-start.10) | copy-done | bytes 147480
  48.2 8.4 %shard_map.56.rest_0_ = f32[32,96,96]{2,1,0:T(8,128)S(1)} custom-call(s32[32]{0:T(128)S(1)} %reshape.37.kept_ref, s32[1]{0:T(128)} %bitcast.me_ref, bf16[32,128,128]{2,1,0:T(8,128)(2,1)S(1)} %pad.8.blocks_ref, f32[32,96,96]{2,1,0:T(8,128)S(1)} %shard_map.55.rest_0_, bf16[6,96,128]{2,1,0:T(8,128)(2,1)S(1)} %copy-done.6, ...), custom_call_target="tpu_custom_call", output_to_operand_aliasing={{}: (3, {})} | custom-call | flops 32 | bytes 32 | tf_op jit(solution)/shard_map/pallas_call | solution.py:98
  56.6 8.9 %shard_map.57.total_ref = f32[32,96,96]{2,1,0:T(8,128)S(1)} custom-call(s32[32]{0:T(128)S(1)} %reshape.37.kept_ref, s32[1]{0:T(128)} %bitcast.me_ref, bf16[32,128,128]{2,1,0:T(8,128)(2,1)S(1)} %pad.8.blocks_ref, f32[32,96,96]{2,1,0:T(8,128)S(1)} %shard_map.56.rest_0_, ...), custom_call_target="tpu_custom_call", output_to_operand_aliasing={{}: (3, {})} | custom-call | flops 32 | bytes 32 | tf_op jit(solution)/shard_map/pallas_call | solution.py:98
  65.5 0.0 copy-start.1
  65.5 0.7 copy-done.1
  66.2 0.9 %copy-done.2 = bf16[32,24,128]{2,1,0:T(8,128)(2,1)S(1)} copy-done((bf16[32,24,128]{2,1,0:T(8,128)(2,1)S(1)}, bf16[32,24,128]{2,1,0:T(8,128)(2,1)}, u32[]{:S(2)}) %copy-start.2) | copy-done | bytes 196632
  67.1 1.0 %shard_map.58 = bf16[32,96,96]{2,1,0:T(8,128)(2,1)S(1)} custom-call(s32[32]{0:T(128)S(1)} %reshape.37.kept_ref, bf16[32,128,128]{2,1,0:T(8,128)(2,1)S(1)} %pad.8.blocks_ref, f32[32,96,96]{2,1,0:T(8,128)S(1)} %shard_map.57.total_ref, bf16[32,24,128]{2,1,0:T(8,128)(2,1)S(1)} %copy-done.2), custom_call_target="tpu_custom_call" | custom-call | flops 56623104 | bytes 1048576 | tf_op jit(solution)/shard_map/pallas_call | solution.py:131
  68.2 1.9 %reshape.41 = bf16[8,4,9216]{2,1,0:T(4,128)(2,1)} reshape(bf16[32,96,96]{2,1,0:T(8,128)(2,1)S(1)} %shard_map.58) | data formatting | bytes 1179648 | tf_op jit(solution)/shard_map/reshape | solution.py:196
  (38 shorter events, 0.2 us)
Async XLA Ops:
  0.0 24.5 %copy-start = (bf16[1,96,96]{2,1,0:T(8,128)(2,1)S(1)}, bf16[1,96,96]{2,1,0:T(8,128)(2,1)}, u32[]{:S(2)}) copy-start(bf16[1,96,96]{2,1,0:T(8,128)(2,1)} %param.9) | copy-start | bytes 55300
  0.8 10.6 %copy-start.12 = (bf16[1,16,96,96]{3,2,1,0:T(8,128)(2,1)S(1)}, bf16[1,16,96,96]{3,2,1,0:T(8,128)(2,1)}, u32[]{:S(2)}) copy-start(bf16[1,16,96,96]{3,2,1,0:T(8,128)(2,1)} %param.8) | copy-start | bytes 884740
  4.1 20.1 %all-to-all-start = ((f32[32,1,2304]{2,1,0:T(1,128)}), f32[32,1,2304]{2,1,0:T(1,128)S(1)}, u32[]{:S(2)}, u32[]{:S(2)}) async-start(f32[32,1,2304]{2,1,0:T(1,128)} %copy.17), calls=%async_computation | async-start | bytes 589824 | tf_op jit(solution)/shard_map/all_to_all | solution.py:165
  11.7 27.4 %copy-start.11 = (bf16[8,4,9216]{2,1,0:T(4,128)(2,1)S(1)}, bf16[8,4,9216]{2,1,0:T(4,128)(2,1)}, u32[]{:S(2)}) copy-start(bf16[8,4,9216]{2,1,0:T(4,128)(2,1)} %param.5) | copy-start | bytes 1769476
  12.0 10.2 %collective-permute-start.2 = (bf16[6,96,128]{2,1,0:T(8,128)(2,1)S(1)}, bf16[6,96,128]{2,1,0:T(8,128)(2,1)S(1)}, u32[]{:S(2)}, u32[]{:S(2)}) collective-permute-start(bf16[6,96,128]{2,1,0:T(8,128)(2,1)S(1)} %bitcast.28), channel_id=1, source_target_pairs={{0,2},{1,3},{2,0},{3,1},{4,6},{5,7},{6,4},{7,5},{8,10},{9,11},{10,... | collective-permute-start | bytes 442376 | tf_op jit(solution)/shard_map/ppermute | solution.py:152
  13.9 9.8 %collective-permute-start = (bf16[6,96,128]{2,1,0:T(8,128)(2,1)S(1)}, bf16[6,96,128]{2,1,0:T(8,128)(2,1)S(1)}, u32[]{:S(2)}, u32[]{:S(2)}) collective-permute-start(bf16[6,96,128]{2,1,0:T(8,128)(2,1)S(1)} %bitcast.29), channel_id=1, source_target_pairs={{0,1},{1,0},{2,3},{3,2},{4,5},{5,4},{6,7},{7,6},{8,9},{9,8},{10,11... | collective-permute-start | bytes 442376 | tf_op jit(solution)/shard_map/ppermute | solution.py:152
  15.3 12.4 %collective-permute-start.10 = (bf16[6,96,128]{2,1,0:T(8,128)(2,1)S(1)}, bf16[6,96,128]{2,1,0:T(8,128)(2,1)S(1)}, u32[]{:S(2)}, u32[]{:S(2)}) collective-permute-start(bf16[6,96,128]{2,1,0:T(8,128)(2,1)S(1)} %bitcast.30), channel_id=1, source_target_pairs={{0,6},{1,7},{2,4},{3,5},{4,2},{5,3},{6,0},{7,1},{8,14},{9,15},{10,... | collective-permute-start | bytes 442376 | tf_op jit(solution)/shard_map/ppermute | solution.py:152
  17.7 16.5 %collective-permute-start.6 = (bf16[6,96,128]{2,1,0:T(8,128)(2,1)S(1)}, bf16[6,96,128]{2,1,0:T(8,128)(2,1)S(1)}, u32[]{:S(2)}, u32[]{:S(2)}) collective-permute-start(bf16[6,96,128]{2,1,0:T(8,128)(2,1)S(1)} %bitcast.31), channel_id=1, source_target_pairs={{0,4},{1,5},{2,6},{3,7},{4,0},{5,1},{6,2},{7,3},{8,12},{9,13},{10,... | collective-permute-start | bytes 442376 | tf_op jit(solution)/shard_map/ppermute | solution.py:152
  22.2 18.9 %copy-start.3 = (bf16[6,96,128]{2,1,0:T(8,128)(2,1)}, bf16[6,96,128]{2,1,0:T(8,128)(2,1)S(1)}, u32[]{:S(2)}) copy-start(bf16[6,96,128]{2,1,0:T(8,128)(2,1)S(1)} %collective-permute-done.2.rest_3_) | copy-start | bytes 442372
  22.2 17.5 %collective-permute-start.4 = (bf16[6,96,128]{2,1,0:T(8,128)(2,1)S(1)}, bf16[6,96,128]{2,1,0:T(8,128)(2,1)}, u32[]{:S(2)}, u32[]{:S(2)}) collective-permute-start(bf16[6,96,128]{2,1,0:T(8,128)(2,1)S(1)} %collective-permute-done.2.rest_3_), channel_id=1, source_target_pairs={{0,1},{1,0},{2,3},{3,2},{4,5},{5,4},{6,7},{7,6},{8,9},{9,8},{10,11... | collective-permute-start | bytes 442376 | tf_op jit(solution)/shard_map/ppermute | solution.py:152
  23.7 16.6 %collective-permute-start.3 = (bf16[6,96,128]{2,1,0:T(8,128)(2,1)S(1)}, bf16[6,96,128]{2,1,0:T(8,128)(2,1)S(1)}, u32[]{:S(2)}, u32[]{:S(2)}) collective-permute-start(bf16[6,96,128]{2,1,0:T(8,128)(2,1)S(1)} %collective-permute-done.2.rest_3_), channel_id=1, source_target_pairs={{0,8},{8,0},{16,24},{24,16},{1,9},{9,1},{17,25},{25,17},{2,10},{10... | collective-permute-start | bytes 442376 | tf_op jit(solution)/shard_map/ppermute | solution.py:155
  23.7 17.6 %copy-start.5 = (bf16[6,96,128]{2,1,0:T(8,128)(2,1)}, bf16[6,96,128]{2,1,0:T(8,128)(2,1)S(1)}, u32[]{:S(2)}) copy-start(bf16[6,96,128]{2,1,0:T(8,128)(2,1)S(1)} %collective-permute-done.rest_1_) | copy-start | bytes 442372
  23.7 16.3 %collective-permute-start.1 = (bf16[6,96,128]{2,1,0:T(8,128)(2,1)S(1)}, bf16[6,96,128]{2,1,0:T(8,128)(2,1)S(1)}, u32[]{:S(2)}, u32[]{:S(2)}) collective-permute-start(bf16[6,96,128]{2,1,0:T(8,128)(2,1)S(1)} %collective-permute-done.rest_1_), channel_id=1, source_target_pairs={{0,8},{8,0},{16,24},{24,16},{1,9},{9,1},{17,25},{25,17},{2,10},{10... | collective-permute-start | bytes 442376 | tf_op jit(solution)/shard_map/ppermute | solution.py:155
  27.8 12.8 %collective-permute-start.12 = (bf16[6,96,128]{2,1,0:T(8,128)(2,1)S(1)}, bf16[6,96,128]{2,1,0:T(8,128)(2,1)}, u32[]{:S(2)}, u32[]{:S(2)}) collective-permute-start(bf16[6,96,128]{2,1,0:T(8,128)(2,1)S(1)} %collective-permute-done.10.rest_5_), channel_id=1, source_target_pairs={{0,1},{1,0},{2,3},{3,2},{4,5},{5,4},{6,7},{7,6},{8,9},{9,8},{10,11... | collective-permute-start | bytes 442376 | tf_op jit(solution)/shard_map/ppermute | solution.py:152
  34.2 6.6 %collective-permute-start.8 = (bf16[6,96,128]{2,1,0:T(8,128)(2,1)S(1)}, bf16[6,96,128]{2,1,0:T(8,128)(2,1)}, u32[]{:S(2)}, u32[]{:S(2)}) collective-permute-start(bf16[6,96,128]{2,1,0:T(8,128)(2,1)S(1)} %collective-permute-done.6.rest_1_), channel_id=1, source_target_pairs={{0,1},{1,0},{2,3},{3,2},{4,5},{5,4},{6,7},{7,6},{8,9},{9,8},{10,11... | collective-permute-start | bytes 442376 | tf_op jit(solution)/shard_map/ppermute | solution.py:152
  36.3 29.2 %all-to-all-start.1 = ((bf16[32,24,128]{2,1,0:T(8,128)(2,1)}), bf16[32,24,128]{2,1,0:T(8,128)(2,1)S(1)}, u32[]{:S(2)}, u32[]{:S(2)}) async-start(bf16[32,24,128]{2,1,0:T(8,128)(2,1)} %broadcast_in_dim.28), calls=%async_computation.1 | async-start | bytes 393216 | tf_op jit(solution)/shard_map/all_to_all | solution.py:169
  39.7 4.8 %collective-permute-start.5 = (bf16[6,96,128]{2,1,0:T(8,128)(2,1)}, bf16[6,96,128]{2,1,0:T(8,128)(2,1)}, u32[]{:S(2)}, u32[]{:S(2)}) collective-permute-start(bf16[6,96,128]{2,1,0:T(8,128)(2,1)} %collective-permute-done.4.rest_5_), channel_id=1, source_target_pairs={{0,8},{8,0},{16,24},{24,16},{1,9},{9,1},{17,25},{25,17},{2,10},{10... | collective-permute-start | bytes 442376 | tf_op jit(solution)/shard_map/ppermute | solution.py:155
  40.0 1.2 %copy-start.9 = (bf16[6,96,128]{2,1,0:T(8,128)(2,1)}, bf16[6,96,128]{2,1,0:T(8,128)(2,1)S(1)}, u32[]{:S(2)}) copy-start(bf16[6,96,128]{2,1,0:T(8,128)(2,1)S(1)} %collective-permute-done.1.rest_2_) | copy-start | bytes 442372
  40.0 16.6 %collective-permute-start.11 = (bf16[6,96,128]{2,1,0:T(8,128)(2,1)S(1)}, bf16[6,96,128]{2,1,0:T(8,128)(2,1)}, u32[]{:S(2)}, u32[]{:S(2)}) collective-permute-start(bf16[6,96,128]{2,1,0:T(8,128)(2,1)S(1)} %collective-permute-done.10.rest_5_), channel_id=1, source_target_pairs={{0,8},{8,0},{16,24},{24,16},{1,9},{9,1},{17,25},{25,17},{2,10},{10... | collective-permute-start | bytes 442376 | tf_op jit(solution)/shard_map/ppermute | solution.py:155
  40.3 1.0 %copy-start.7 = (bf16[6,96,128]{2,1,0:T(8,128)(2,1)}, bf16[6,96,128]{2,1,0:T(8,128)(2,1)S(1)}, u32[]{:S(2)}) copy-start(bf16[6,96,128]{2,1,0:T(8,128)(2,1)S(1)} %collective-permute-done.3.rest_4_) | copy-start | bytes 442372
  40.3 16.3 %collective-permute-start.7 = (bf16[6,96,128]{2,1,0:T(8,128)(2,1)S(1)}, bf16[6,96,128]{2,1,0:T(8,128)(2,1)}, u32[]{:S(2)}, u32[]{:S(2)}) collective-permute-start(bf16[6,96,128]{2,1,0:T(8,128)(2,1)S(1)} %collective-permute-done.6.rest_1_), channel_id=1, source_target_pairs={{0,8},{8,0},{16,24},{24,16},{1,9},{9,1},{17,25},{25,17},{2,10},{10... | collective-permute-start | bytes 442376 | tf_op jit(solution)/shard_map/ppermute | solution.py:155
  40.5 16.1 %collective-permute-start.13 = (bf16[6,96,128]{2,1,0:T(8,128)(2,1)}, bf16[6,96,128]{2,1,0:T(8,128)(2,1)}, u32[]{:S(2)}, u32[]{:S(2)}) collective-permute-start(bf16[6,96,128]{2,1,0:T(8,128)(2,1)} %collective-permute-done.12.rest_7_), channel_id=1, source_target_pairs={{0,8},{8,0},{16,24},{24,16},{1,9},{9,1},{17,25},{25,17},{2,10},{10... | collective-permute-start | bytes 442376 | tf_op jit(solution)/shard_map/ppermute | solution.py:155
  40.8 15.8 %collective-permute-start.9 = (bf16[6,96,128]{2,1,0:T(8,128)(2,1)}, bf16[6,96,128]{2,1,0:T(8,128)(2,1)}, u32[]{:S(2)}, u32[]{:S(2)}) collective-permute-start(bf16[6,96,128]{2,1,0:T(8,128)(2,1)} %collective-permute-done.8.rest_3_), channel_id=1, source_target_pairs={{0,8},{8,0},{16,24},{24,16},{1,9},{9,1},{17,25},{25,17},{2,10},{10... | collective-permute-start | bytes 442376 | tf_op jit(solution)/shard_map/ppermute | solution.py:155
  44.6 0.9 %copy-start.4 = (bf16[6,96,128]{2,1,0:T(8,128)(2,1)S(1)}, bf16[6,96,128]{2,1,0:T(8,128)(2,1)}, u32[]{:S(2)}) copy-start(bf16[6,96,128]{2,1,0:T(8,128)(2,1)} %copy-done.3) | copy-start | bytes 442372
  45.5 0.9 %copy-start.6 = (bf16[6,96,128]{2,1,0:T(8,128)(2,1)S(1)}, bf16[6,96,128]{2,1,0:T(8,128)(2,1)}, u32[]{:S(2)}) copy-start(bf16[6,96,128]{2,1,0:T(8,128)(2,1)} %copy-done.5) | copy-start | bytes 442372
  46.4 0.9 %copy-start.8 = (bf16[6,96,128]{2,1,0:T(8,128)(2,1)S(1)}, bf16[6,96,128]{2,1,0:T(8,128)(2,1)}, u32[]{:S(2)}) copy-start(bf16[6,96,128]{2,1,0:T(8,128)(2,1)} %copy-done.7) | copy-start | bytes 442372
  47.3 0.9 %copy-start.10 = (bf16[6,96,128]{2,1,0:T(8,128)(2,1)S(1)}, bf16[6,96,128]{2,1,0:T(8,128)(2,1)}, u32[]{:S(2)}) copy-start(bf16[6,96,128]{2,1,0:T(8,128)(2,1)} %copy-done.9) | copy-start | bytes 442372
  65.5 0.7 copy-start.1
  66.2 0.9 %copy-start.2 = (bf16[32,24,128]{2,1,0:T(8,128)(2,1)S(1)}, bf16[32,24,128]{2,1,0:T(8,128)(2,1)}, u32[]{:S(2)}) copy-start(bf16[32,24,128]{2,1,0:T(8,128)(2,1)} %copy-done.1) | copy-start | bytes 589828
where the time goes:
time: 70.6 us; the launch traced here: 70.1 us
  starting transfers between devices  22 us (31%)
  Pallas kernels  21.1 us (30%)
  local copies, waits for them, and re-layouts  13.6 us (19%)
  waiting for transfers between devices  12.5 us (18%)
    pallas_call x3, Pallas kernels, ladder(): pl.pallas_call(functools.partial(ladder_kernel, near, tiles, width, total...  20 us
    ppermute x7, waiting for transfers between devices, to_tile(): return lax.ppermute(array, 'tile', [(i, i ^ flip) for i in range(tiles)])  12.5 us
    ppermute x7, starting transfers between devices, to_tile(): return lax.ppermute(array, 'tile', [(i, i ^ flip) for i in range(tiles)])  10.1 us
    all_to_all x1, starting transfers between devices, on_device(): lax.all_to_all(shares, ALL, split_axis=0, concat_axis=0, tiled=True)  7.3 us
    unnamed x29, local copies, waits for them, and re-layouts  6.4 us
    all_to_all x1, starting transfers between devices, on_device(): lax.all_to_all(jnp.broadcast_to(hidden[None], (groups * tiles,) + hidden....  2.72 us
    reshape x1, local copies, waits for them, and re-layouts, on_device(): return residual.reshape(pairs, slots, flat)  1.94 us
    ppermute x7, starting transfers between devices, to_core(): return lax.ppermute(array, 'grp', [(i, i ^ 1) for i in range(groups)])  1.85 us
  transfers between devices with their start and end apart: 16, of which 3 were waited for; matrix products, arithmetic and copies ran while one was open for 4% of the time, Pallas kernels for 29%

commit v1 on v0

v1 whole, which is shorter than its diff:
```python
import functools

import jax
import jax.numpy as jnp
from jax import lax
from jax.experimental import pallas as pl
from jax.experimental.pallas import tpu as pltpu
from jax.sharding import PartitionSpec as P

LANES = 128
ALL = ("grp", "tile")


def pack_factors(factors):
    count, width, _ = factors.shape
    quads = factors.reshape(count // 4, 4, width, width)
    spare = LANES - width
    pieces = [quads[:, 3, :, i * spare:(i + 1) * spare] for i in range(3)]
    packed = jnp.concatenate([quads[:, :3], jnp.stack(pieces, axis=1)], axis=-1)
    return packed.reshape(2, count // 8 * 3, width, LANES)


def unpack(refs, stacked, beside, width):
    spare = LANES - width
    lane = lax.broadcasted_iota(jnp.int32, (width, LANES), 1)
    number = 0
    for ref in refs:
        for quad in range(ref.shape[0] // 3):
            parts = [ref[quad * 3 + i] for i in range(3)]
            wide = [part.astype(jnp.float32) for part in parts]
            moved = [pltpu.roll(wide[i], spare * (i + 1), 1) for i in range(3)]
            fourth = jnp.where(lane < spare, moved[0], jnp.where(lane < 2 * spare, moved[1], moved[2]))
            parts.append(fourth.astype(jnp.bfloat16))
            for part in parts:
                stacked[number * width:(number + 1) * width, :] = part
                beside[:, number * LANES:(number + 1) * LANES] = part
                number += 1


def ladder_kernel(near, tiles, width, carried, kept_ref, me_ref, blocks_ref, *rest):
    rest = rest[carried:]
    factor_refs, total_ref = rest[:2 * len(near)], rest[2 * len(near)]
    table, counts, jobs, landed, stacked, beside, grown, sems = rest[2 * len(near) + 1:]
    rows = blocks_ref.shape[0]
    most = table.shape[0] // tiles
    me = me_ref[0]
    copies = [pltpu.make_async_copy(ref, landed.at[i], sems.at[i]) for i, ref in enumerate(factor_refs)]
    for copy in copies:
        copy.start()

    def clear(j, _):
        counts[j] = 0
        return 0

    lax.fori_loop(0, tiles, clear, 0)

    def fill(r, _):
        slot = kept_ref[r] ^ me
        n = counts[slot]
        table[slot * most + n] = r
        counts[slot] = n + 1
        return 0

    lax.fori_loop(0, rows, fill, 0)

    last = jnp.int32(0)
    for number, slot in enumerate(near):
        count = counts[slot]

        def add(i, at, number=number, slot=slot, count=count):
            jobs[3 * at] = number
            jobs[3 * at + 1] = table[slot * most + 2 * i]
            jobs[3 * at + 2] = table[slot * most + jnp.minimum(2 * i + 1, count - 1)]
            return at + 1

        last = lax.fori_loop(0, (count + 1) // 2, add, last)
    for number in range(len(near)):
        copies[2 * number].wait()
        copies[2 * number + 1].wait()
        unpack((landed.at[2 * number], landed.at[2 * number + 1]), stacked.at[number], beside.at[number], width)

    factor_count = stacked.shape[1] // width
    step = 4

    def grow(at, side):
        number = jobs[3 * at]
        pair = jnp.concatenate([blocks_ref[jobs[3 * at + 1]], blocks_ref[jobs[3 * at + 2]]], axis=1)
        for q in range(0, factor_count, step):
            inner = jnp.dot(
                stacked[number, q * width:(q + step) * width], pair, preferred_element_type=jnp.float32
            ).astype(jnp.bfloat16)
            for f in range(step):
                part, lanes = inner[f * width:(f + 1) * width], slice((q + f) * LANES, (q + f + 1) * LANES)
                grown[side, 0:width, lanes] = part[:, :LANES]
                grown[side, width:2 * width, lanes] = part[:, LANES:]

    def reduce(at, side):
        total = lax.dot_general(
            grown[side], beside[jobs[3 * at]], (((1,), (1,)), ((), ())), preferred_element_type=jnp.float32
        )
        total_ref[jobs[3 * at + 1]] = total[:width]
        total_ref[jobs[3 * at + 2]] = total[width:]

    def two(i, _):
        first, second = 2 * i, jnp.minimum(2 * i + 1, last - 1)
        grow(first, 0)
        grow(second, 1)
        reduce(first, 0)
        reduce(second, 1)
        return 0

    lax.fori_loop(0, (last + 1) // 2, two, 0)


SMEM, VMEM = pl.BlockSpec(memory_space=pltpu.SMEM), pl.BlockSpec(memory_space=pltpu.VMEM)
FREE = pl.BlockSpec(memory_space=pl.ANY)


def ladder(near, kept, me, blocks, total, parts, tiles, width, most, cost):
    rows = blocks.shape[0]
    factor_count = parts[0].shape[0] // 3 * 4 * 2
    carried = [] if total is None else [total]
    return pl.pallas_call(
        functools.partial(ladder_kernel, near, tiles, width, len(carried)),
        out_shape=jax.ShapeDtypeStruct((rows, width, width), jnp.float32),
        in_specs=[SMEM, SMEM] + [VMEM] * (1 + len(carried)) + [FREE] * len(parts),
        out_specs=VMEM,
        input_output_aliases={} if total is None else {3: 0},
        scratch_shapes=[
            pltpu.SMEM((tiles * most,), jnp.int32),
            pltpu.SMEM((tiles,), jnp.int32),
            pltpu.SMEM((3 * (rows + tiles),), jnp.int32),
            pltpu.VMEM((len(parts),) + parts[0].shape, jnp.bfloat16),
            pltpu.VMEM((len(near), factor_count * width, LANES), jnp.bfloat16),
            pltpu.VMEM((len(near), width, factor_count * LANES), jnp.bfloat16),
            pltpu.VMEM((2, 2 * width, factor_count * LANES), jnp.bfloat16),
            pltpu.SemaphoreType.DMA((len(parts),)),
        ],
        compiler_params=pltpu.CompilerParams(vmem_limit_bytes=(10 << 20) + (len(near) << 21)),
        cost_estimate=pl.CostEstimate(flops=cost, bytes_accessed=rows, transcendentals=0),
    )(kept, me, blocks, *carried, *parts)


def close_kernel(tiles, width, kept_ref, blocks_ref, total_ref, spread_ref, out_ref, landed, hidden, sem):
    groups = spread_ref.shape[0] // tiles
    copy = pltpu.make_async_copy(spread_ref, landed, sem)
    copy.start()
    hidden[:, width:, :] = jnp.zeros((tiles, LANES - width, LANES), jnp.bfloat16)
    copy.wait()
    for tile in range(tiles):
        pieces = [landed[g * tiles + tile].astype(jnp.float32) for g in range(groups)]
        hidden[tile, :width, :] = jnp.concatenate(pieces, axis=0).astype(jnp.bfloat16)
    for r in range(blocks_ref.shape[0]):
        term = jnp.dot(blocks_ref[r, :width, :], hidden[kept_ref[r]], preferred_element_type=jnp.float32)
        out_ref[r] = (total_ref[r] + term[:, :width]).astype(jnp.bfloat16)


def close(kept, blocks, total, spread, tiles, width):
    rows = blocks.shape[0]
    return pl.pallas_call(
        functools.partial(close_kernel, tiles, width),
        out_shape=jax.ShapeDtypeStruct((rows, width, width), jnp.bfloat16),
        in_specs=[SMEM] + [VMEM] * 2 + [FREE],
        out_specs=VMEM,
        scratch_shapes=[
            pltpu.VMEM(spread.shape, jnp.bfloat16),
            pltpu.VMEM((tiles, LANES, LANES), jnp.bfloat16),
            pltpu.SemaphoreType.DMA,
        ],
        compiler_params=pltpu.CompilerParams(vmem_limit_bytes=16 << 20),
        cost_estimate=pl.CostEstimate(flops=rows, bytes_accessed=rows, transcendentals=0),
    )(kept, blocks, total, spread)


def on_device(amplitudes, kept, coef, ladder_factor, cycle_integral_tiles):
    pairs, slots, flat = amplitudes.shape
    width = ladder_factor.shape[-1]
    tiles, groups = lax.axis_size("tile"), lax.axis_size("grp")
    across = 1 << ((tiles.bit_length() - 1) // 2)
    rows = pairs * slots
    me = lax.axis_index("tile")
    core = lax.axis_index("grp") % 2

    def to_tile(array, flip):
        return lax.ppermute(array, "tile", [(i, i ^ flip) for i in range(tiles)])

    def to_core(array):
        return lax.ppermute(array, "grp", [(i, i ^ 1) for i in range(groups)])

    block_list = amplitudes.reshape(rows, flat)
    names = kept.reshape(rows)
    weights = jnp.where(
        jnp.arange(tiles, dtype=jnp.int32)[:, None] == names[None, :], jnp.repeat(coef, slots)[None, :], jnp.zeros((), coef.dtype)
    )
    part_sum = jnp.dot(weights, block_list, preferred_element_type=jnp.float32)
    share = flat // groups
    shares = part_sum.reshape(tiles, groups, share).transpose(1, 0, 2).reshape(groups * tiles, share)
    arrived = lax.all_to_all(shares, ALL, split_axis=0, concat_axis=0, tiled=True)
    running = jnp.sum(arrived, axis=0).astype(jnp.bfloat16).reshape(width // groups, width)
    hidden = jnp.dot(running, cycle_integral_tiles[0], preferred_element_type=jnp.float32).astype(jnp.bfloat16)
    hidden = jnp.pad(hidden, ((0, 0), (0, LANES - width)))
    spread = lax.all_to_all(
        jnp.broadcast_to(hidden[None], (groups * tiles,) + hidden.shape), ALL, split_axis=0, concat_axis=0, tiled=True
    )

    blocks = jnp.pad(block_list.reshape(rows, width, width), ((0, 0), (0, LANES - width), (0, LANES - width)))
    place = me.reshape(1)
    packed = pack_factors(ladder_factor[0])
    mine = lax.dynamic_index_in_dim(packed, core, 0, keepdims=False)
    half = tiles // 2
    halves = {0: mine}
    for up in range(across, tiles, across):
        halves[up] = to_tile(mine, up)
    total = ladder((0,), names, place, blocks, None, [packed[0], packed[1]], tiles, width, pairs, rows)

    def cross(starts, gate):
        for up in starts:
            source = halves[up]
            if up:
                source, _ = lax.optimization_barrier((source, gate))
                halves[up] = source
            for side in range(1, across):
                halves[up + side] = to_tile(source, side)

    def stage(near, total, gate, cost):
        parts = []
        for slot in near:
            parts += [halves[slot], to_core(halves[slot])]
        total, _, *parts = lax.optimization_barrier((total, gate, *parts))
        return ladder(near, names, place, blocks, total, parts, tiles, width, pairs, cost)

    cross(range(0, half, across), total)
    early = tuple(range(1, across + 1))
    total = stage(early, total, hidden, 30 * 10**9)
    cross(range(half, tiles, across), total)
    total = stage(tuple(s for s in range(1, tiles) if s not in early), total, total, rows)
    residual = close(names, blocks, total, spread, tiles, width)
    return residual.reshape(pairs, slots, flat)


def solution(mesh):
    in_specs = (
        P(("grp", "tile"), None, None),
        P(("grp", "tile"), None),
        P(("grp", "tile")),
        P("tile", None, None, None),
        P("tile", None, None),
    )
    out_specs = P(("grp", "tile"), None, None)
    return jax.shard_map(
        on_device, mesh=mesh, in_specs=in_specs, out_specs=out_specs, check_vma=False
    )
```

time: 70.6 us -> 64.4 us (0.912)
  waiting for transfers between devices: 12.5 us -> 8.07 us
  Pallas kernels: 21.1 us -> 17.8 us
  starting transfers between devices: 22 us -> 23 us
  other arithmetic: 0.29 us -> 1.24 us
    ppermute x7, waiting for transfers between devices: 12.5 us -> 6.7 us  [to_tile(): return lax.ppermute(array, 'tile', [(i, i ^ flip) for i in range(tiles)])]
    pallas_call x3, Pallas kernels: 20 us -> 16.5 us  [ladder(): pl.pallas_call(functools.partial(ladder_kernel, near, tiles, width, len(c...]
    all_to_all x1, starting transfers between devices: 2.72 us -> 5.52 us  [on_device(): lax.all_to_all(jnp.broadcast_to(hidden[None], (groups * tiles,) + hidden....]
    ppermute x7, waiting for transfers between devices: 0.02 us -> 1.37 us  [to_core(): return lax.ppermute(array, 'grp', [(i, i ^ 1) for i in range(groups)])]
    ppermute x7, starting transfers between devices: 1.85 us -> 0.76 us  [to_core(): return lax.ppermute(array, 'grp', [(i, i ^ 1) for i in range(groups)])]
    reduce_sum x1, other arithmetic: 0.2 us -> 1.15 us  [on_device(): jnp.sum(arrived, axis=0).astype(jnp.bfloat16)]
    ppermute x7, starting transfers between devices: 10.1 us -> 9.28 us  [to_tile(): return lax.ppermute(array, 'tile', [(i, i ^ flip) for i in range(tiles)])]
    unnamed x29 -> x21, local copies, waits for them, and re-layouts: 6.4 us -> 5.88 us
  transfers between devices with their start and end apart: 16 -> 16, of which waited for: 3 -> 3; matrix products, arithmetic and copies ran while one was open for 4% -> 7% of each run, Pallas kernels for 29% -> 26%
where the time goes in v1:
time: 64.4 us; the launch traced here: 63.8 us
  starting transfers between devices  23 us (36%)
  Pallas kernels  17.8 us (28%)
  local copies, waits for them, and re-layouts  13.1 us (20%)
  waiting for transfers between devices  8.07 us (13%)
  other arithmetic  1.24 us (2%)
    pallas_call x3, Pallas kernels, ladder(): pl.pallas_call(functools.partial(ladder_kernel, near, tiles, width, len(c...  16.5 us
    ppermute x7, starting transfers between devices, to_tile(): return lax.ppermute(array, 'tile', [(i, i ^ flip) for i in range(tiles)])  9.28 us
    all_to_all x1, starting transfers between devices, on_device(): lax.all_to_all(shares, ALL, split_axis=0, concat_axis=0, tiled=True)  7.41 us
    ppermute x7, waiting for transfers between devices, to_tile(): return lax.ppermute(array, 'tile', [(i, i ^ flip) for i in range(tiles)])  6.7 us
    unnamed x21, local copies, waits for them, and re-layouts  5.88 us
    all_to_all x1, starting transfers between devices, on_device(): lax.all_to_all(jnp.broadcast_to(hidden[None], (groups * tiles,) + hidden....  5.52 us
    reshape x1, local copies, waits for them, and re-layouts, on_device(): return residual.reshape(pairs, slots, flat)  1.94 us
    ppermute x7, waiting for transfers between devices, to_core(): return lax.ppermute(array, 'grp', [(i, i ^ 1) for i in range(groups)])  1.37 us
  transfers between devices with their start and end apart: 16, of which 3 were waited for; matrix products, arithmetic and copies ran while one was open for 7% of the time, Pallas kernels for 26%

profile of v1, /device:TPU:0, one launch (start us, length us, event | category | flops | bytes accessed | tf_op | source)
XLA Modules:
  0.0 63.8 jit_solution(5350241600932231786)
XLA Ops:
  0.0 0.8 %copy.11 = s32[8,4]{1,0:T(8,128)S(1)} copy(s32[8,4]{0,1:T(4,128)} %param.6) | data formatting | bytes 256 | tf_op args[1]
  0.8 0.1 reshape.37.kept_ref
  0.8 1.2 %reshape.39 = bf16[32,9216]{1,0:T(8,128)(2,1)S(1)} reshape(bf16[8,4,9216]{2,1,0:T(4,128)(2,1)} %param.5) | data formatting | bytes 1179648 | tf_op jit(solution)/shard_map/reshape | solution.py:190
  2.1 0.7 %broadcast_in_dim.24 = bf16[8,4]{1,0:T(8,128)(2,1)S(1)} broadcast(bf16[8]{0:T(256)(128)(2,1)} %param.7), dimensions={0} | broadcast | bytes 80 | tf_op jit(solution)/shard_map/broadcast_in_dim | solution.py:193
  2.8 0.1 broadcast_in_dim.25
  2.9 0.2 convolution_bitcast_fusion
  3.1 1.0 %copy.16 = f32[32,1,2304]{2,1,0:T(1,128)} copy(f32[32,1,2304]{2,0,1:T(8,128)S(1)} %convolution_bitcast_fusion) | data formatting | bytes 589824 | tf_op jit(solution)/shard_map/all_to_all | solution.py:198
  4.1 7.4 %all-to-all-start = ((f32[32,1,2304]{2,1,0:T(1,128)}), f32[32,1,2304]{2,1,0:T(1,128)}, u32[]{:S(2)}, u32[]{:S(2)}) async-start(f32[32,1,2304]{2,1,0:T(1,128)} %copy.16), calls=%async_computation | async-start | bytes 589824 | tf_op jit(solution)/shard_map/all_to_all | solution.py:198
  11.6 0.0 copy-start.7
  11.6 0.2 copy.12
  11.9 0.1 maximum_maximum_fusion
  12.0 0.8 %copy.18 = bf16[1,6,96,128]{3,2,1,0:T(8,128)(2,1)} copy(bf16[1,6,96,128]{2,3,1,0:T(8,128)(2,1)S(1)} %constant_dynamic-slice_fusion) | data formatting | bytes 294912
  12.8 1.7 %collective-permute-start.2 = (bf16[6,96,128]{2,1,0:T(8,128)(2,1)}, bf16[6,96,128]{2,1,0:T(8,128)(2,1)}, u32[]{:S(2)}, u32[]{:S(2)}) collective-permute-start(bf16[6,96,128]{2,1,0:T(8,128)(2,1)} %bitcast.10), channel_id=1, source_target_pairs={{0,2},{1,3},{2,0},{3,1},{4,6},{5,7},{6,4},{7,5},{8,10},{9,11},{10,... | collective-permute-start | bytes 442376 | tf_op jit(solution)/shard_map/ppermute | solution.py:185
  14.5 1.5 %collective-permute-start = (bf16[6,96,128]{2,1,0:T(8,128)(2,1)}, bf16[6,96,128]{2,1,0:T(8,128)(2,1)}, u32[]{:S(2)}, u32[]{:S(2)}) collective-permute-start(bf16[6,96,128]{2,1,0:T(8,128)(2,1)} %bitcast.10), channel_id=1, source_target_pairs={{0,1},{1,0},{2,3},{3,2},{4,5},{5,4},{6,7},{7,6},{8,9},{9,8},{10,11... | collective-permute-start | bytes 442376 | tf_op jit(solution)/shard_map/ppermute | solution.py:185
  16.0 2.4 %collective-permute-start.10 = (bf16[6,96,128]{2,1,0:T(8,128)(2,1)}, bf16[6,96,128]{2,1,0:T(8,128)(2,1)S(1)}, u32[]{:S(2)}, u32[]{:S(2)}) collective-permute-start(bf16[6,96,128]{2,1,0:T(8,128)(2,1)} %bitcast.10), channel_id=1, source_target_pairs={{0,6},{1,7},{2,4},{3,5},{4,2},{5,3},{6,0},{7,1},{8,14},{9,15},{10,... | collective-permute-start | bytes 442376 | tf_op jit(solution)/shard_map/ppermute | solution.py:185
  18.3 0.1 collective-permute-start.6
  18.4 0.6 reshape_reshape.3
  19.1 0.2 copy.13
  19.2 0.2 copy.14
  19.4 0.3 pad.8.blocks_ref
  19.7 2.6 %shard_map.55.rest_0_ = f32[32,96,96]{2,1,0:T(8,128)S(1)} custom-call(s32[32]{0:T(128)S(1)} %reshape.37.kept_ref, s32[1]{0:T(128)} %bitcast.me_ref, bf16[32,128,128]{2,1,0:T(8,128)(2,1)S(1)} %pad.8.blocks_ref, bf16[6,96,128]{2,1,0:T(8,128)(2,1)S(1)} %bitcast.22, bf16[6,96,128]{2,1,0:T(8,128)(2,1)S(1)} %bitcast.23), custom_call_target="tpu_custom_call" | custom-call | flops 32 | bytes 32 | tf_op jit(solution)/shard_map/pallas_call | solution.py:123
  22.3 0.0 collective-permute-done.2.rest_3_
  22.3 0.1 collective-permute-start.3
  22.4 1.6 %collective-permute-start.4 = (bf16[6,96,128]{2,1,0:T(8,128)(2,1)}, bf16[6,96,128]{2,1,0:T(8,128)(2,1)S(1)}, u32[]{:S(2)}, u32[]{:S(2)}) collective-permute-start(bf16[6,96,128]{2,1,0:T(8,128)(2,1)} %collective-permute-done.2.rest_3_), channel_id=1, source_target_pairs={{0,1},{1,0},{2,3},{3,2},{4,5},{5,4},{6,7},{7,6},{8,9},{9,8},{10,11... | collective-permute-start | bytes 442376 | tf_op jit(solution)/shard_map/ppermute | solution.py:185
  24.0 0.2 collective-permute-start.1
  24.2 1.1 %reduce_sum.9 = bf16[2304]{0:T(1024)(128)(2,1)S(1)} reduce(f32[32,1,2304]{2,1,0:T(1,128)} %all-to-all-done, f32[]{:T(128)} %constant.26.clone.1), dimensions={0,1}, to_apply=%region_0.1 | reduce | flops 71424 | bytes 299524 | tf_op jit(solution)/shard_map/reduce_sum | solution.py:199
  25.3 0.1 convert_element_type.21
  25.4 0.1 convolution_convert_fusion
  25.6 0.0 collective-permute-done.1.rest_2_
  25.6 0.7 %copy-done.5 = bf16[6,96,128]{2,1,0:T(8,128)(2,1)} copy-done((bf16[6,96,128]{2,1,0:T(8,128)(2,1)}, bf16[6,96,128]{2,1,0:T(8,128)(2,1)S(1)}, u32[]{:S(2)}) %copy-start.5) | copy-done | bytes 147480
  26.3 0.7 %broadcast_in_dim.28 = bf16[32,24,128]{2,1,0:T(8,128)(2,1)} broadcast(bf16[24,128]{1,0:T(8,128)(2,1)S(1)} %pad.9), dimensions={1,2} | broadcast | bytes 202752 | tf_op jit(solution)/shard_map/broadcast_in_dim | solution.py:203
  27.0 5.5 %all-to-all-start.1 = ((bf16[32,24,128]{2,1,0:T(8,128)(2,1)}), bf16[32,24,128]{2,1,0:T(8,128)(2,1)S(1)}, u32[]{:S(2)}, u32[]{:S(2)}) async-start(bf16[32,24,128]{2,1,0:T(8,128)(2,1)} %broadcast_in_dim.28), calls=%async_computation.1 | async-start | bytes 393216 | tf_op jit(solution)/shard_map/all_to_all | solution.py:202
  32.5 0.9 %copy-done.4 = bf16[6,96,128]{2,1,0:T(8,128)(2,1)S(1)} copy-done((bf16[6,96,128]{2,1,0:T(8,128)(2,1)S(1)}, bf16[6,96,128]{2,1,0:T(8,128)(2,1)}, u32[]{:S(2)}) %copy-start.4) | copy-done | bytes 147480
  33.4 0.9 %copy-done.6 = bf16[6,96,128]{2,1,0:T(8,128)(2,1)S(1)} copy-done((bf16[6,96,128]{2,1,0:T(8,128)(2,1)S(1)}, bf16[6,96,128]{2,1,0:T(8,128)(2,1)}, u32[]{:S(2)}) %copy-start.6) | copy-done | bytes 147480
  34.3 3.9 %shard_map.56.rest_0_ = f32[32,96,96]{2,1,0:T(8,128)S(1)} custom-call(s32[32]{0:T(128)S(1)} %reshape.37.kept_ref, s32[1]{0:T(128)} %bitcast.me_ref, bf16[32,128,128]{2,1,0:T(8,128)(2,1)S(1)} %pad.8.blocks_ref, f32[32,96,96]{2,1,0:T(8,128)S(1)} %shard_map.55.rest_0_, ...), custom_call_target="tpu_custom_call", output_to_operand_aliasing={{}: (3, {})} | custom-call | flops 30000001024 | bytes 32 | tf_op jit(solution)/shard_map/pallas_call | solution.py:123
  38.2 1.8 %collective-permute-start.12 = (bf16[6,96,128]{2,1,0:T(8,128)(2,1)S(1)}, bf16[6,96,128]{2,1,0:T(8,128)(2,1)S(1)}, u32[]{:S(2)}, u32[]{:S(2)}) collective-permute-start(bf16[6,96,128]{2,1,0:T(8,128)(2,1)S(1)} %collective-permute-done.10.rest_7_), channel_id=1, source_target_pairs={{0,1},{1,0},{2,3},{3,2},{4,5},{5,4},{6,7},{7,6},{8,9},{9,8},{10,11... | collective-permute-start | bytes 442376 | tf_op jit(solution)/shard_map/ppermute | solution.py:185
  40.0 0.3 collective-permute-start.8
  40.3 0.5 collective-permute-start.11
  40.8 0.0 collective-permute-start.7
  40.8 4.1 %collective-permute-done.12.rest_9_ = bf16[6,96,128]{2,1,0:T(8,128)(2,1)S(1)} collective-permute-done((bf16[6,96,128]{2,1,0:T(8,128)(2,1)S(1)}, bf16[6,96,128]{2,1,0:T(8,128)(2,1)S(1)}, u32[]{:S(2)}, u32[]{:S(2)}) %collective-permute-start.12) | collective-permute-done | bytes 147488 | tf_op jit(solution)/shard_map/ppermute | solution.py:185
  44.9 2.6 %collective-permute-done.8.rest_5_ = bf16[6,96,128]{2,1,0:T(8,128)(2,1)S(1)} collective-permute-done((bf16[6,96,128]{2,1,0:T(8,128)(2,1)S(1)}, bf16[6,96,128]{2,1,0:T(8,128)(2,1)S(1)}, u32[]{:S(2)}, u32[]{:S(2)}) %collective-permute-start.8) | collective-permute-done | bytes 147488 | tf_op jit(solution)/shard_map/ppermute | solution.py:185
  47.5 1.3 %collective-permute-done.9.rest_6_ = bf16[6,96,128]{2,1,0:T(8,128)(2,1)S(1)} collective-permute-done((bf16[6,96,128]{2,1,0:T(8,128)(2,1)S(1)}, bf16[6,96,128]{2,1,0:T(8,128)(2,1)S(1)}, u32[]{:S(2)}, u32[]{:S(2)}) %collective-permute-start.9) | collective-permute-done | bytes 147488 | tf_op jit(solution)/shard_map/ppermute | solution.py:188
  48.9 10.1 %shard_map.57.total_ref = f32[32,96,96]{2,1,0:T(8,128)S(1)} custom-call(s32[32]{0:T(128)S(1)} %reshape.37.kept_ref, s32[1]{0:T(128)} %bitcast.me_ref, bf16[32,128,128]{2,1,0:T(8,128)(2,1)S(1)} %pad.8.blocks_ref, f32[32,96,96]{2,1,0:T(8,128)S(1)} %shard_map.56.rest_0_, ...), custom_call_target="tpu_custom_call", output_to_operand_aliasing={{}: (3, {})} | custom-call | flops 32 | bytes 32 | tf_op jit(solution)/shard_map/pallas_call | solution.py:123
  58.9 0.0 copy-start.1
  58.9 0.7 %copy-done.1 = bf16[32,24,128]{2,1,0:T(8,128)(2,1)} copy-done((bf16[32,24,128]{2,1,0:T(8,128)(2,1)}, bf16[32,24,128]{2,1,0:T(8,128)(2,1)S(1)}, u32[]{:S(2)}) %copy-start.1) | copy-done | bytes 196632
  59.6 0.9 %copy-done.2 = bf16[32,24,128]{2,1,0:T(8,128)(2,1)S(1)} copy-done((bf16[32,24,128]{2,1,0:T(8,128)(2,1)S(1)}, bf16[32,24,128]{2,1,0:T(8,128)(2,1)}, u32[]{:S(2)}) %copy-start.2) | copy-done | bytes 196632
  60.5 1.3 %shard_map.58 = bf16[32,96,96]{2,1,0:T(8,128)(2,1)S(1)} custom-call(s32[32]{0:T(128)S(1)} %reshape.37.kept_ref, bf16[32,128,128]{2,1,0:T(8,128)(2,1)S(1)} %pad.8.blocks_ref, f32[32,96,96]{2,1,0:T(8,128)S(1)} %shard_map.57.total_ref, bf16[32,24,128]{2,1,0:T(8,128)(2,1)S(1)} %copy-done.2), custom_call_target="tpu_custom_call" | custom-call | flops 32 | bytes 32 | tf_op jit(solution)/shard_map/pallas_call | solution.py:160
  61.8 1.9 %reshape.41 = bf16[8,4,9216]{2,1,0:T(4,128)(2,1)} reshape(bf16[32,96,96]{2,1,0:T(8,128)(2,1)S(1)} %shard_map.58) | data formatting | bytes 1179648 | tf_op jit(solution)/shard_map/reshape | solution.py:238
  (30 shorter events, 0.1 us)
Async XLA Ops:
  0.0 25.4 %copy-start = (bf16[1,96,96]{2,1,0:T(8,128)(2,1)S(1)}, bf16[1,96,96]{2,1,0:T(8,128)(2,1)}, u32[]{:S(2)}) copy-start(bf16[1,96,96]{2,1,0:T(8,128)(2,1)} %param.9) | copy-start | bytes 55300
  0.8 10.7 %copy-start.8 = (bf16[1,16,96,96]{3,2,1,0:T(8,128)(2,1)S(1)}, bf16[1,16,96,96]{3,2,1,0:T(8,128)(2,1)}, u32[]{:S(2)}) copy-start(bf16[1,16,96,96]{3,2,1,0:T(8,128)(2,1)} %param.8) | copy-start | bytes 884740
  4.1 20.0 %all-to-all-start = ((f32[32,1,2304]{2,1,0:T(1,128)}), f32[32,1,2304]{2,1,0:T(1,128)}, u32[]{:S(2)}, u32[]{:S(2)}) async-start(f32[32,1,2304]{2,1,0:T(1,128)} %copy.16), calls=%async_computation | async-start | bytes 589824 | tf_op jit(solution)/shard_map/all_to_all | solution.py:198
  11.6 6.8 %copy-start.7 = (bf16[8,4,9216]{2,1,0:T(4,128)(2,1)S(1)}, bf16[8,4,9216]{2,1,0:T(4,128)(2,1)}, u32[]{:S(2)}) copy-start(bf16[8,4,9216]{2,1,0:T(4,128)(2,1)} %param.5) | copy-start | bytes 1769476
  12.8 9.5 %collective-permute-start.2 = (bf16[6,96,128]{2,1,0:T(8,128)(2,1)}, bf16[6,96,128]{2,1,0:T(8,128)(2,1)}, u32[]{:S(2)}, u32[]{:S(2)}) collective-permute-start(bf16[6,96,128]{2,1,0:T(8,128)(2,1)} %bitcast.10), channel_id=1, source_target_pairs={{0,2},{1,3},{2,0},{3,1},{4,6},{5,7},{6,4},{7,5},{8,10},{9,11},{10,... | collective-permute-start | bytes 442376 | tf_op jit(solution)/shard_map/ppermute | solution.py:185
  14.5 9.5 %collective-permute-start = (bf16[6,96,128]{2,1,0:T(8,128)(2,1)}, bf16[6,96,128]{2,1,0:T(8,128)(2,1)}, u32[]{:S(2)}, u32[]{:S(2)}) collective-permute-start(bf16[6,96,128]{2,1,0:T(8,128)(2,1)} %bitcast.10), channel_id=1, source_target_pairs={{0,1},{1,0},{2,3},{3,2},{4,5},{5,4},{6,7},{7,6},{8,9},{9,8},{10,11... | collective-permute-start | bytes 442376 | tf_op jit(solution)/shard_map/ppermute | solution.py:185
  16.0 22.2 %collective-permute-start.10 = (bf16[6,96,128]{2,1,0:T(8,128)(2,1)}, bf16[6,96,128]{2,1,0:T(8,128)(2,1)S(1)}, u32[]{:S(2)}, u32[]{:S(2)}) collective-permute-start(bf16[6,96,128]{2,1,0:T(8,128)(2,1)} %bitcast.10), channel_id=1, source_target_pairs={{0,6},{1,7},{2,4},{3,5},{4,2},{5,3},{6,0},{7,1},{8,14},{9,15},{10,... | collective-permute-start | bytes 442376 | tf_op jit(solution)/shard_map/ppermute | solution.py:185
  18.3 21.7 %collective-permute-start.6 = (bf16[6,96,128]{2,1,0:T(8,128)(2,1)}, bf16[6,96,128]{2,1,0:T(8,128)(2,1)S(1)}, u32[]{:S(2)}, u32[]{:S(2)}) collective-permute-start(bf16[6,96,128]{2,1,0:T(8,128)(2,1)} %bitcast.10), channel_id=1, source_target_pairs={{0,4},{1,5},{2,6},{3,7},{4,0},{5,1},{6,2},{7,3},{8,12},{9,13},{10,... | collective-permute-start | bytes 442376 | tf_op jit(solution)/shard_map/ppermute | solution.py:185
  22.3 3.2 %collective-permute-start.3 = (bf16[6,96,128]{2,1,0:T(8,128)(2,1)}, bf16[6,96,128]{2,1,0:T(8,128)(2,1)S(1)}, u32[]{:S(2)}, u32[]{:S(2)}) collective-permute-start(bf16[6,96,128]{2,1,0:T(8,128)(2,1)} %collective-permute-done.2.rest_3_), channel_id=1, source_target_pairs={{0,8},{8,0},{16,24},{24,16},{1,9},{9,1},{17,25},{25,17},{2,10},{10... | collective-permute-start | bytes 442376 | tf_op jit(solution)/shard_map/ppermute | solution.py:188
  22.4 17.9 %collective-permute-start.4 = (bf16[6,96,128]{2,1,0:T(8,128)(2,1)}, bf16[6,96,128]{2,1,0:T(8,128)(2,1)S(1)}, u32[]{:S(2)}, u32[]{:S(2)}) collective-permute-start(bf16[6,96,128]{2,1,0:T(8,128)(2,1)} %collective-permute-done.2.rest_3_), channel_id=1, source_target_pairs={{0,1},{1,0},{2,3},{3,2},{4,5},{5,4},{6,7},{7,6},{8,9},{9,8},{10,11... | collective-permute-start | bytes 442376 | tf_op jit(solution)/shard_map/ppermute | solution.py:185
  24.0 1.6 %collective-permute-start.1 = (bf16[6,96,128]{2,1,0:T(8,128)(2,1)}, bf16[6,96,128]{2,1,0:T(8,128)(2,1)S(1)}, u32[]{:S(2)}, u32[]{:S(2)}) collective-permute-start(bf16[6,96,128]{2,1,0:T(8,128)(2,1)} %collective-permute-done.rest_1_), channel_id=1, source_target_pairs={{0,8},{8,0},{16,24},{24,16},{1,9},{9,1},{17,25},{25,17},{2,10},{10... | collective-permute-start | bytes 442376 | tf_op jit(solution)/shard_map/ppermute | solution.py:188
  25.5 1.4 %copy-start.3 = (bf16[6,96,128]{2,1,0:T(8,128)(2,1)}, bf16[6,96,128]{2,1,0:T(8,128)(2,1)S(1)}, u32[]{:S(2)}) copy-start(bf16[6,96,128]{2,1,0:T(8,128)(2,1)S(1)} %collective-permute-done.3.rest_4_) | copy-start | bytes 442372
  25.6 0.7 %copy-start.5 = (bf16[6,96,128]{2,1,0:T(8,128)(2,1)}, bf16[6,96,128]{2,1,0:T(8,128)(2,1)S(1)}, u32[]{:S(2)}) copy-start(bf16[6,96,128]{2,1,0:T(8,128)(2,1)S(1)} %collective-permute-done.1.rest_2_) | copy-start | bytes 442372
  27.0 32.0 %all-to-all-start.1 = ((bf16[32,24,128]{2,1,0:T(8,128)(2,1)}), bf16[32,24,128]{2,1,0:T(8,128)(2,1)S(1)}, u32[]{:S(2)}, u32[]{:S(2)}) async-start(bf16[32,24,128]{2,1,0:T(8,128)(2,1)} %broadcast_in_dim.28), calls=%async_computation.1 | async-start | bytes 393216 | tf_op jit(solution)/shard_map/all_to_all | solution.py:202
  32.5 0.9 %copy-start.4 = (bf16[6,96,128]{2,1,0:T(8,128)(2,1)S(1)}, bf16[6,96,128]{2,1,0:T(8,128)(2,1)}, u32[]{:S(2)}) copy-start(bf16[6,96,128]{2,1,0:T(8,128)(2,1)} %copy-done.3) | copy-start | bytes 442372
  33.4 0.9 %copy-start.6 = (bf16[6,96,128]{2,1,0:T(8,128)(2,1)S(1)}, bf16[6,96,128]{2,1,0:T(8,128)(2,1)}, u32[]{:S(2)}) copy-start(bf16[6,96,128]{2,1,0:T(8,128)(2,1)} %copy-done.5) | copy-start | bytes 442372
  38.2 6.7 %collective-permute-start.12 = (bf16[6,96,128]{2,1,0:T(8,128)(2,1)S(1)}, bf16[6,96,128]{2,1,0:T(8,128)(2,1)S(1)}, u32[]{:S(2)}, u32[]{:S(2)}) collective-permute-start(bf16[6,96,128]{2,1,0:T(8,128)(2,1)S(1)} %collective-permute-done.10.rest_7_), channel_id=1, source_target_pairs={{0,1},{1,0},{2,3},{3,2},{4,5},{5,4},{6,7},{7,6},{8,9},{9,8},{10,11... | collective-permute-start | bytes 442376 | tf_op jit(solution)/shard_map/ppermute | solution.py:185
  40.0 7.5 %collective-permute-start.8 = (bf16[6,96,128]{2,1,0:T(8,128)(2,1)S(1)}, bf16[6,96,128]{2,1,0:T(8,128)(2,1)S(1)}, u32[]{:S(2)}, u32[]{:S(2)}) collective-permute-start(bf16[6,96,128]{2,1,0:T(8,128)(2,1)S(1)} %collective-permute-done.6.rest_3_), channel_id=1, source_target_pairs={{0,1},{1,0},{2,3},{3,2},{4,5},{5,4},{6,7},{7,6},{8,9},{9,8},{10,11... | collective-permute-start | bytes 442376 | tf_op jit(solution)/shard_map/ppermute | solution.py:185
  40.3 7.2 %collective-permute-start.5 = (bf16[6,96,128]{2,1,0:T(8,128)(2,1)S(1)}, bf16[6,96,128]{2,1,0:T(8,128)(2,1)S(1)}, u32[]{:S(2)}, u32[]{:S(2)}) collective-permute-start(bf16[6,96,128]{2,1,0:T(8,128)(2,1)S(1)} %collective-permute-done.4.rest_1_), channel_id=1, source_target_pairs={{0,8},{8,0},{16,24},{24,16},{1,9},{9,1},{17,25},{25,17},{2,10},{10... | collective-permute-start | bytes 442376 | tf_op jit(solution)/shard_map/ppermute | solution.py:188
  40.3 7.2 %collective-permute-start.11 = (bf16[6,96,128]{2,1,0:T(8,128)(2,1)S(1)}, bf16[6,96,128]{2,1,0:T(8,128)(2,1)S(1)}, u32[]{:S(2)}, u32[]{:S(2)}) collective-permute-start(bf16[6,96,128]{2,1,0:T(8,128)(2,1)S(1)} %collective-permute-done.10.rest_7_), channel_id=1, source_target_pairs={{0,8},{8,0},{16,24},{24,16},{1,9},{9,1},{17,25},{25,17},{2,10},{10... | collective-permute-start | bytes 442376 | tf_op jit(solution)/shard_map/ppermute | solution.py:188
  40.8 6.7 %collective-permute-start.7 = (bf16[6,96,128]{2,1,0:T(8,128)(2,1)S(1)}, bf16[6,96,128]{2,1,0:T(8,128)(2,1)S(1)}, u32[]{:S(2)}, u32[]{:S(2)}) collective-permute-start(bf16[6,96,128]{2,1,0:T(8,128)(2,1)S(1)} %collective-permute-done.6.rest_3_), channel_id=1, source_target_pairs={{0,8},{8,0},{16,24},{24,16},{1,9},{9,1},{17,25},{25,17},{2,10},{10... | collective-permute-start | bytes 442376 | tf_op jit(solution)/shard_map/ppermute | solution.py:188
  44.9 2.6 %collective-permute-start.13 = (bf16[6,96,128]{2,1,0:T(8,128)(2,1)S(1)}, bf16[6,96,128]{2,1,0:T(8,128)(2,1)S(1)}, u32[]{:S(2)}, u32[]{:S(2)}) collective-permute-start(bf16[6,96,128]{2,1,0:T(8,128)(2,1)S(1)} %collective-permute-done.12.rest_9_), channel_id=1, source_target_pairs={{0,8},{8,0},{16,24},{24,16},{1,9},{9,1},{17,25},{25,17},{2,10},{10... | collective-permute-start | bytes 442376 | tf_op jit(solution)/shard_map/ppermute | solution.py:188
  47.5 1.4 %collective-permute-start.9 = (bf16[6,96,128]{2,1,0:T(8,128)(2,1)S(1)}, bf16[6,96,128]{2,1,0:T(8,128)(2,1)S(1)}, u32[]{:S(2)}, u32[]{:S(2)}) collective-permute-start(bf16[6,96,128]{2,1,0:T(8,128)(2,1)S(1)} %collective-permute-done.8.rest_5_), channel_id=1, source_target_pairs={{0,8},{8,0},{16,24},{24,16},{1,9},{9,1},{17,25},{25,17},{2,10},{10... | collective-permute-start | bytes 442376 | tf_op jit(solution)/shard_map/ppermute | solution.py:188
  58.9 0.7 %copy-start.1 = (bf16[32,24,128]{2,1,0:T(8,128)(2,1)}, bf16[32,24,128]{2,1,0:T(8,128)(2,1)S(1)}, u32[]{:S(2)}) copy-start(bf16[32,24,128]{2,1,0:T(8,128)(2,1)S(1)} %all-to-all-done.1.spread_ref) | copy-start | bytes 589828
  59.6 0.9 %copy-start.2 = (bf16[32,24,128]{2,1,0:T(8,128)(2,1)S(1)}, bf16[32,24,128]{2,1,0:T(8,128)(2,1)}, u32[]{:S(2)}) copy-start(bf16[32,24,128]{2,1,0:T(8,128)(2,1)} %copy-done.1) | copy-start | bytes 589828

commit v2 on v1

--- a/solution.py
+++ b/solution.py
@@ -196,13 +196,6 @@
     share = flat // groups
     shares = part_sum.reshape(tiles, groups, share).transpose(1, 0, 2).reshape(groups * tiles, share)
     arrived = lax.all_to_all(shares, ALL, split_axis=0, concat_axis=0, tiled=True)
-    running = jnp.sum(arrived, axis=0).astype(jnp.bfloat16).reshape(width // groups, width)
-    hidden = jnp.dot(running, cycle_integral_tiles[0], preferred_element_type=jnp.float32).astype(jnp.bfloat16)
-    hidden = jnp.pad(hidden, ((0, 0), (0, LANES - width)))
-    spread = lax.all_to_all(
-        jnp.broadcast_to(hidden[None], (groups * tiles,) + hidden.shape), ALL, split_axis=0, concat_axis=0, tiled=True
-    )
-
     blocks = jnp.pad(block_list.reshape(rows, width, width), ((0, 0), (0, LANES - width), (0, LANES - width)))
     place = me.reshape(1)
     packed = pack_factors(ladder_factor[0])
@@ -230,10 +223,23 @@
         return ladder(near, names, place, blocks, total, parts, tiles, width, pairs, cost)
 
     cross(range(0, half, across), total)
+    cross(range(half, tiles, across), total)
+    arrived, _ = lax.optimization_barrier((arrived, total))
+    running = jnp.sum(arrived, axis=0).astype(jnp.bfloat16).reshape(width // groups, width)
+    hidden = jnp.dot(running, cycle_integral_tiles[0], preferred_element_type=jnp.float32).astype(jnp.bfloat16)
+    hidden = jnp.pad(hidden, ((0, 0), (0, LANES - width)))
+    spread = lax.all_to_all(
+        jnp.broadcast_to(hidden[None], (groups * tiles,) + hidden.shape), ALL, split_axis=0, concat_axis=0, tiled=True
+    )
+
     early = tuple(range(1, across + 1))
-    total = stage(early, total, hidden, 30 * 10**9)
-    cross(range(half, tiles, across), total)
-    total = stage(tuple(s for s in range(1, tiles) if s not in early), total, total, rows)
+    last = tuple(range(half, half + across))
+    middle = tuple(s for s in range(1, tiles) if s not in early + last)
+    total = stage(early, total, total, rows)
+    for slot in middle + last:
+        halves[slot], _ = lax.optimization_barrier((halves[slot], total))
+    total = stage(middle, total, total, rows)
+    total = stage(last, total, total, rows)
     residual = close(names, blocks, total, spread, tiles, width)
     return residual.reshape(pairs, slots, flat)
 

time: 64.4 us -> 61.6 us (0.957)
  waiting for transfers between devices: 8.07 us -> 4.56 us
  Pallas kernels: 17.8 us -> 20.2 us
  local copies, waits for them, and re-layouts: 13.1 us -> 11.6 us
  other arithmetic: 1.24 us -> 0.13 us
    pallas_call x3 -> x4, Pallas kernels: 16.5 us -> 18.9 us  [ladder(): pl.pallas_call(functools.partial(ladder_kernel, near, tiles, width, len(c...]
    ppermute x7, waiting for transfers between devices: 6.7 us -> 4.53 us  [to_tile(): return lax.ppermute(array, 'tile', [(i, i ^ flip) for i in range(tiles)])]
    unnamed x21 -> x14, local copies, waits for them, and re-layouts: 5.88 us -> 4.37 us
    ppermute x7, waiting for transfers between devices: 1.37 us -> 0.02 us  [to_core(): return lax.ppermute(array, 'grp', [(i, i ^ 1) for i in range(groups)])]
    reduce_sum x1, other arithmetic: 1.15 us -> 0.04 us  [on_device(): jnp.sum(arrived, axis=0).astype(jnp.bfloat16)]
    all_to_all x1, starting transfers between devices: 5.52 us -> 4.61 us  [on_device(): lax.all_to_all(jnp.broadcast_to(hidden[None], (groups * tiles,) + hidden....]
    ppermute x7, starting transfers between devices: 0.76 us -> 1.66 us  [to_core(): return lax.ppermute(array, 'grp', [(i, i ^ 1) for i in range(groups)])]
  transfers between devices with their start and end apart: 16 -> 16, of which waited for: 3 -> 2; matrix products, arithmetic and copies ran while one was open for 7% -> 7% of each run, Pallas kernels for 26% -> 31%
where the time goes in v2:
time: 61.6 us; the launch traced here: 60.6 us
  starting transfers between devices  23.6 us (38%)
  Pallas kernels  20.2 us (33%)
  local copies, waits for them, and re-layouts  11.6 us (19%)
  waiting for transfers between devices  4.56 us (7%)
    pallas_call x4, Pallas kernels, ladder(): pl.pallas_call(functools.partial(ladder_kernel, near, tiles, width, len(c...  18.9 us
    ppermute x7, starting transfers between devices, to_tile(): return lax.ppermute(array, 'tile', [(i, i ^ flip) for i in range(tiles)])  9.88 us
    all_to_all x1, starting transfers between devices, on_device(): lax.all_to_all(shares, ALL, split_axis=0, concat_axis=0, tiled=True)  7.41 us
    all_to_all x1, starting transfers between devices, on_device(): lax.all_to_all(jnp.broadcast_to(hidden[None], (groups * tiles,) + hidden....  4.61 us
    ppermute x7, waiting for transfers between devices, to_tile(): return lax.ppermute(array, 'tile', [(i, i ^ flip) for i in range(tiles)])  4.53 us
    unnamed x14, local copies, waits for them, and re-layouts  4.37 us
    reshape x1, local copies, waits for them, and re-layouts, on_device(): return residual.reshape(pairs, slots, flat)  1.94 us
    ppermute x7, starting transfers between devices, to_core(): return lax.ppermute(array, 'grp', [(i, i ^ 1) for i in range(groups)])  1.66 us
  transfers between devices with their start and end apart: 16, of which 2 were waited for; matrix products, arithmetic and copies ran while one was open for 7% of the time, Pallas kernels for 31%

profile of v2, /device:TPU:0, one launch (start us, length us, event | category | flops | bytes accessed | tf_op | source)
XLA Modules:
  0.0 60.6 jit_solution(8169647129660180968)
XLA Ops:
  0.0 0.8 %copy.12 = s32[8,4]{1,0:T(8,128)S(1)} copy(s32[8,4]{0,1:T(4,128)} %param.6) | data formatting | bytes 256 | tf_op args[1]
  0.8 0.1 reshape.37.kept_ref
  0.8 1.2 %reshape.40 = bf16[32,9216]{1,0:T(8,128)(2,1)S(1)} reshape(bf16[8,4,9216]{2,1,0:T(4,128)(2,1)} %param.5) | data formatting | bytes 1179648 | tf_op jit(solution)/shard_map/reshape | solution.py:190
  2.1 0.7 %broadcast_in_dim.24 = bf16[8,4]{1,0:T(8,128)(2,1)S(1)} broadcast(bf16[8]{0:T(256)(128)(2,1)} %param.7), dimensions={0} | broadcast | bytes 80 | tf_op jit(solution)/shard_map/broadcast_in_dim | solution.py:193
  2.8 0.1 broadcast_in_dim.25
  2.9 0.2 convolution_bitcast_fusion
  3.1 1.0 %copy.18 = f32[32,1,2304]{2,1,0:T(1,128)} copy(f32[32,1,2304]{2,0,1:T(8,128)S(1)} %convolution_bitcast_fusion) | data formatting | bytes 589824 | tf_op jit(solution)/shard_map/all_to_all | solution.py:198
  4.1 7.4 %all-to-all-start = ((f32[32,1,2304]{2,1,0:T(1,128)}), f32[32,1,2304]{2,1,0:T(1,128)}, u32[]{:S(2)}, u32[]{:S(2)}) async-start(f32[32,1,2304]{2,1,0:T(1,128)} %copy.18), calls=%async_computation | async-start | bytes 589824 | tf_op jit(solution)/shard_map/all_to_all | solution.py:198
  11.6 0.0 copy-start.3
  11.6 0.2 copy.13
  11.9 0.1 maximum_maximum_fusion
  12.0 0.8 %copy.20 = bf16[1,6,96,128]{3,2,1,0:T(8,128)(2,1)} copy(bf16[1,6,96,128]{2,3,1,0:T(8,128)(2,1)S(1)} %constant_dynamic-slice_fusion) | data formatting | bytes 294912
  12.8 1.7 %collective-permute-start.2 = (bf16[6,96,128]{2,1,0:T(8,128)(2,1)}, bf16[6,96,128]{2,1,0:T(8,128)(2,1)S(1)}, u32[]{:S(2)}, u32[]{:S(2)}) collective-permute-start(bf16[6,96,128]{2,1,0:T(8,128)(2,1)} %bitcast.5), channel_id=1, source_target_pairs={{0,2},{1,3},{2,0},{3,1},{4,6},{5,7},{6,4},{7,5},{8,10},{9,11},{10,... | collective-permute-start | bytes 442376 | tf_op jit(solution)/shard_map/ppermute | solution.py:185
  14.5 1.5 %collective-permute-start = (bf16[6,96,128]{2,1,0:T(8,128)(2,1)}, bf16[6,96,128]{2,1,0:T(8,128)(2,1)S(1)}, u32[]{:S(2)}, u32[]{:S(2)}) collective-permute-start(bf16[6,96,128]{2,1,0:T(8,128)(2,1)} %bitcast.5), channel_id=1, source_target_pairs={{0,1},{1,0},{2,3},{3,2},{4,5},{5,4},{6,7},{7,6},{8,9},{9,8},{10,11... | collective-permute-start | bytes 442376 | tf_op jit(solution)/shard_map/ppermute | solution.py:185
  16.0 2.4 %collective-permute-start.10 = (bf16[6,96,128]{2,1,0:T(8,128)(2,1)}, bf16[6,96,128]{2,1,0:T(8,128)(2,1)S(1)}, u32[]{:S(2)}, u32[]{:S(2)}) collective-permute-start(bf16[6,96,128]{2,1,0:T(8,128)(2,1)} %bitcast.5), channel_id=1, source_target_pairs={{0,4},{1,5},{2,6},{3,7},{4,0},{5,1},{6,2},{7,3},{8,12},{9,13},{10,... | collective-permute-start | bytes 442376 | tf_op jit(solution)/shard_map/ppermute | solution.py:185
  18.4 0.5 collective-permute-start.6
  18.9 0.6 %reshape_reshape.3 = bf16[32,96,96]{2,1,0:T(8,128)(2,1)S(1)} reshape(bf16[8,4,9216]{2,1,0:T(4,128)(2,1)S(1)} %copy-done.3) | data formatting | bytes 1179648 | tf_op jit(solution)/shard_map/reshape;reshape | solution.py:199
  19.5 0.2 copy.14
  19.7 0.2 copy.15
  19.9 0.3 pad.8.blocks_ref
  20.2 3.6 %shard_map.55.rest_0_ = f32[32,96,96]{2,1,0:T(8,128)S(1)} custom-call(s32[32]{0:T(128)S(1)} %reshape.37.kept_ref, s32[1]{0:T(128)} %bitcast.me_ref, bf16[32,128,128]{2,1,0:T(8,128)(2,1)S(1)} %pad.8.blocks_ref, bf16[6,96,128]{2,1,0:T(8,128)(2,1)S(1)} %bitcast.25, bf16[6,96,128]{2,1,0:T(8,128)(2,1)S(1)} %bitcast.26), custom_call_target="tpu_custom_call" | custom-call | flops 32 | bytes 32 | tf_op jit(solution)/shard_map/pallas_call | solution.py:123
  23.8 0.0 all-to-all-done
  23.8 1.0 %copy.27 = f32[32,1,2304]{2,0,1:T(8,128)S(1)} copy(f32[32,1,2304]{2,1,0:T(1,128)} %all-to-all-done) | data formatting | bytes 589824
  24.8 0.1 convert_element_type.21
  24.9 0.1 convolution_convert_fusion
  25.0 0.7 %broadcast_in_dim.28 = bf16[32,24,128]{2,1,0:T(8,128)(2,1)} broadcast(bf16[24,128]{1,0:T(8,128)(2,1)S(1)} %pad.9), dimensions={1,2} | broadcast | bytes 202752 | tf_op jit(solution)/shard_map/broadcast_in_dim | solution.py:232
  25.8 4.6 %all-to-all-start.1 = ((bf16[32,24,128]{2,1,0:T(8,128)(2,1)}), bf16[32,24,128]{2,1,0:T(8,128)(2,1)S(1)}, u32[]{:S(2)}, u32[]{:S(2)}) async-start(bf16[32,24,128]{2,1,0:T(8,128)(2,1)} %broadcast_in_dim.28), calls=%async_computation.1 | async-start | bytes 393216 | tf_op jit(solution)/shard_map/all_to_all | solution.py:231
  30.4 0.3 collective-permute-start.3
  30.7 0.0 collective-permute-done.rest_1_
  30.7 0.3 collective-permute-start.1
  31.0 0.0 collective-permute-done.6.rest_3_
  31.0 1.8 %collective-permute-start.8 = (bf16[6,96,128]{2,1,0:T(8,128)(2,1)S(1)}, bf16[6,96,128]{2,1,0:T(8,128)(2,1)S(1)}, u32[]{:S(2)}, u32[]{:S(2)}) collective-permute-start(bf16[6,96,128]{2,1,0:T(8,128)(2,1)S(1)} %collective-permute-done.6.rest_3_), channel_id=1, source_target_pairs={{0,1},{1,0},{2,3},{3,2},{4,5},{5,4},{6,7},{7,6},{8,9},{9,8},{10,11... | collective-permute-start | bytes 442376 | tf_op jit(solution)/shard_map/ppermute | solution.py:185
  32.7 0.3 collective-permute-start.4
  33.0 1.8 %collective-permute-start.12 = (bf16[6,96,128]{2,1,0:T(8,128)(2,1)S(1)}, bf16[6,96,128]{2,1,0:T(8,128)(2,1)S(1)}, u32[]{:S(2)}, u32[]{:S(2)}) collective-permute-start(bf16[6,96,128]{2,1,0:T(8,128)(2,1)S(1)} %collective-permute-done.10.rest_1_), channel_id=1, source_target_pairs={{0,1},{1,0},{2,3},{3,2},{4,5},{5,4},{6,7},{7,6},{8,9},{9,8},{10,11... | collective-permute-start | bytes 442376 | tf_op jit(solution)/shard_map/ppermute | solution.py:185
  34.8 0.0 collective-permute-done.3.rest_4_
  34.8 5.2 %shard_map.56.rest_0_ = f32[32,96,96]{2,1,0:T(8,128)S(1)} custom-call(s32[32]{0:T(128)S(1)} %reshape.37.kept_ref, s32[1]{0:T(128)} %bitcast.me_ref, bf16[32,128,128]{2,1,0:T(8,128)(2,1)S(1)} %pad.8.blocks_ref, f32[32,96,96]{2,1,0:T(8,128)S(1)} %shard_map.55.rest_0_, ...), custom_call_target="tpu_custom_call", output_to_operand_aliasing={{}: (3, {})} | custom-call | flops 32 | bytes 32 | tf_op jit(solution)/shard_map/pallas_call | solution.py:123
  40.0 0.1 collective-permute-start.9
  40.1 0.5 collective-permute-start.7
  40.6 1.7 %collective-permute-done.4.rest_1_ = bf16[6,96,128]{2,1,0:T(8,128)(2,1)S(1)} collective-permute-done((bf16[6,96,128]{2,1,0:T(8,128)(2,1)S(1)}, bf16[6,96,128]{2,1,0:T(8,128)(2,1)S(1)}, u32[]{:S(2)}, u32[]{:S(2)}) %collective-permute-start.4) | collective-permute-done | bytes 147488 | tf_op jit(solution)/shard_map/ppermute | solution.py:185
  42.3 2.8 %collective-permute-done.12.rest_3_ = bf16[6,96,128]{2,1,0:T(8,128)(2,1)S(1)} collective-permute-done((bf16[6,96,128]{2,1,0:T(8,128)(2,1)S(1)}, bf16[6,96,128]{2,1,0:T(8,128)(2,1)S(1)}, u32[]{:S(2)}, u32[]{:S(2)}) %collective-permute-start.12) | collective-permute-done | bytes 147488 | tf_op jit(solution)/shard_map/ppermute | solution.py:185
  45.1 0.5 collective-permute-start.13
  45.6 5.8 %shard_map.57.rest_0_ = f32[32,96,96]{2,1,0:T(8,128)S(1)} custom-call(s32[32]{0:T(128)S(1)} %reshape.37.kept_ref, s32[1]{0:T(128)} %bitcast.me_ref, bf16[32,128,128]{2,1,0:T(8,128)(2,1)S(1)} %pad.8.blocks_ref, f32[32,96,96]{2,1,0:T(8,128)S(1)} %shard_map.56.rest_0_, ...), custom_call_target="tpu_custom_call", output_to_operand_aliasing={{}: (3, {})} | custom-call | flops 32 | bytes 32 | tf_op jit(solution)/shard_map/pallas_call | solution.py:123
  51.5 4.2 %shard_map.58.total_ref = f32[32,96,96]{2,1,0:T(8,128)S(1)} custom-call(s32[32]{0:T(128)S(1)} %reshape.37.kept_ref, s32[1]{0:T(128)} %bitcast.me_ref, bf16[32,128,128]{2,1,0:T(8,128)(2,1)S(1)} %pad.8.blocks_ref, f32[32,96,96]{2,1,0:T(8,128)S(1)} %shard_map.57.rest_0_, ...), custom_call_target="tpu_custom_call", output_to_operand_aliasing={{}: (3, {})} | custom-call | flops 32 | bytes 32 | tf_op jit(solution)/shard_map/pallas_call | solution.py:123
  55.8 0.0 copy-start.1
  55.8 0.7 %copy-done.1 = bf16[32,24,128]{2,1,0:T(8,128)(2,1)} copy-done((bf16[32,24,128]{2,1,0:T(8,128)(2,1)}, bf16[32,24,128]{2,1,0:T(8,128)(2,1)S(1)}, u32[]{:S(2)}) %copy-start.1) | copy-done | bytes 196632
  56.4 0.9 %copy-done.2 = bf16[32,24,128]{2,1,0:T(8,128)(2,1)S(1)} copy-done((bf16[32,24,128]{2,1,0:T(8,128)(2,1)S(1)}, bf16[32,24,128]{2,1,0:T(8,128)(2,1)}, u32[]{:S(2)}) %copy-start.2) | copy-done | bytes 196632
  57.4 1.3 %shard_map.59 = bf16[32,96,96]{2,1,0:T(8,128)(2,1)S(1)} custom-call(s32[32]{0:T(128)S(1)} %reshape.37.kept_ref, bf16[32,128,128]{2,1,0:T(8,128)(2,1)S(1)} %pad.8.blocks_ref, f32[32,96,96]{2,1,0:T(8,128)S(1)} %shard_map.58.total_ref, bf16[32,24,128]{2,1,0:T(8,128)(2,1)S(1)} %copy-done.2), custom_call_target="tpu_custom_call" | custom-call | flops 32 | bytes 32 | tf_op jit(solution)/shard_map/pallas_call | solution.py:160
  58.7 1.9 %reshape.41 = bf16[8,4,9216]{2,1,0:T(4,128)(2,1)} reshape(bf16[32,96,96]{2,1,0:T(8,128)(2,1)S(1)} %shard_map.59) | data formatting | bytes 1179648 | tf_op jit(solution)/shard_map/reshape | solution.py:244
  (24 shorter events, 0.2 us)
Async XLA Ops:
  0.0 24.9 %copy-start = (bf16[1,96,96]{2,1,0:T(8,128)(2,1)S(1)}, bf16[1,96,96]{2,1,0:T(8,128)(2,1)}, u32[]{:S(2)}) copy-start(bf16[1,96,96]{2,1,0:T(8,128)(2,1)} %param.9) | copy-start | bytes 55300
  0.8 10.7 %copy-start.4 = (bf16[1,16,96,96]{3,2,1,0:T(8,128)(2,1)S(1)}, bf16[1,16,96,96]{3,2,1,0:T(8,128)(2,1)}, u32[]{:S(2)}) copy-start(bf16[1,16,96,96]{3,2,1,0:T(8,128)(2,1)} %param.8) | copy-start | bytes 884740
  4.1 19.6 %all-to-all-start = ((f32[32,1,2304]{2,1,0:T(1,128)}), f32[32,1,2304]{2,1,0:T(1,128)}, u32[]{:S(2)}, u32[]{:S(2)}) async-start(f32[32,1,2304]{2,1,0:T(1,128)} %copy.18), calls=%async_computation | async-start | bytes 589824 | tf_op jit(solution)/shard_map/all_to_all | solution.py:198
  11.6 7.3 %copy-start.3 = (bf16[8,4,9216]{2,1,0:T(4,128)(2,1)S(1)}, bf16[8,4,9216]{2,1,0:T(4,128)(2,1)}, u32[]{:S(2)}) copy-start(bf16[8,4,9216]{2,1,0:T(4,128)(2,1)} %param.5) | copy-start | bytes 1769476
  12.8 17.6 %collective-permute-start.2 = (bf16[6,96,128]{2,1,0:T(8,128)(2,1)}, bf16[6,96,128]{2,1,0:T(8,128)(2,1)S(1)}, u32[]{:S(2)}, u32[]{:S(2)}) collective-permute-start(bf16[6,96,128]{2,1,0:T(8,128)(2,1)} %bitcast.5), channel_id=1, source_target_pairs={{0,2},{1,3},{2,0},{3,1},{4,6},{5,7},{6,4},{7,5},{8,10},{9,11},{10,... | collective-permute-start | bytes 442376 | tf_op jit(solution)/shard_map/ppermute | solution.py:185
  14.5 16.2 %collective-permute-start = (bf16[6,96,128]{2,1,0:T(8,128)(2,1)}, bf16[6,96,128]{2,1,0:T(8,128)(2,1)S(1)}, u32[]{:S(2)}, u32[]{:S(2)}) collective-permute-start(bf16[6,96,128]{2,1,0:T(8,128)(2,1)} %bitcast.5), channel_id=1, source_target_pairs={{0,1},{1,0},{2,3},{3,2},{4,5},{5,4},{6,7},{7,6},{8,9},{9,8},{10,11... | collective-permute-start | bytes 442376 | tf_op jit(solution)/shard_map/ppermute | solution.py:185
  16.0 17.0 %collective-permute-start.10 = (bf16[6,96,128]{2,1,0:T(8,128)(2,1)}, bf16[6,96,128]{2,1,0:T(8,128)(2,1)S(1)}, u32[]{:S(2)}, u32[]{:S(2)}) collective-permute-start(bf16[6,96,128]{2,1,0:T(8,128)(2,1)} %bitcast.5), channel_id=1, source_target_pairs={{0,4},{1,5},{2,6},{3,7},{4,0},{5,1},{6,2},{7,3},{8,12},{9,13},{10,... | collective-permute-start | bytes 442376 | tf_op jit(solution)/shard_map/ppermute | solution.py:185
  18.4 12.6 %collective-permute-start.6 = (bf16[6,96,128]{2,1,0:T(8,128)(2,1)}, bf16[6,96,128]{2,1,0:T(8,128)(2,1)S(1)}, u32[]{:S(2)}, u32[]{:S(2)}) collective-permute-start(bf16[6,96,128]{2,1,0:T(8,128)(2,1)} %bitcast.5), channel_id=1, source_target_pairs={{0,6},{1,7},{2,4},{3,5},{4,2},{5,3},{6,0},{7,1},{8,14},{9,15},{10,... | collective-permute-start | bytes 442376 | tf_op jit(solution)/shard_map/ppermute | solution.py:185
  25.8 30.0 %all-to-all-start.1 = ((bf16[32,24,128]{2,1,0:T(8,128)(2,1)}), bf16[32,24,128]{2,1,0:T(8,128)(2,1)S(1)}, u32[]{:S(2)}, u32[]{:S(2)}) async-start(bf16[32,24,128]{2,1,0:T(8,128)(2,1)} %broadcast_in_dim.28), calls=%async_computation.1 | async-start | bytes 393216 | tf_op jit(solution)/shard_map/all_to_all | solution.py:231
  30.4 4.4 %collective-permute-start.3 = (bf16[6,96,128]{2,1,0:T(8,128)(2,1)S(1)}, bf16[6,96,128]{2,1,0:T(8,128)(2,1)S(1)}, u32[]{:S(2)}, u32[]{:S(2)}) collective-permute-start(bf16[6,96,128]{2,1,0:T(8,128)(2,1)S(1)} %collective-permute-done.2.rest_3_), channel_id=1, source_target_pairs={{0,8},{8,0},{16,24},{24,16},{1,9},{9,1},{17,25},{25,17},{2,10},{10... | collective-permute-start | bytes 442376 | tf_op jit(solution)/shard_map/ppermute | solution.py:188
  30.7 4.1 %collective-permute-start.1 = (bf16[6,96,128]{2,1,0:T(8,128)(2,1)S(1)}, bf16[6,96,128]{2,1,0:T(8,128)(2,1)S(1)}, u32[]{:S(2)}, u32[]{:S(2)}) collective-permute-start(bf16[6,96,128]{2,1,0:T(8,128)(2,1)S(1)} %collective-permute-done.rest_1_), channel_id=1, source_target_pairs={{0,8},{8,0},{16,24},{24,16},{1,9},{9,1},{17,25},{25,17},{2,10},{10... | collective-permute-start | bytes 442376 | tf_op jit(solution)/shard_map/ppermute | solution.py:188
  31.0 9.0 %collective-permute-start.8 = (bf16[6,96,128]{2,1,0:T(8,128)(2,1)S(1)}, bf16[6,96,128]{2,1,0:T(8,128)(2,1)S(1)}, u32[]{:S(2)}, u32[]{:S(2)}) collective-permute-start(bf16[6,96,128]{2,1,0:T(8,128)(2,1)S(1)} %collective-permute-done.6.rest_3_), channel_id=1, source_target_pairs={{0,1},{1,0},{2,3},{3,2},{4,5},{5,4},{6,7},{7,6},{8,9},{9,8},{10,11... | collective-permute-start | bytes 442376 | tf_op jit(solution)/shard_map/ppermute | solution.py:185
  32.7 9.5 %collective-permute-start.4 = (bf16[6,96,128]{2,1,0:T(8,128)(2,1)S(1)}, bf16[6,96,128]{2,1,0:T(8,128)(2,1)S(1)}, u32[]{:S(2)}, u32[]{:S(2)}) collective-permute-start(bf16[6,96,128]{2,1,0:T(8,128)(2,1)S(1)} %collective-permute-done.2.rest_3_), channel_id=1, source_target_pairs={{0,1},{1,0},{2,3},{3,2},{4,5},{5,4},{6,7},{7,6},{8,9},{9,8},{10,11... | collective-permute-start | bytes 442376 | tf_op jit(solution)/shard_map/ppermute | solution.py:185
  33.0 12.1 %collective-permute-start.12 = (bf16[6,96,128]{2,1,0:T(8,128)(2,1)S(1)}, bf16[6,96,128]{2,1,0:T(8,128)(2,1)S(1)}, u32[]{:S(2)}, u32[]{:S(2)}) collective-permute-start(bf16[6,96,128]{2,1,0:T(8,128)(2,1)S(1)} %collective-permute-done.10.rest_1_), channel_id=1, source_target_pairs={{0,1},{1,0},{2,3},{3,2},{4,5},{5,4},{6,7},{7,6},{8,9},{9,8},{10,11... | collective-permute-start | bytes 442376 | tf_op jit(solution)/shard_map/ppermute | solution.py:185
  40.0 5.6 %collective-permute-start.9 = (bf16[6,96,128]{2,1,0:T(8,128)(2,1)S(1)}, bf16[6,96,128]{2,1,0:T(8,128)(2,1)S(1)}, u32[]{:S(2)}, u32[]{:S(2)}) collective-permute-start(bf16[6,96,128]{2,1,0:T(8,128)(2,1)S(1)} %collective-permute-done.8.rest_5_), channel_id=1, source_target_pairs={{0,8},{8,0},{16,24},{24,16},{1,9},{9,1},{17,25},{25,17},{2,10},{10... | collective-permute-start | bytes 442376 | tf_op jit(solution)/shard_map/ppermute | solution.py:188
  40.1 5.5 %collective-permute-start.7 = (bf16[6,96,128]{2,1,0:T(8,128)(2,1)S(1)}, bf16[6,96,128]{2,1,0:T(8,128)(2,1)S(1)}, u32[]{:S(2)}, u32[]{:S(2)}) collective-permute-start(bf16[6,96,128]{2,1,0:T(8,128)(2,1)S(1)} %collective-permute-done.6.rest_3_), channel_id=1, source_target_pairs={{0,8},{8,0},{16,24},{24,16},{1,9},{9,1},{17,25},{25,17},{2,10},{10... | collective-permute-start | bytes 442376 | tf_op jit(solution)/shard_map/ppermute | solution.py:188
  42.3 3.4 %collective-permute-start.5 = (bf16[6,96,128]{2,1,0:T(8,128)(2,1)S(1)}, bf16[6,96,128]{2,1,0:T(8,128)(2,1)S(1)}, u32[]{:S(2)}, u32[]{:S(2)}) collective-permute-start(bf16[6,96,128]{2,1,0:T(8,128)(2,1)S(1)} %collective-permute-done.4.rest_1_), channel_id=1, source_target_pairs={{0,8},{8,0},{16,24},{24,16},{1,9},{9,1},{17,25},{25,17},{2,10},{10... | collective-permute-start | bytes 442376 | tf_op jit(solution)/shard_map/ppermute | solution.py:188
  45.1 6.4 %collective-permute-start.11 = (bf16[6,96,128]{2,1,0:T(8,128)(2,1)S(1)}, bf16[6,96,128]{2,1,0:T(8,128)(2,1)S(1)}, u32[]{:S(2)}, u32[]{:S(2)}) collective-permute-start(bf16[6,96,128]{2,1,0:T(8,128)(2,1)S(1)} %collective-permute-done.10.rest_1_), channel_id=1, source_target_pairs={{0,8},{8,0},{16,24},{24,16},{1,9},{9,1},{17,25},{25,17},{2,10},{10... | collective-permute-start | bytes 442376 | tf_op jit(solution)/shard_map/ppermute | solution.py:188
  45.1 6.4 %collective-permute-start.13 = (bf16[6,96,128]{2,1,0:T(8,128)(2,1)S(1)}, bf16[6,96,128]{2,1,0:T(8,128)(2,1)S(1)}, u32[]{:S(2)}, u32[]{:S(2)}) collective-permute-start(bf16[6,96,128]{2,1,0:T(8,128)(2,1)S(1)} %collective-permute-done.12.rest_3_), channel_id=1, source_target_pairs={{0,8},{8,0},{16,24},{24,16},{1,9},{9,1},{17,25},{25,17},{2,10},{10... | collective-permute-start | bytes 442376 | tf_op jit(solution)/shard_map/ppermute | solution.py:188
  55.8 0.7 %copy-start.1 = (bf16[32,24,128]{2,1,0:T(8,128)(2,1)}, bf16[32,24,128]{2,1,0:T(8,128)(2,1)S(1)}, u32[]{:S(2)}) copy-start(bf16[32,24,128]{2,1,0:T(8,128)(2,1)S(1)} %all-to-all-done.1.spread_ref) | copy-start | bytes 589828
  56.4 0.9 %copy-start.2 = (bf16[32,24,128]{2,1,0:T(8,128)(2,1)S(1)}, bf16[32,24,128]{2,1,0:T(8,128)(2,1)}, u32[]{:S(2)}) copy-start(bf16[32,24,128]{2,1,0:T(8,128)(2,1)} %copy-done.1) | copy-start | bytes 589828

commit v3 on v2

--- a/solution.py
+++ b/solution.py
@@ -141,8 +141,11 @@
     )(kept, me, blocks, *carried, *parts)
 
 
-def close_kernel(tiles, width, kept_ref, blocks_ref, total_ref, spread_ref, out_ref, landed, hidden, sem):
+def close_kernel(tiles, width, kept_ref, blocks_ref, total_ref, spread_ref, out_ref, landed, hidden, square, lines, sem):
     groups = spread_ref.shape[0] // tiles
+    pairs, slots, flat = out_ref.shape
+    count = flat // LANES
+    parts = width * 4 // LANES
     copy = pltpu.make_async_copy(spread_ref, landed, sem)
     copy.start()
     hidden[:, width:, :] = jnp.zeros((tiles, LANES - width, LANES), jnp.bfloat16)
@@ -150,21 +153,40 @@
     for tile in range(tiles):
         pieces = [landed[g * tiles + tile].astype(jnp.float32) for g in range(groups)]
         hidden[tile, :width, :] = jnp.concatenate(pieces, axis=0).astype(jnp.bfloat16)
-    for r in range(blocks_ref.shape[0]):
-        term = jnp.dot(blocks_ref[r, :width, :], hidden[kept_ref[r]], preferred_element_type=jnp.float32)
-        out_ref[r] = (total_ref[r] + term[:, :width]).astype(jnp.bfloat16)
-
-
-def close(kept, blocks, total, spread, tiles, width):
+    spare = LANES - width
+    lane = lax.broadcasted_iota(jnp.int32, (width // 4, LANES), 1)
+    for pair in range(pairs):
+        for slot in range(slots):
+            r = pair * slots + slot
+            term = jnp.dot(blocks_ref[r, :width, :], hidden[kept_ref[r]], preferred_element_type=jnp.float32)
+            square[r, :, :width] = total_ref[r] + term[:, :width]
+            quarter = [square[r, pl.ds(j, width // 4, stride=4), :] for j in range(4)]
+            second = pltpu.roll(quarter[1], width, 1)
+            third = pltpu.roll(quarter[2], 2 * spare, 1)
+            fourth = pltpu.roll(quarter[3], spare, 1)
+            packed = (
+                jnp.where(lane < width, quarter[0], second),
+                jnp.where(lane < 2 * spare, second, third),
+                jnp.where(lane < spare, third, fourth),
+            )
+            for i in range(parts):
+                lines[pair, pl.ds(slot * count + i, width // 4, stride=parts), :] = packed[i]
+        for t in range(count):
+            out_ref[pair, :, t * LANES:(t + 1) * LANES] = lines[pair, pl.ds(t, slots, stride=count), :].astype(jnp.bfloat16)
+
+
+def close(kept, blocks, total, spread, tiles, width, shape):
     rows = blocks.shape[0]
     return pl.pallas_call(
         functools.partial(close_kernel, tiles, width),
-        out_shape=jax.ShapeDtypeStruct((rows, width, width), jnp.bfloat16),
+        out_shape=jax.ShapeDtypeStruct(shape, jnp.bfloat16),
         in_specs=[SMEM] + [VMEM] * 2 + [FREE],
         out_specs=VMEM,
         scratch_shapes=[
             pltpu.VMEM(spread.shape, jnp.bfloat16),
             pltpu.VMEM((tiles, LANES, LANES), jnp.bfloat16),
+            pltpu.VMEM((rows, width, LANES), jnp.float32),
+            pltpu.VMEM((shape[0], shape[1] * shape[2] // LANES, LANES), jnp.float32),
             pltpu.SemaphoreType.DMA,
         ],
         compiler_params=pltpu.CompilerParams(vmem_limit_bytes=16 << 20),
@@ -222,7 +244,9 @@
         total, _, *parts = lax.optimization_barrier((total, gate, *parts))
         return ladder(near, names, place, blocks, total, parts, tiles, width, pairs, cost)
 
-    cross(range(0, half, across), total)
+    for slot in range(1, half):
+        if slot % across:
+            halves[slot] = to_tile(mine, slot)
     cross(range(half, tiles, across), total)
     arrived, _ = lax.optimization_barrier((arrived, total))
     running = jnp.sum(arrived, axis=0).astype(jnp.bfloat16).reshape(width // groups, width)
@@ -232,7 +256,7 @@
         jnp.broadcast_to(hidden[None], (groups * tiles,) + hidden.shape), ALL, split_axis=0, concat_axis=0, tiled=True
     )
 
-    early = tuple(range(1, across + 1))
+    early = tuple(range(1, half))
     last = tuple(range(half, half + across))
     middle = tuple(s for s in range(1, tiles) if s not in early + last)
     total = stage(early, total, total, rows)
@@ -240,8 +264,7 @@
         halves[slot], _ = lax.optimization_barrier((halves[slot], total))
     total = stage(middle, total, total, rows)
     total = stage(last, total, total, rows)
-    residual = close(names, blocks, total, spread, tiles, width)
-    return residual.reshape(pairs, slots, flat)
+    return close(names, blocks, total, spread, tiles, width, amplitudes.shape)
 
 
 def solution(mesh):

time: 61.6 us -> 57.9 us (0.940)
  local copies, waits for them, and re-layouts: 11.6 us -> 8.04 us
  starting transfers between devices: 23.6 us -> 21.1 us
  waiting for transfers between devices: 4.56 us -> 6.28 us
  Pallas kernels: 20.2 us -> 21.2 us
    all_to_all x1, waiting for transfers between devices: 0.01 us -> 4.86 us  [on_device(): lax.all_to_all(shares, ALL, split_axis=0, concat_axis=0, tiled=True)]
    ppermute x7, waiting for transfers between devices: 4.53 us -> 1.4 us  [to_tile(): return lax.ppermute(array, 'tile', [(i, i ^ flip) for i in range(tiles)])]
    all_to_all x1, starting transfers between devices: 4.61 us -> 2.6 us  [on_device(): lax.all_to_all(jnp.broadcast_to(hidden[None], (groups * tiles,) + hidden....]
    reshape x1 -> x0, local copies, waits for them, and re-layouts: 1.94 us -> none  [on_device(): return residual.reshape(pairs, slots, flat)]
    unnamed x14 -> x10, local copies, waits for them, and re-layouts: 4.37 us -> 2.76 us
    pallas_call x1, Pallas kernels: 1.29 us -> 2.45 us  [close(): pl.pallas_call(functools.partial(close_kernel, tiles, width), out_shape=j...]
  transfers between devices with their start and end apart: 16 -> 16, of which waited for: 2 -> 2; matrix products, arithmetic and copies ran while one was open for 7% -> 8% of each run, Pallas kernels for 31% -> 33%
where the time goes in v3:
time: 57.9 us; the launch traced here: 57.2 us
  Pallas kernels  21.2 us (37%)
  starting transfers between devices  21.1 us (36%)
  local copies, waits for them, and re-layouts  8.04 us (14%)
  waiting for transfers between devices  6.28 us (11%)
    pallas_call x4, Pallas kernels, ladder(): pl.pallas_call(functools.partial(ladder_kernel, near, tiles, width, len(c...  18.7 us
    ppermute x7, starting transfers between devices, to_tile(): return lax.ppermute(array, 'tile', [(i, i ^ flip) for i in range(tiles)])  9.58 us
    all_to_all x1, starting transfers between devices, on_device(): lax.all_to_all(shares, ALL, split_axis=0, concat_axis=0, tiled=True)  7.41 us
    all_to_all x1, waiting for transfers between devices, on_device(): lax.all_to_all(shares, ALL, split_axis=0, concat_axis=0, tiled=True)  4.86 us
    unnamed x10, local copies, waits for them, and re-layouts  2.76 us
    all_to_all x1, starting transfers between devices, on_device(): lax.all_to_all(jnp.broadcast_to(hidden[None], (groups * tiles,) + hidden....  2.6 us
    pallas_call x1, Pallas kernels, close(): pl.pallas_call(functools.partial(close_kernel, tiles, width), out_shape=j...  2.45 us
    ppermute x7, starting transfers between devices, to_core(): return lax.ppermute(array, 'grp', [(i, i ^ 1) for i in range(groups)])  1.47 us
  transfers between devices with their start and end apart: 16, of which 2 were waited for; matrix products, arithmetic and copies ran while one was open for 8% of the time, Pallas kernels for 33%

profile of v3, /device:TPU:0, one launch (start us, length us, event | category | flops | bytes accessed | tf_op | source)
XLA Modules:
  0.0 57.2 jit_solution(8839272765778149701)
XLA Ops:
  0.0 0.7 %broadcast_in_dim.24 = bf16[8,4]{1,0:T(8,128)(2,1)S(1)} broadcast(bf16[8]{0:T(256)(128)(2,1)} %param.7), dimensions={0} | broadcast | bytes 80 | tf_op jit(solution)/shard_map/broadcast_in_dim | solution.py:215
  0.7 0.1 broadcast_in_dim.25
  0.8 0.8 %copy.12 = s32[8,4]{1,0:T(8,128)S(1)} copy(s32[8,4]{0,1:T(4,128)} %param.6) | data formatting | bytes 256 | tf_op args[1]
  1.6 0.1 reshape.34.kept_ref
  1.7 1.2 %reshape.37 = bf16[32,9216]{1,0:T(8,128)(2,1)S(1)} reshape(bf16[8,4,9216]{2,1,0:T(4,128)(2,1)} %param.5) | data formatting | bytes 1179648 | tf_op jit(solution)/shard_map/reshape | solution.py:212
  2.9 0.2 convolution_bitcast_fusion
  3.1 1.0 %copy.18 = f32[32,1,2304]{2,1,0:T(1,128)} copy(f32[32,1,2304]{2,0,1:T(8,128)S(1)} %convolution_bitcast_fusion) | data formatting | bytes 589824 | tf_op jit(solution)/shard_map/all_to_all | solution.py:220
  4.1 7.4 %all-to-all-start = ((f32[32,1,2304]{2,1,0:T(1,128)}), f32[32,1,2304]{2,1,0:T(1,128)}, u32[]{:S(2)}, u32[]{:S(2)}) async-start(f32[32,1,2304]{2,1,0:T(1,128)} %copy.18), calls=%async_computation | async-start | bytes 589824 | tf_op jit(solution)/shard_map/all_to_all | solution.py:220
  11.6 0.0 copy-start.1
  11.6 0.2 copy.13
  11.9 0.1 maximum_maximum_fusion
  12.0 0.8 %copy.20 = bf16[1,6,96,128]{3,2,1,0:T(8,128)(2,1)} copy(bf16[1,6,96,128]{2,3,1,0:T(8,128)(2,1)S(1)} %constant_dynamic-slice_fusion) | data formatting | bytes 294912
  12.8 2.6 %collective-permute-start.10 = (bf16[6,96,128]{2,1,0:T(8,128)(2,1)}, bf16[6,96,128]{2,1,0:T(8,128)(2,1)S(1)}, u32[]{:S(2)}, u32[]{:S(2)}) collective-permute-start(bf16[6,96,128]{2,1,0:T(8,128)(2,1)} %bitcast.5), channel_id=1, source_target_pairs={{0,4},{1,5},{2,6},{3,7},{4,0},{5,1},{6,2},{7,3},{8,12},{9,13},{10,... | collective-permute-start | bytes 442376 | tf_op jit(solution)/shard_map/ppermute | solution.py:207
  15.4 1.5 %collective-permute-start.6 = (bf16[6,96,128]{2,1,0:T(8,128)(2,1)}, bf16[6,96,128]{2,1,0:T(8,128)(2,1)}, u32[]{:S(2)}, u32[]{:S(2)}) collective-permute-start(bf16[6,96,128]{2,1,0:T(8,128)(2,1)} %bitcast.5), channel_id=1, source_target_pairs={{0,6},{1,7},{2,4},{3,5},{4,2},{5,3},{6,0},{7,1},{8,14},{9,15},{10,... | collective-permute-start | bytes 442376 | tf_op jit(solution)/shard_map/ppermute | solution.py:207
  16.9 1.0 %collective-permute-start.4 = (bf16[6,96,128]{2,1,0:T(8,128)(2,1)}, bf16[6,96,128]{2,1,0:T(8,128)(2,1)S(1)}, u32[]{:S(2)}, u32[]{:S(2)}) collective-permute-start(bf16[6,96,128]{2,1,0:T(8,128)(2,1)} %bitcast.5), channel_id=1, source_target_pairs={{0,3},{1,2},{2,1},{3,0},{4,7},{5,6},{6,5},{7,4},{8,11},{9,10},{10,... | collective-permute-start | bytes 442376 | tf_op jit(solution)/shard_map/ppermute | solution.py:207
  17.8 2.0 %collective-permute-start.2 = (bf16[6,96,128]{2,1,0:T(8,128)(2,1)}, bf16[6,96,128]{2,1,0:T(8,128)(2,1)S(1)}, u32[]{:S(2)}, u32[]{:S(2)}) collective-permute-start(bf16[6,96,128]{2,1,0:T(8,128)(2,1)} %bitcast.5), channel_id=1, source_target_pairs={{0,2},{1,3},{2,0},{3,1},{4,6},{5,7},{6,4},{7,5},{8,10},{9,11},{10,... | collective-permute-start | bytes 442376 | tf_op jit(solution)/shard_map/ppermute | solution.py:207
  19.8 0.6 collective-permute-start
  20.4 0.6 %reshape_reshape.3 = bf16[32,96,96]{2,1,0:T(8,128)(2,1)S(1)} reshape(bf16[8,4,9216]{2,1,0:T(4,128)(2,1)S(1)} %copy-done.1) | data formatting | bytes 1179648 | tf_op jit(solution)/shard_map/reshape;reshape | solution.py:221
  21.0 0.2 copy.15
  21.2 0.2 copy.14
  21.3 0.3 pad.8.blocks_ref
  21.6 2.6 %shard_map.55.rest_0_ = f32[32,96,96]{2,1,0:T(8,128)S(1)} custom-call(s32[32]{0:T(128)S(1)} %reshape.34.kept_ref, s32[1]{0:T(128)} %bitcast.me_ref, bf16[32,128,128]{2,1,0:T(8,128)(2,1)S(1)} %pad.8.blocks_ref, bf16[6,96,128]{2,1,0:T(8,128)(2,1)S(1)} %bitcast.26, bf16[6,96,128]{2,1,0:T(8,128)(2,1)S(1)} %bitcast.25), custom_call_target="tpu_custom_call" | custom-call | flops 32 | bytes 32 | tf_op jit(solution)/shard_map/pallas_call | solution.py:123
  24.3 4.9 %all-to-all-done = f32[32,1,2304]{2,1,0:T(1,128)} async-done(((f32[32,1,2304]{2,1,0:T(1,128)}), f32[32,1,2304]{2,1,0:T(1,128)}, u32[]{:S(2)}, u32[]{:S(2)}) %all-to-all-start) | async-done | bytes 294944 | tf_op jit(solution)/shard_map/all_to_all | solution.py:220
  29.1 1.0 %copy.27 = f32[32,1,2304]{2,0,1:T(8,128)S(1)} copy(f32[32,1,2304]{2,1,0:T(1,128)} %all-to-all-done) | data formatting | bytes 589824
  30.1 0.1 convert_element_type.21
  30.2 0.1 convolution_convert_fusion
  30.4 0.7 %broadcast_in_dim.28 = bf16[32,24,128]{2,1,0:T(8,128)(2,1)} broadcast(bf16[24,128]{1,0:T(8,128)(2,1)S(1)} %pad.9), dimensions={1,2} | broadcast | bytes 202752 | tf_op jit(solution)/shard_map/broadcast_in_dim | solution.py:256
  31.1 2.6 %all-to-all-start.1 = ((bf16[32,24,128]{2,1,0:T(8,128)(2,1)}), bf16[32,24,128]{2,1,0:T(8,128)(2,1)S(1)}, u32[]{:S(2)}, u32[]{:S(2)}) async-start(bf16[32,24,128]{2,1,0:T(8,128)(2,1)} %broadcast_in_dim.28), calls=%async_computation.1 | async-start | bytes 393216 | tf_op jit(solution)/shard_map/all_to_all | solution.py:255
  33.7 0.0 collective-permute-done.4.rest_5_
  33.7 0.3 collective-permute-start.5
  34.0 0.3 collective-permute-start.3
  34.3 0.2 collective-permute-start.1
  34.5 1.7 %collective-permute-start.8 = (bf16[6,96,128]{2,1,0:T(8,128)(2,1)}, bf16[6,96,128]{2,1,0:T(8,128)(2,1)S(1)}, u32[]{:S(2)}, u32[]{:S(2)}) collective-permute-start(bf16[6,96,128]{2,1,0:T(8,128)(2,1)} %collective-permute-done.6.rest_1_), channel_id=1, source_target_pairs={{0,1},{1,0},{2,3},{3,2},{4,5},{5,4},{6,7},{7,6},{8,9},{9,8},{10,11... | collective-permute-start | bytes 442376 | tf_op jit(solution)/shard_map/ppermute | solution.py:207
  36.2 0.0 collective-permute-done.10.rest_1_
  36.2 0.3 collective-permute-start.12
  36.6 0.0 collective-permute-done.5.rest_6_
  36.6 0.0 collective-permute-done.3.rest_4_
  36.6 0.0 collective-permute-done.1.rest_2_
  36.6 6.8 %shard_map.56.rest_0_ = f32[32,96,96]{2,1,0:T(8,128)S(1)} custom-call(s32[32]{0:T(128)S(1)} %reshape.34.kept_ref, s32[1]{0:T(128)} %bitcast.me_ref, bf16[32,128,128]{2,1,0:T(8,128)(2,1)S(1)} %pad.8.blocks_ref, f32[32,96,96]{2,1,0:T(8,128)S(1)} %shard_map.55.rest_0_, ...), custom_call_target="tpu_custom_call", output_to_operand_aliasing={{}: (3, {})} | custom-call | flops 32 | bytes 32 | tf_op jit(solution)/shard_map/pallas_call | solution.py:123
  43.4 0.1 collective-permute-start.7
  43.5 0.5 collective-permute-start.9
  44.0 0.1 collective-permute-start.11
  44.1 1.4 %collective-permute-done.12.rest_3_ = bf16[6,96,128]{2,1,0:T(8,128)(2,1)S(1)} collective-permute-done((bf16[6,96,128]{2,1,0:T(8,128)(2,1)S(1)}, bf16[6,96,128]{2,1,0:T(8,128)(2,1)S(1)}, u32[]{:S(2)}, u32[]{:S(2)}) %collective-permute-start.12) | collective-permute-done | bytes 147488 | tf_op jit(solution)/shard_map/ppermute | solution.py:207
  45.5 0.0 collective-permute-start.13
  45.5 0.0 collective-permute-done.7.rest_2_
  45.5 5.0 %shard_map.57.rest_0_ = f32[32,96,96]{2,1,0:T(8,128)S(1)} custom-call(s32[32]{0:T(128)S(1)} %reshape.34.kept_ref, s32[1]{0:T(128)} %bitcast.me_ref, bf16[32,128,128]{2,1,0:T(8,128)(2,1)S(1)} %pad.8.blocks_ref, f32[32,96,96]{2,1,0:T(8,128)S(1)} %shard_map.56.rest_0_, ...), custom_call_target="tpu_custom_call", output_to_operand_aliasing={{}: (3, {})} | custom-call | flops 32 | bytes 32 | tf_op jit(solution)/shard_map/pallas_call | solution.py:123
  50.5 4.2 %shard_map.58.total_ref = f32[32,96,96]{2,1,0:T(8,128)S(1)} custom-call(s32[32]{0:T(128)S(1)} %reshape.34.kept_ref, s32[1]{0:T(128)} %bitcast.me_ref, bf16[32,128,128]{2,1,0:T(8,128)(2,1)S(1)} %pad.8.blocks_ref, f32[32,96,96]{2,1,0:T(8,128)S(1)} %shard_map.57.rest_0_, ...), custom_call_target="tpu_custom_call", output_to_operand_aliasing={{}: (3, {})} | custom-call | flops 32 | bytes 32 | tf_op jit(solution)/shard_map/pallas_call | solution.py:123
  54.8 2.4 %shard_map.59 = bf16[8,4,9216]{2,1,0:T(4,128)(2,1)} custom-call(s32[32]{0:T(128)S(1)} %reshape.34.kept_ref, bf16[32,128,128]{2,1,0:T(8,128)(2,1)S(1)} %pad.8.blocks_ref, f32[32,96,96]{2,1,0:T(8,128)S(1)} %shard_map.58.total_ref, bf16[32,24,128]{2,1,0:T(8,128)(2,1)S(1)} %all-to-all-done.1.spread_ref), custom_call_target="tpu_custom_call" | custom-call | flops 32 | bytes 32 | tf_op jit(solution)/shard_map/pallas_call | solution.py:180
  (19 shorter events, 0.2 us)
Async XLA Ops:
  0.0 30.2 %copy-start = (bf16[1,96,96]{2,1,0:T(8,128)(2,1)S(1)}, bf16[1,96,96]{2,1,0:T(8,128)(2,1)}, u32[]{:S(2)}) copy-start(bf16[1,96,96]{2,1,0:T(8,128)(2,1)} %param.9) | copy-start | bytes 55300
  1.7 9.9 %copy-start.2 = (bf16[1,16,96,96]{3,2,1,0:T(8,128)(2,1)S(1)}, bf16[1,16,96,96]{3,2,1,0:T(8,128)(2,1)}, u32[]{:S(2)}) copy-start(bf16[1,16,96,96]{3,2,1,0:T(8,128)(2,1)} %param.8) | copy-start | bytes 884740
  4.1 25.0 %all-to-all-start = ((f32[32,1,2304]{2,1,0:T(1,128)}), f32[32,1,2304]{2,1,0:T(1,128)}, u32[]{:S(2)}, u32[]{:S(2)}) async-start(f32[32,1,2304]{2,1,0:T(1,128)} %copy.18), calls=%async_computation | async-start | bytes 589824 | tf_op jit(solution)/shard_map/all_to_all | solution.py:220
  11.6 8.8 %copy-start.1 = (bf16[8,4,9216]{2,1,0:T(4,128)(2,1)S(1)}, bf16[8,4,9216]{2,1,0:T(4,128)(2,1)}, u32[]{:S(2)}) copy-start(bf16[8,4,9216]{2,1,0:T(4,128)(2,1)} %param.5) | copy-start | bytes 1769476
  12.8 23.4 %collective-permute-start.10 = (bf16[6,96,128]{2,1,0:T(8,128)(2,1)}, bf16[6,96,128]{2,1,0:T(8,128)(2,1)S(1)}, u32[]{:S(2)}, u32[]{:S(2)}) collective-permute-start(bf16[6,96,128]{2,1,0:T(8,128)(2,1)} %bitcast.5), channel_id=1, source_target_pairs={{0,4},{1,5},{2,6},{3,7},{4,0},{5,1},{6,2},{7,3},{8,12},{9,13},{10,... | collective-permute-start | bytes 442376 | tf_op jit(solution)/shard_map/ppermute | solution.py:207
  15.4 19.1 %collective-permute-start.6 = (bf16[6,96,128]{2,1,0:T(8,128)(2,1)}, bf16[6,96,128]{2,1,0:T(8,128)(2,1)}, u32[]{:S(2)}, u32[]{:S(2)}) collective-permute-start(bf16[6,96,128]{2,1,0:T(8,128)(2,1)} %bitcast.5), channel_id=1, source_target_pairs={{0,6},{1,7},{2,4},{3,5},{4,2},{5,3},{6,0},{7,1},{8,14},{9,15},{10,... | collective-permute-start | bytes 442376 | tf_op jit(solution)/shard_map/ppermute | solution.py:207
  16.9 16.8 %collective-permute-start.4 = (bf16[6,96,128]{2,1,0:T(8,128)(2,1)}, bf16[6,96,128]{2,1,0:T(8,128)(2,1)S(1)}, u32[]{:S(2)}, u32[]{:S(2)}) collective-permute-start(bf16[6,96,128]{2,1,0:T(8,128)(2,1)} %bitcast.5), channel_id=1, source_target_pairs={{0,3},{1,2},{2,1},{3,0},{4,7},{5,6},{6,5},{7,4},{8,11},{9,10},{10,... | collective-permute-start | bytes 442376 | tf_op jit(solution)/shard_map/ppermute | solution.py:207
  17.8 16.2 %collective-permute-start.2 = (bf16[6,96,128]{2,1,0:T(8,128)(2,1)}, bf16[6,96,128]{2,1,0:T(8,128)(2,1)S(1)}, u32[]{:S(2)}, u32[]{:S(2)}) collective-permute-start(bf16[6,96,128]{2,1,0:T(8,128)(2,1)} %bitcast.5), channel_id=1, source_target_pairs={{0,2},{1,3},{2,0},{3,1},{4,6},{5,7},{6,4},{7,5},{8,10},{9,11},{10,... | collective-permute-start | bytes 442376 | tf_op jit(solution)/shard_map/ppermute | solution.py:207
  19.8 14.5 %collective-permute-start = (bf16[6,96,128]{2,1,0:T(8,128)(2,1)}, bf16[6,96,128]{2,1,0:T(8,128)(2,1)S(1)}, u32[]{:S(2)}, u32[]{:S(2)}) collective-permute-start(bf16[6,96,128]{2,1,0:T(8,128)(2,1)} %bitcast.5), channel_id=1, source_target_pairs={{0,1},{1,0},{2,3},{3,2},{4,5},{5,4},{6,7},{7,6},{8,9},{9,8},{10,11... | collective-permute-start | bytes 442376 | tf_op jit(solution)/shard_map/ppermute | solution.py:207
  31.1 23.7 %all-to-all-start.1 = ((bf16[32,24,128]{2,1,0:T(8,128)(2,1)}), bf16[32,24,128]{2,1,0:T(8,128)(2,1)S(1)}, u32[]{:S(2)}, u32[]{:S(2)}) async-start(bf16[32,24,128]{2,1,0:T(8,128)(2,1)} %broadcast_in_dim.28), calls=%async_computation.1 | async-start | bytes 393216 | tf_op jit(solution)/shard_map/all_to_all | solution.py:255
  33.7 2.9 %collective-permute-start.5 = (bf16[6,96,128]{2,1,0:T(8,128)(2,1)S(1)}, bf16[6,96,128]{2,1,0:T(8,128)(2,1)S(1)}, u32[]{:S(2)}, u32[]{:S(2)}) collective-permute-start(bf16[6,96,128]{2,1,0:T(8,128)(2,1)S(1)} %collective-permute-done.4.rest_5_), channel_id=1, source_target_pairs={{0,8},{8,0},{16,24},{24,16},{1,9},{9,1},{17,25},{25,17},{2,10},{10... | collective-permute-start | bytes 442376 | tf_op jit(solution)/shard_map/ppermute | solution.py:210
  34.0 2.6 %collective-permute-start.3 = (bf16[6,96,128]{2,1,0:T(8,128)(2,1)S(1)}, bf16[6,96,128]{2,1,0:T(8,128)(2,1)S(1)}, u32[]{:S(2)}, u32[]{:S(2)}) collective-permute-start(bf16[6,96,128]{2,1,0:T(8,128)(2,1)S(1)} %collective-permute-done.2.rest_3_), channel_id=1, source_target_pairs={{0,8},{8,0},{16,24},{24,16},{1,9},{9,1},{17,25},{25,17},{2,10},{10... | collective-permute-start | bytes 442376 | tf_op jit(solution)/shard_map/ppermute | solution.py:210
  34.3 2.3 %collective-permute-start.1 = (bf16[6,96,128]{2,1,0:T(8,128)(2,1)S(1)}, bf16[6,96,128]{2,1,0:T(8,128)(2,1)S(1)}, u32[]{:S(2)}, u32[]{:S(2)}) collective-permute-start(bf16[6,96,128]{2,1,0:T(8,128)(2,1)S(1)} %collective-permute-done.rest_1_), channel_id=1, source_target_pairs={{0,8},{8,0},{16,24},{24,16},{1,9},{9,1},{17,25},{25,17},{2,10},{10... | collective-permute-start | bytes 442376 | tf_op jit(solution)/shard_map/ppermute | solution.py:210
  34.5 9.0 %collective-permute-start.8 = (bf16[6,96,128]{2,1,0:T(8,128)(2,1)}, bf16[6,96,128]{2,1,0:T(8,128)(2,1)S(1)}, u32[]{:S(2)}, u32[]{:S(2)}) collective-permute-start(bf16[6,96,128]{2,1,0:T(8,128)(2,1)} %collective-permute-done.6.rest_1_), channel_id=1, source_target_pairs={{0,1},{1,0},{2,3},{3,2},{4,5},{5,4},{6,7},{7,6},{8,9},{9,8},{10,11... | collective-permute-start | bytes 442376 | tf_op jit(solution)/shard_map/ppermute | solution.py:207
  36.2 9.2 %collective-permute-start.12 = (bf16[6,96,128]{2,1,0:T(8,128)(2,1)S(1)}, bf16[6,96,128]{2,1,0:T(8,128)(2,1)S(1)}, u32[]{:S(2)}, u32[]{:S(2)}) collective-permute-start(bf16[6,96,128]{2,1,0:T(8,128)(2,1)S(1)} %collective-permute-done.10.rest_1_), channel_id=1, source_target_pairs={{0,1},{1,0},{2,3},{3,2},{4,5},{5,4},{6,7},{7,6},{8,9},{9,8},{10,11... | collective-permute-start | bytes 442376 | tf_op jit(solution)/shard_map/ppermute | solution.py:207
  43.4 2.1 %collective-permute-start.7 = (bf16[6,96,128]{2,1,0:T(8,128)(2,1)}, bf16[6,96,128]{2,1,0:T(8,128)(2,1)S(1)}, u32[]{:S(2)}, u32[]{:S(2)}) collective-permute-start(bf16[6,96,128]{2,1,0:T(8,128)(2,1)} %collective-permute-done.6.rest_1_), channel_id=1, source_target_pairs={{0,8},{8,0},{16,24},{24,16},{1,9},{9,1},{17,25},{25,17},{2,10},{10... | collective-permute-start | bytes 442376 | tf_op jit(solution)/shard_map/ppermute | solution.py:210
  43.5 2.0 %collective-permute-start.9 = (bf16[6,96,128]{2,1,0:T(8,128)(2,1)S(1)}, bf16[6,96,128]{2,1,0:T(8,128)(2,1)S(1)}, u32[]{:S(2)}, u32[]{:S(2)}) collective-permute-start(bf16[6,96,128]{2,1,0:T(8,128)(2,1)S(1)} %collective-permute-done.8.rest_3_), channel_id=1, source_target_pairs={{0,8},{8,0},{16,24},{24,16},{1,9},{9,1},{17,25},{25,17},{2,10},{10... | collective-permute-start | bytes 442376 | tf_op jit(solution)/shard_map/ppermute | solution.py:210
  44.0 6.5 %collective-permute-start.11 = (bf16[6,96,128]{2,1,0:T(8,128)(2,1)S(1)}, bf16[6,96,128]{2,1,0:T(8,128)(2,1)S(1)}, u32[]{:S(2)}, u32[]{:S(2)}) collective-permute-start(bf16[6,96,128]{2,1,0:T(8,128)(2,1)S(1)} %collective-permute-done.10.rest_1_), channel_id=1, source_target_pairs={{0,8},{8,0},{16,24},{24,16},{1,9},{9,1},{17,25},{25,17},{2,10},{10... | collective-permute-start | bytes 442376 | tf_op jit(solution)/shard_map/ppermute | solution.py:210
  45.5 5.1 %collective-permute-start.13 = (bf16[6,96,128]{2,1,0:T(8,128)(2,1)S(1)}, bf16[6,96,128]{2,1,0:T(8,128)(2,1)S(1)}, u32[]{:S(2)}, u32[]{:S(2)}) collective-permute-start(bf16[6,96,128]{2,1,0:T(8,128)(2,1)S(1)} %collective-permute-done.12.rest_3_), channel_id=1, source_target_pairs={{0,8},{8,0},{16,24},{24,16},{1,9},{9,1},{17,25},{25,17},{2,10},{10... | collective-permute-start | bytes 442376 | tf_op jit(solution)/shard_map/ppermute | solution.py:210

commit v4 on v3

--- a/solution.py
+++ b/solution.py
@@ -217,37 +217,26 @@
     part_sum = jnp.dot(weights, block_list, preferred_element_type=jnp.float32)
     share = flat // groups
     shares = part_sum.reshape(tiles, groups, share).transpose(1, 0, 2).reshape(groups * tiles, share)
-    arrived = lax.all_to_all(shares, ALL, split_axis=0, concat_axis=0, tiled=True)
     blocks = jnp.pad(block_list.reshape(rows, width, width), ((0, 0), (0, LANES - width), (0, LANES - width)))
     place = me.reshape(1)
     packed = pack_factors(ladder_factor[0])
     mine = lax.dynamic_index_in_dim(packed, core, 0, keepdims=False)
     half = tiles // 2
-    halves = {0: mine}
-    for up in range(across, tiles, across):
+    halves = {slot: to_tile(mine, slot) for slot in range(1, half)}
+    shares, *_ = lax.optimization_barrier((shares, *halves.values()))
+    arrived = lax.all_to_all(shares, ALL, split_axis=0, concat_axis=0, tiled=True)
+    for up in range(half, tiles, across):
         halves[up] = to_tile(mine, up)
-    total = ladder((0,), names, place, blocks, None, [packed[0], packed[1]], tiles, width, pairs, rows)
-
-    def cross(starts, gate):
-        for up in starts:
-            source = halves[up]
-            if up:
-                source, _ = lax.optimization_barrier((source, gate))
-                halves[up] = source
-            for side in range(1, across):
-                halves[up + side] = to_tile(source, side)
-
-    def stage(near, total, gate, cost):
+
+    def stage(near, total, cost):
         parts = []
         for slot in near:
-            parts += [halves[slot], to_core(halves[slot])]
-        total, _, *parts = lax.optimization_barrier((total, gate, *parts))
+            parts += [halves[slot], to_core(halves[slot])] if slot else [packed[0], packed[1]]
         return ladder(near, names, place, blocks, total, parts, tiles, width, pairs, cost)
 
-    for slot in range(1, half):
-        if slot % across:
-            halves[slot] = to_tile(mine, slot)
-    cross(range(half, tiles, across), total)
+    total = stage((0,), None, 1)
+    first = total
+    total = stage(tuple(range(1, half)), total, 1)
     arrived, _ = lax.optimization_barrier((arrived, total))
     running = jnp.sum(arrived, axis=0).astype(jnp.bfloat16).reshape(width // groups, width)
     hidden = jnp.dot(running, cycle_integral_tiles[0], preferred_element_type=jnp.float32).astype(jnp.bfloat16)
@@ -255,15 +244,12 @@
     spread = lax.all_to_all(
         jnp.broadcast_to(hidden[None], (groups * tiles,) + hidden.shape), ALL, split_axis=0, concat_axis=0, tiled=True
     )
-
-    early = tuple(range(1, half))
-    last = tuple(range(half, half + across))
-    middle = tuple(s for s in range(1, tiles) if s not in early + last)
-    total = stage(early, total, total, rows)
-    for slot in middle + last:
-        halves[slot], _ = lax.optimization_barrier((halves[slot], total))
-    total = stage(middle, total, total, rows)
-    total = stage(last, total, total, rows)
+    for up in range(half, tiles, across):
+        halves[up], _ = lax.optimization_barrier((halves[up], total))
+        for side in range(1, across):
+            halves[up + side] = to_tile(halves[up], side)
+    total = stage(tuple(range(half, tiles, across)), total, 1)
+    total = stage(tuple(s for s in range(half, tiles) if s % across), total, 1)
     return close(names, blocks, total, spread, tiles, width, amplitudes.shape)
 
 

time: 57.9 us -> 66.2 us (1.14)
  waiting for transfers between devices: 6.28 us -> 18 us
  local copies, waits for them, and re-layouts: 8.04 us -> 6.53 us
  starting transfers between devices: 21.1 us -> 20 us
    ppermute x7, waiting for transfers between devices: 1.4 us -> 14.9 us  [to_tile(): return lax.ppermute(array, 'tile', [(i, i ^ flip) for i in range(tiles)])]
    all_to_all x1, waiting for transfers between devices: 4.86 us -> 3.08 us  [on_device(): lax.all_to_all(shares, ALL, split_axis=0, concat_axis=0, tiled=True)]
    all_to_all x1, starting transfers between devices: 7.41 us -> 6.1 us  [on_device(): lax.all_to_all(shares, ALL, split_axis=0, concat_axis=0, tiled=True)]
    reshape x1, local copies, waits for them, and re-layouts: 1.25 us -> 0.14 us  [on_device(): block_list = amplitudes.reshape(rows, flat)]
    unnamed x10 -> x12, local copies, waits for them, and re-layouts: 2.76 us -> 3.14 us
  transfers between devices with their start and end apart: 16 -> 16, of which waited for: 2 -> 7; matrix products, arithmetic and copies ran while one was open for 8% -> 6% of each run, Pallas kernels for 33% -> 28%
where the time goes in v4:
time: 66.2 us; the launch traced here: 65.8 us
  Pallas kernels  20.6 us (31%)
  starting transfers between devices  20 us (30%)
  waiting for transfers between devices  18 us (27%)
  local copies, waits for them, and re-layouts  6.53 us (10%)
    pallas_call x4, Pallas kernels, ladder(): pl.pallas_call(functools.partial(ladder_kernel, near, tiles, width, len(c...  18.2 us
    ppermute x7, waiting for transfers between devices, to_tile(): return lax.ppermute(array, 'tile', [(i, i ^ flip) for i in range(tiles)])  14.9 us
    ppermute x7, starting transfers between devices, to_tile(): return lax.ppermute(array, 'tile', [(i, i ^ flip) for i in range(tiles)])  10.2 us
    all_to_all x1, starting transfers between devices, on_device(): lax.all_to_all(shares, ALL, split_axis=0, concat_axis=0, tiled=True)  6.1 us
    unnamed x12, local copies, waits for them, and re-layouts  3.14 us
    all_to_all x1, waiting for transfers between devices, on_device(): lax.all_to_all(shares, ALL, split_axis=0, concat_axis=0, tiled=True)  3.08 us
    all_to_all x1, starting transfers between devices, on_device(): lax.all_to_all(jnp.broadcast_to(hidden[None], (groups * tiles,) + hidden....  2.58 us
    pallas_call x1, Pallas kernels, close(): pl.pallas_call(functools.partial(close_kernel, tiles, width), out_shape=j...  2.46 us
  transfers between devices with their start and end apart: 16, of which 7 were waited for; matrix products, arithmetic and copies ran while one was open for 6% of the time, Pallas kernels for 28%

profile of v4, /device:TPU:0, one launch (start us, length us, event | category | flops | bytes accessed | tf_op | source)
XLA Modules:
  0.0 65.8 jit_solution(8792836236531746998)
XLA Ops:
  0.0 1.3 %copy.13 = bf16[1,16,96,96]{2,3,1,0:T(8,128)(2,1)S(1)} copy(bf16[1,16,96,96]{3,2,1,0:T(8,128)(2,1)} %param.8) | data formatting | bytes 589824 | tf_op args[3]
  1.3 0.0 copy-start.3
  1.3 0.1 maximum_maximum_fusion
  1.5 0.8 %copy.19 = bf16[1,6,96,128]{3,2,1,0:T(8,128)(2,1)} copy(bf16[1,6,96,128]{2,3,1,0:T(8,128)(2,1)S(1)} %constant_dynamic-slice_fusion) | data formatting | bytes 294912
  2.3 3.0 %collective-permute-start = (bf16[6,96,128]{2,1,0:T(8,128)(2,1)}, bf16[6,96,128]{2,1,0:T(8,128)(2,1)S(1)}, u32[]{:S(2)}, u32[]{:S(2)}) collective-permute-start(bf16[6,96,128]{2,1,0:T(8,128)(2,1)} %bitcast.5), channel_id=1, source_target_pairs={{0,1},{1,0},{2,3},{3,2},{4,5},{5,4},{6,7},{7,6},{8,9},{9,8},{10,11... | collective-permute-start | bytes 442376 | tf_op jit(solution)/shard_map/ppermute | solution.py:207
  5.2 1.6 %collective-permute-start.2 = (bf16[6,96,128]{2,1,0:T(8,128)(2,1)}, bf16[6,96,128]{2,1,0:T(8,128)(2,1)S(1)}, u32[]{:S(2)}, u32[]{:S(2)}) collective-permute-start(bf16[6,96,128]{2,1,0:T(8,128)(2,1)} %bitcast.5), channel_id=1, source_target_pairs={{0,2},{1,3},{2,0},{3,1},{4,6},{5,7},{6,4},{7,5},{8,10},{9,11},{10,... | collective-permute-start | bytes 442376 | tf_op jit(solution)/shard_map/ppermute | solution.py:207
  6.8 0.0 collective-permute-start.4
  6.8 0.1 copy.12
  6.9 0.1 reshape.35.kept_ref
  7.0 0.1 reshape.38
  7.1 0.1 broadcast_in_dim.24
  7.2 0.1 broadcast_in_dim.25
  7.3 0.2 convolution_bitcast_fusion
  7.5 1.8 %collective-permute-done.rest_1_ = bf16[6,96,128]{2,1,0:T(8,128)(2,1)S(1)} collective-permute-done((bf16[6,96,128]{2,1,0:T(8,128)(2,1)}, bf16[6,96,128]{2,1,0:T(8,128)(2,1)S(1)}, u32[]{:S(2)}, u32[]{:S(2)}) %collective-permute-start) | collective-permute-done | bytes 147488 | tf_op jit(solution)/shard_map/ppermute | solution.py:207
  9.3 2.9 %collective-permute-done.2.rest_3_ = bf16[6,96,128]{2,1,0:T(8,128)(2,1)S(1)} collective-permute-done((bf16[6,96,128]{2,1,0:T(8,128)(2,1)}, bf16[6,96,128]{2,1,0:T(8,128)(2,1)S(1)}, u32[]{:S(2)}, u32[]{:S(2)}) %collective-permute-start.2) | collective-permute-done | bytes 147488 | tf_op jit(solution)/shard_map/ppermute | solution.py:207
  12.2 1.5 %collective-permute-done.4.rest_5_ = bf16[6,96,128]{2,1,0:T(8,128)(2,1)S(1)} collective-permute-done((bf16[6,96,128]{2,1,0:T(8,128)(2,1)}, bf16[6,96,128]{2,1,0:T(8,128)(2,1)S(1)}, u32[]{:S(2)}, u32[]{:S(2)}) %collective-permute-start.4) | collective-permute-done | bytes 147488 | tf_op jit(solution)/shard_map/ppermute | solution.py:207
  13.7 0.9 %all_to_all.11 = f32[32,1,2304]{2,1,0:T(1,128)} reshape(f32[32,2304]{1,0:T(8,128)S(1)} %convolution_bitcast_fusion) | data formatting | bytes 589824 | tf_op jit(solution)/shard_map/all_to_all | solution.py:227
  14.6 6.1 %all-to-all-start = ((f32[32,1,2304]{2,1,0:T(1,128)}), f32[32,1,2304]{2,1,0:T(1,128)}, u32[]{:S(2)}, u32[]{:S(2)}) async-start(f32[32,1,2304]{2,1,0:T(1,128)} %all_to_all.11), calls=%async_computation | async-start | bytes 589824 | tf_op jit(solution)/shard_map/all_to_all | solution.py:227
  20.8 3.6 %collective-permute-start.8 = (bf16[6,96,128]{2,1,0:T(8,128)(2,1)}, bf16[6,96,128]{2,1,0:T(8,128)(2,1)}, u32[]{:S(2)}, u32[]{:S(2)}) collective-permute-start(bf16[6,96,128]{2,1,0:T(8,128)(2,1)} %bitcast.5), channel_id=1, source_target_pairs={{0,6},{1,7},{2,4},{3,5},{4,2},{5,3},{6,0},{7,1},{8,14},{9,15},{10,... | collective-permute-start | bytes 442376 | tf_op jit(solution)/shard_map/ppermute | solution.py:207
  24.4 0.0 collective-permute-start.6
  24.4 0.6 reshape_reshape.3
  25.0 0.1 collective-permute-start.1
  25.1 0.5 collective-permute-start.3
  25.6 0.1 collective-permute-start.5
  25.7 0.2 copy.14
  25.8 0.2 copy.15
  26.0 0.3 pad.8.blocks_ref
  26.3 2.6 %shard_map.55.rest_0_ = f32[32,96,96]{2,1,0:T(8,128)S(1)} custom-call(s32[32]{0:T(128)S(1)} %reshape.35.kept_ref, s32[1]{0:T(128)} %bitcast.me_ref, bf16[32,128,128]{2,1,0:T(8,128)(2,1)S(1)} %pad.8.blocks_ref, bf16[6,96,128]{2,1,0:T(8,128)(2,1)S(1)} %bitcast.25, bf16[6,96,128]{2,1,0:T(8,128)(2,1)S(1)} %bitcast.26), custom_call_target="tpu_custom_call" | custom-call | flops 1 | bytes 32 | tf_op jit(solution)/shard_map/pallas_call | solution.py:123
  28.9 0.0 collective-permute-done.1.rest_2_
  29.0 0.0 collective-permute-done.5.rest_6_
  29.0 6.4 %shard_map.56.rest_0_ = f32[32,96,96]{2,1,0:T(8,128)S(1)} custom-call(s32[32]{0:T(128)S(1)} %reshape.35.kept_ref, s32[1]{0:T(128)} %bitcast.me_ref, bf16[32,128,128]{2,1,0:T(8,128)(2,1)S(1)} %pad.8.blocks_ref, f32[32,96,96]{2,1,0:T(8,128)S(1)} %shard_map.55.rest_0_, ...), custom_call_target="tpu_custom_call", output_to_operand_aliasing={{}: (3, {})} | custom-call | flops 1 | bytes 32 | tf_op jit(solution)/shard_map/pallas_call | solution.py:123
  35.4 3.1 %all-to-all-done = f32[32,1,2304]{2,1,0:T(1,128)} async-done(((f32[32,1,2304]{2,1,0:T(1,128)}), f32[32,1,2304]{2,1,0:T(1,128)}, u32[]{:S(2)}, u32[]{:S(2)}) %all-to-all-start) | async-done | bytes 294944 | tf_op jit(solution)/shard_map/all_to_all | solution.py:227
  38.5 1.0 %copy.26 = f32[32,1,2304]{2,0,1:T(8,128)S(1)} copy(f32[32,1,2304]{2,1,0:T(1,128)} %all-to-all-done) | data formatting | bytes 589824
  39.5 0.1 convert_element_type.21
  39.6 0.1 convolution_convert_fusion
  39.8 0.7 %broadcast_in_dim.28 = bf16[32,24,128]{2,1,0:T(8,128)(2,1)} broadcast(bf16[24,128]{1,0:T(8,128)(2,1)S(1)} %pad.9), dimensions={1,2} | broadcast | bytes 202752 | tf_op jit(solution)/shard_map/broadcast_in_dim | solution.py:245
  40.5 2.6 %all-to-all-start.1 = ((bf16[32,24,128]{2,1,0:T(8,128)(2,1)}), bf16[32,24,128]{2,1,0:T(8,128)(2,1)S(1)}, u32[]{:S(2)}, u32[]{:S(2)}) async-start(bf16[32,24,128]{2,1,0:T(8,128)(2,1)} %broadcast_in_dim.28), calls=%async_computation.1 | async-start | bytes 393216 | tf_op jit(solution)/shard_map/all_to_all | solution.py:244
  43.1 0.0 collective-permute-done.8.rest_3_
  43.1 0.4 collective-permute-done.6.rest_1_
  43.5 1.5 %collective-permute-start.12 = (bf16[6,96,128]{2,1,0:T(8,128)(2,1)}, bf16[6,96,128]{2,1,0:T(8,128)(2,1)S(1)}, u32[]{:S(2)}, u32[]{:S(2)}) collective-permute-start(bf16[6,96,128]{2,1,0:T(8,128)(2,1)} %collective-permute-done.8.rest_3_), channel_id=1, source_target_pairs={{0,1},{1,0},{2,3},{3,2},{4,5},{5,4},{6,7},{7,6},{8,9},{9,8},{10,11... | collective-permute-start | bytes 442376 | tf_op jit(solution)/shard_map/ppermute | solution.py:207
  44.9 0.6 collective-permute-start.10
  45.5 0.0 collective-permute-start.9
  45.5 0.5 collective-permute-start.7
  46.0 5.7 %collective-permute-done.12.rest_3_ = bf16[6,96,128]{2,1,0:T(8,128)(2,1)S(1)} collective-permute-done((bf16[6,96,128]{2,1,0:T(8,128)(2,1)}, bf16[6,96,128]{2,1,0:T(8,128)(2,1)S(1)}, u32[]{:S(2)}, u32[]{:S(2)}) %collective-permute-start.12) | collective-permute-done | bytes 147488 | tf_op jit(solution)/shard_map/ppermute | solution.py:207
  51.7 2.5 %collective-permute-done.10.rest_1_ = bf16[6,96,128]{2,1,0:T(8,128)(2,1)S(1)} collective-permute-done((bf16[6,96,128]{2,1,0:T(8,128)(2,1)}, bf16[6,96,128]{2,1,0:T(8,128)(2,1)S(1)}, u32[]{:S(2)}, u32[]{:S(2)}) %collective-permute-start.10) | collective-permute-done | bytes 147488 | tf_op jit(solution)/shard_map/ppermute | solution.py:207
  54.2 3.9 %shard_map.57.rest_0_ = f32[32,96,96]{2,1,0:T(8,128)S(1)} custom-call(s32[32]{0:T(128)S(1)} %reshape.35.kept_ref, s32[1]{0:T(128)} %bitcast.me_ref, bf16[32,128,128]{2,1,0:T(8,128)(2,1)S(1)} %pad.8.blocks_ref, f32[32,96,96]{2,1,0:T(8,128)S(1)} %shard_map.56.rest_0_, ...), custom_call_target="tpu_custom_call", output_to_operand_aliasing={{}: (3, {})} | custom-call | flops 1 | bytes 32 | tf_op jit(solution)/shard_map/pallas_call | solution.py:123
  58.1 5.2 %shard_map.58.total_ref = f32[32,96,96]{2,1,0:T(8,128)S(1)} custom-call(s32[32]{0:T(128)S(1)} %reshape.35.kept_ref, s32[1]{0:T(128)} %bitcast.me_ref, bf16[32,128,128]{2,1,0:T(8,128)(2,1)S(1)} %pad.8.blocks_ref, f32[32,96,96]{2,1,0:T(8,128)S(1)} %shard_map.57.rest_0_, ...), custom_call_target="tpu_custom_call", output_to_operand_aliasing={{}: (3, {})} | custom-call | flops 1 | bytes 32 | tf_op jit(solution)/shard_map/pallas_call | solution.py:123
  63.4 2.5 %shard_map.59 = bf16[8,4,9216]{2,1,0:T(4,128)(2,1)} custom-call(s32[32]{0:T(128)S(1)} %reshape.35.kept_ref, bf16[32,128,128]{2,1,0:T(8,128)(2,1)S(1)} %pad.8.blocks_ref, f32[32,96,96]{2,1,0:T(8,128)S(1)} %shard_map.58.total_ref, bf16[32,24,128]{2,1,0:T(8,128)(2,1)S(1)} %all-to-all-done.1.spread_ref), custom_call_target="tpu_custom_call" | custom-call | flops 32 | bytes 32 | tf_op jit(solution)/shard_map/pallas_call | solution.py:180
  (21 shorter events, 0.2 us)
Async XLA Ops:
  0.0 39.6 %copy-start = (bf16[1,96,96]{2,1,0:T(8,128)(2,1)S(1)}, bf16[1,96,96]{2,1,0:T(8,128)(2,1)}, u32[]{:S(2)}) copy-start(bf16[1,96,96]{2,1,0:T(8,128)(2,1)} %param.9) | copy-start | bytes 55300
  0.0 6.8 %copy-start.2 = (s32[8,4]{0,1:T(4,128)S(1)}, s32[8,4]{0,1:T(4,128)}, u32[]{:S(2)}) copy-start(s32[8,4]{0,1:T(4,128)} %param.6) | copy-start | bytes 388
  0.0 7.0 %copy-start.1 = (bf16[8,4,9216]{2,1,0:T(4,128)(2,1)S(1)}, bf16[8,4,9216]{2,1,0:T(4,128)(2,1)}, u32[]{:S(2)}) copy-start(bf16[8,4,9216]{2,1,0:T(4,128)(2,1)} %param.5) | copy-start | bytes 1769476
  1.3 5.8 %copy-start.3 = (bf16[8]{0:T(256)(128)(2,1)S(1)}, bf16[8]{0:T(256)(128)(2,1)}, u32[]{:S(2)}) copy-start(bf16[8]{0:T(256)(128)(2,1)} %param.7) | copy-start | bytes 52
  2.3 7.0 %collective-permute-start = (bf16[6,96,128]{2,1,0:T(8,128)(2,1)}, bf16[6,96,128]{2,1,0:T(8,128)(2,1)S(1)}, u32[]{:S(2)}, u32[]{:S(2)}) collective-permute-start(bf16[6,96,128]{2,1,0:T(8,128)(2,1)} %bitcast.5), channel_id=1, source_target_pairs={{0,1},{1,0},{2,3},{3,2},{4,5},{5,4},{6,7},{7,6},{8,9},{9,8},{10,11... | collective-permute-start | bytes 442376 | tf_op jit(solution)/shard_map/ppermute | solution.py:207
  5.2 7.0 %collective-permute-start.2 = (bf16[6,96,128]{2,1,0:T(8,128)(2,1)}, bf16[6,96,128]{2,1,0:T(8,128)(2,1)S(1)}, u32[]{:S(2)}, u32[]{:S(2)}) collective-permute-start(bf16[6,96,128]{2,1,0:T(8,128)(2,1)} %bitcast.5), channel_id=1, source_target_pairs={{0,2},{1,3},{2,0},{3,1},{4,6},{5,7},{6,4},{7,5},{8,10},{9,11},{10,... | collective-permute-start | bytes 442376 | tf_op jit(solution)/shard_map/ppermute | solution.py:207
  6.8 6.9 %collective-permute-start.4 = (bf16[6,96,128]{2,1,0:T(8,128)(2,1)}, bf16[6,96,128]{2,1,0:T(8,128)(2,1)S(1)}, u32[]{:S(2)}, u32[]{:S(2)}) collective-permute-start(bf16[6,96,128]{2,1,0:T(8,128)(2,1)} %bitcast.5), channel_id=1, source_target_pairs={{0,3},{1,2},{2,1},{3,0},{4,7},{5,6},{6,5},{7,4},{8,11},{9,10},{10,... | collective-permute-start | bytes 442376 | tf_op jit(solution)/shard_map/ppermute | solution.py:207
  14.6 23.9 %all-to-all-start = ((f32[32,1,2304]{2,1,0:T(1,128)}), f32[32,1,2304]{2,1,0:T(1,128)}, u32[]{:S(2)}, u32[]{:S(2)}) async-start(f32[32,1,2304]{2,1,0:T(1,128)} %all_to_all.11), calls=%async_computation | async-start | bytes 589824 | tf_op jit(solution)/shard_map/all_to_all | solution.py:227
  20.8 22.3 %collective-permute-start.8 = (bf16[6,96,128]{2,1,0:T(8,128)(2,1)}, bf16[6,96,128]{2,1,0:T(8,128)(2,1)}, u32[]{:S(2)}, u32[]{:S(2)}) collective-permute-start(bf16[6,96,128]{2,1,0:T(8,128)(2,1)} %bitcast.5), channel_id=1, source_target_pairs={{0,6},{1,7},{2,4},{3,5},{4,2},{5,3},{6,0},{7,1},{8,14},{9,15},{10,... | collective-permute-start | bytes 442376 | tf_op jit(solution)/shard_map/ppermute | solution.py:207
  24.4 19.1 %collective-permute-start.6 = (bf16[6,96,128]{2,1,0:T(8,128)(2,1)}, bf16[6,96,128]{2,1,0:T(8,128)(2,1)}, u32[]{:S(2)}, u32[]{:S(2)}) collective-permute-start(bf16[6,96,128]{2,1,0:T(8,128)(2,1)} %bitcast.5), channel_id=1, source_target_pairs={{0,4},{1,5},{2,6},{3,7},{4,0},{5,1},{6,2},{7,3},{8,12},{9,13},{10,... | collective-permute-start | bytes 442376 | tf_op jit(solution)/shard_map/ppermute | solution.py:207
  25.0 3.9 %collective-permute-start.1 = (bf16[6,96,128]{2,1,0:T(8,128)(2,1)S(1)}, bf16[6,96,128]{2,1,0:T(8,128)(2,1)S(1)}, u32[]{:S(2)}, u32[]{:S(2)}) collective-permute-start(bf16[6,96,128]{2,1,0:T(8,128)(2,1)S(1)} %collective-permute-done.rest_1_), channel_id=1, source_target_pairs={{0,8},{8,0},{16,24},{24,16},{1,9},{9,1},{17,25},{25,17},{2,10},{10... | collective-permute-start | bytes 442376 | tf_op jit(solution)/shard_map/ppermute | solution.py:210
  25.1 3.9 %collective-permute-start.3 = (bf16[6,96,128]{2,1,0:T(8,128)(2,1)S(1)}, bf16[6,96,128]{2,1,0:T(8,128)(2,1)}, u32[]{:S(2)}, u32[]{:S(2)}) collective-permute-start(bf16[6,96,128]{2,1,0:T(8,128)(2,1)S(1)} %collective-permute-done.2.rest_3_), channel_id=1, source_target_pairs={{0,8},{8,0},{16,24},{24,16},{1,9},{9,1},{17,25},{25,17},{2,10},{10... | collective-permute-start | bytes 442376 | tf_op jit(solution)/shard_map/ppermute | solution.py:210
  25.6 3.4 %collective-permute-start.5 = (bf16[6,96,128]{2,1,0:T(8,128)(2,1)S(1)}, bf16[6,96,128]{2,1,0:T(8,128)(2,1)}, u32[]{:S(2)}, u32[]{:S(2)}) collective-permute-start(bf16[6,96,128]{2,1,0:T(8,128)(2,1)S(1)} %collective-permute-done.4.rest_5_), channel_id=1, source_target_pairs={{0,8},{8,0},{16,24},{24,16},{1,9},{9,1},{17,25},{25,17},{2,10},{10... | collective-permute-start | bytes 442376 | tf_op jit(solution)/shard_map/ppermute | solution.py:210
  40.5 22.9 %all-to-all-start.1 = ((bf16[32,24,128]{2,1,0:T(8,128)(2,1)}), bf16[32,24,128]{2,1,0:T(8,128)(2,1)S(1)}, u32[]{:S(2)}, u32[]{:S(2)}) async-start(bf16[32,24,128]{2,1,0:T(8,128)(2,1)} %broadcast_in_dim.28), calls=%async_computation.1 | async-start | bytes 393216 | tf_op jit(solution)/shard_map/all_to_all | solution.py:244
  43.5 8.3 %collective-permute-start.12 = (bf16[6,96,128]{2,1,0:T(8,128)(2,1)}, bf16[6,96,128]{2,1,0:T(8,128)(2,1)S(1)}, u32[]{:S(2)}, u32[]{:S(2)}) collective-permute-start(bf16[6,96,128]{2,1,0:T(8,128)(2,1)} %collective-permute-done.8.rest_3_), channel_id=1, source_target_pairs={{0,1},{1,0},{2,3},{3,2},{4,5},{5,4},{6,7},{7,6},{8,9},{9,8},{10,11... | collective-permute-start | bytes 442376 | tf_op jit(solution)/shard_map/ppermute | solution.py:207
  44.9 9.3 %collective-permute-start.10 = (bf16[6,96,128]{2,1,0:T(8,128)(2,1)}, bf16[6,96,128]{2,1,0:T(8,128)(2,1)S(1)}, u32[]{:S(2)}, u32[]{:S(2)}) collective-permute-start(bf16[6,96,128]{2,1,0:T(8,128)(2,1)} %collective-permute-done.6.rest_1_), channel_id=1, source_target_pairs={{0,1},{1,0},{2,3},{3,2},{4,5},{5,4},{6,7},{7,6},{8,9},{9,8},{10,11... | collective-permute-start | bytes 442376 | tf_op jit(solution)/shard_map/ppermute | solution.py:207
  45.5 8.7 %collective-permute-start.9 = (bf16[6,96,128]{2,1,0:T(8,128)(2,1)}, bf16[6,96,128]{2,1,0:T(8,128)(2,1)S(1)}, u32[]{:S(2)}, u32[]{:S(2)}) collective-permute-start(bf16[6,96,128]{2,1,0:T(8,128)(2,1)} %collective-permute-done.8.rest_3_), channel_id=1, source_target_pairs={{0,8},{8,0},{16,24},{24,16},{1,9},{9,1},{17,25},{25,17},{2,10},{10... | collective-permute-start | bytes 442376 | tf_op jit(solution)/shard_map/ppermute | solution.py:210
  45.5 8.7 %collective-permute-start.7 = (bf16[6,96,128]{2,1,0:T(8,128)(2,1)}, bf16[6,96,128]{2,1,0:T(8,128)(2,1)S(1)}, u32[]{:S(2)}, u32[]{:S(2)}) collective-permute-start(bf16[6,96,128]{2,1,0:T(8,128)(2,1)} %collective-permute-done.6.rest_1_), channel_id=1, source_target_pairs={{0,8},{8,0},{16,24},{24,16},{1,9},{9,1},{17,25},{25,17},{2,10},{10... | collective-permute-start | bytes 442376 | tf_op jit(solution)/shard_map/ppermute | solution.py:210
  51.7 6.4 %collective-permute-start.13 = (bf16[6,96,128]{2,1,0:T(8,128)(2,1)S(1)}, bf16[6,96,128]{2,1,0:T(8,128)(2,1)S(1)}, u32[]{:S(2)}, u32[]{:S(2)}) collective-permute-start(bf16[6,96,128]{2,1,0:T(8,128)(2,1)S(1)} %collective-permute-done.12.rest_3_), channel_id=1, source_target_pairs={{0,8},{8,0},{16,24},{24,16},{1,9},{9,1},{17,25},{25,17},{2,10},{10... | collective-permute-start | bytes 442376 | tf_op jit(solution)/shard_map/ppermute | solution.py:210
  54.2 3.9 %collective-permute-start.11 = (bf16[6,96,128]{2,1,0:T(8,128)(2,1)S(1)}, bf16[6,96,128]{2,1,0:T(8,128)(2,1)S(1)}, u32[]{:S(2)}, u32[]{:S(2)}) collective-permute-start(bf16[6,96,128]{2,1,0:T(8,128)(2,1)S(1)} %collective-permute-done.10.rest_1_), channel_id=1, source_target_pairs={{0,8},{8,0},{16,24},{24,16},{1,9},{9,1},{17,25},{25,17},{2,10},{10... | collective-permute-start | bytes 442376 | tf_op jit(solution)/shard_map/ppermute | solution.py:210

commit v5 on v4

--- a/solution.py
+++ b/solution.py
@@ -40,28 +40,18 @@
 def ladder_kernel(near, tiles, width, carried, kept_ref, me_ref, blocks_ref, *rest):
     rest = rest[carried:]
     factor_refs, total_ref = rest[:2 * len(near)], rest[2 * len(near)]
-    table, counts, jobs, landed, stacked, beside, grown, sems = rest[2 * len(near) + 1:]
+    table, counts, jobs, stacked, beside, grown = rest[2 * len(near) + 1:]
     rows = blocks_ref.shape[0]
     most = table.shape[0] // tiles
     me = me_ref[0]
-    copies = [pltpu.make_async_copy(ref, landed.at[i], sems.at[i]) for i, ref in enumerate(factor_refs)]
-    for copy in copies:
-        copy.start()
-
-    def clear(j, _):
-        counts[j] = 0
-        return 0
-
-    lax.fori_loop(0, tiles, clear, 0)
-
-    def fill(r, _):
-        slot = kept_ref[r] ^ me
+    slots = kept_ref.shape[0]
+    for slot in range(tiles):
+        counts[slot] = 0
+    for r in range(rows):
+        slot = kept_ref[r % slots, r // slots] ^ me
         n = counts[slot]
         table[slot * most + n] = r
         counts[slot] = n + 1
-        return 0
-
-    lax.fori_loop(0, rows, fill, 0)
 
     last = jnp.int32(0)
     for number, slot in enumerate(near):
@@ -75,9 +65,7 @@
 
         last = lax.fori_loop(0, (count + 1) // 2, add, last)
     for number in range(len(near)):
-        copies[2 * number].wait()
-        copies[2 * number + 1].wait()
-        unpack((landed.at[2 * number], landed.at[2 * number + 1]), stacked.at[number], beside.at[number], width)
+        unpack(factor_refs[2 * number:2 * number + 2], stacked.at[number], beside.at[number], width)
 
     factor_count = stacked.shape[1] // width
     step = 4
@@ -123,18 +111,16 @@
     return pl.pallas_call(
         functools.partial(ladder_kernel, near, tiles, width, len(carried)),
         out_shape=jax.ShapeDtypeStruct((rows, width, width), jnp.float32),
-        in_specs=[SMEM, SMEM] + [VMEM] * (1 + len(carried)) + [FREE] * len(parts),
+        in_specs=[SMEM, SMEM] + [VMEM] * (1 + len(carried)) + [VMEM] * len(parts),
         out_specs=VMEM,
         input_output_aliases={} if total is None else {3: 0},
         scratch_shapes=[
             pltpu.SMEM((tiles * most,), jnp.int32),
             pltpu.SMEM((tiles,), jnp.int32),
             pltpu.SMEM((3 * (rows + tiles),), jnp.int32),
-            pltpu.VMEM((len(parts),) + parts[0].shape, jnp.bfloat16),
             pltpu.VMEM((len(near), factor_count * width, LANES), jnp.bfloat16),
             pltpu.VMEM((len(near), width, factor_count * LANES), jnp.bfloat16),
             pltpu.VMEM((2, 2 * width, factor_count * LANES), jnp.bfloat16),
-            pltpu.SemaphoreType.DMA((len(parts),)),
         ],
         compiler_params=pltpu.CompilerParams(vmem_limit_bytes=(10 << 20) + (len(near) << 21)),
         cost_estimate=pl.CostEstimate(flops=cost, bytes_accessed=rows, transcendentals=0),
@@ -158,7 +144,7 @@
     for pair in range(pairs):
         for slot in range(slots):
             r = pair * slots + slot
-            term = jnp.dot(blocks_ref[r, :width, :], hidden[kept_ref[r]], preferred_element_type=jnp.float32)
+            term = jnp.dot(blocks_ref[r, :width, :], hidden[kept_ref[slot, pair]], preferred_element_type=jnp.float32)
             square[r, :, :width] = total_ref[r] + term[:, :width]
             quarter = [square[r, pl.ds(j, width // 4, stride=4), :] for j in range(4)]
             second = pltpu.roll(quarter[1], width, 1)
@@ -194,6 +180,82 @@
     )(kept, blocks, total, spread)
 
 
+def prepare_kernel(tiles, width, kept_ref, coef_ref, flat_ref, blocks_ref, shares_ref, lines, square, partial):
+    pairs, slots, flat = flat_ref.shape
+    count, share, _ = shares_ref.shape
+    length = flat // LANES
+    parts = width * 4 // LANES
+    spare = LANES - width
+    partial[...] = jnp.zeros_like(partial)
+    scales = coef_ref[...].astype(jnp.float32)
+    lane = lax.broadcasted_iota(jnp.int32, (width // 4, LANES), 1)
+    foot = jnp.zeros((spare, LANES), jnp.bfloat16)
+    for pair in range(pairs):
+        for t in range(length):
+            lines[pair, pl.ds(t, slots, stride=length), :] = flat_ref[pair, :, t * LANES:(t + 1) * LANES].astype(jnp.float32)
+        for slot in range(slots):
+            r = pair * slots + slot
+            first, second, third = (lines[pair, pl.ds(slot * length + i, width // 4, stride=parts), :] for i in range(parts))
+            quarters = (
+                first,
+                jnp.where(lane < spare, pltpu.roll(first, spare, 1), pltpu.roll(second, spare, 1)),
+                jnp.where(lane < 2 * spare, pltpu.roll(second, 2 * spare, 1), pltpu.roll(third, 2 * spare, 1)),
+                pltpu.roll(third, width, 1),
+            )
+            for j in range(4):
+                square[r, pl.ds(j, width // 4, stride=4), :] = jnp.where(lane < width, quarters[j], 0.0)
+            block = square[r]
+            blocks_ref[r, :width, :] = block.astype(jnp.bfloat16)
+            blocks_ref[r, width:, :] = foot
+            partial[kept_ref[slot, pair]] += block * scales[:, pair:pair + 1]
+    for i in range(count):
+        begin = i // tiles * share
+        shares_ref[i] = partial[i % tiles, begin:begin + share, :]
+
+
+def prepare(kept, coef, amplitudes, tiles, groups, width):
+    pairs, slots, flat = amplitudes.shape
+    rows = pairs * slots
+    return pl.pallas_call(
+        functools.partial(prepare_kernel, tiles, width),
+        out_shape=(
+            jax.ShapeDtypeStruct((rows, LANES, LANES), jnp.bfloat16),
+            jax.ShapeDtypeStruct((groups * tiles, width // groups, LANES), jnp.float32),
+        ),
+        in_specs=[SMEM, VMEM, VMEM],
+        out_specs=(VMEM, VMEM),
+        scratch_shapes=[
+            pltpu.VMEM((pairs, slots * flat // LANES, LANES), jnp.float32),
+            pltpu.VMEM((rows, width, LANES), jnp.float32),
+            pltpu.VMEM((tiles, width, LANES), jnp.float32),
+        ],
+        compiler_params=pltpu.CompilerParams(vmem_limit_bytes=56 << 20),
+        cost_estimate=pl.CostEstimate(flops=rows, bytes_accessed=rows, transcendentals=0),
+    )(kept, coef, amplitudes)
+
+
+def hide_kernel(arrived_ref, integral_ref, out_ref):
+    width = integral_ref.shape[-1]
+    count, share, _ = out_ref.shape
+    running = jnp.sum(arrived_ref[...], axis=0)[:, :width].astype(jnp.bfloat16)
+    hidden = jnp.dot(running, integral_ref[0], preferred_element_type=jnp.float32).astype(jnp.bfloat16)
+    tail = jnp.zeros((share, LANES - width), jnp.bfloat16)
+    for i in range(count):
+        out_ref[i, :, :width] = hidden
+        out_ref[i, :, width:] = tail
+
+
+def hide(arrived, integral):
+    return pl.pallas_call(
+        hide_kernel,
+        out_shape=jax.ShapeDtypeStruct(arrived.shape, jnp.bfloat16),
+        in_specs=[VMEM, VMEM],
+        out_specs=VMEM,
+        compiler_params=pltpu.CompilerParams(vmem_limit_bytes=8 << 20),
+        cost_estimate=pl.CostEstimate(flops=1000, bytes_accessed=1000, transcendentals=0),
+    )(arrived, integral)
+
+
 def on_device(amplitudes, kept, coef, ladder_factor, cycle_integral_tiles):
     pairs, slots, flat = amplitudes.shape
     width = ladder_factor.shape[-1]
@@ -209,47 +271,39 @@
     def to_core(array):
         return lax.ppermute(array, "grp", [(i, i ^ 1) for i in range(groups)])
 
-    block_list = amplitudes.reshape(rows, flat)
-    names = kept.reshape(rows)
-    weights = jnp.where(
-        jnp.arange(tiles, dtype=jnp.int32)[:, None] == names[None, :], jnp.repeat(coef, slots)[None, :], jnp.zeros((), coef.dtype)
-    )
-    part_sum = jnp.dot(weights, block_list, preferred_element_type=jnp.float32)
-    share = flat // groups
-    shares = part_sum.reshape(tiles, groups, share).transpose(1, 0, 2).reshape(groups * tiles, share)
-    blocks = jnp.pad(block_list.reshape(rows, width, width), ((0, 0), (0, LANES - width), (0, LANES - width)))
+    names = kept.T
+    blocks, shares = prepare(names, coef.reshape(1, pairs), amplitudes, tiles, groups, width)
+    arrived = lax.all_to_all(shares, ALL, split_axis=0, concat_axis=0, tiled=True)
     place = me.reshape(1)
     packed = pack_factors(ladder_factor[0])
     mine = lax.dynamic_index_in_dim(packed, core, 0, keepdims=False)
     half = tiles // 2
     halves = {slot: to_tile(mine, slot) for slot in range(1, half)}
-    shares, *_ = lax.optimization_barrier((shares, *halves.values()))
-    arrived = lax.all_to_all(shares, ALL, split_axis=0, concat_axis=0, tiled=True)
-    for up in range(half, tiles, across):
-        halves[up] = to_tile(mine, up)
-
-    def stage(near, total, cost):
+
+    def stage(near, total):
         parts = []
         for slot in near:
             parts += [halves[slot], to_core(halves[slot])] if slot else [packed[0], packed[1]]
-        return ladder(near, names, place, blocks, total, parts, tiles, width, pairs, cost)
-
-    total = stage((0,), None, 1)
+        return ladder(near, names, place, blocks, total, parts, tiles, width, pairs, rows)
+
+    total = stage((0,), None)
     first = total
-    total = stage(tuple(range(1, half)), total, 1)
-    arrived, _ = lax.optimization_barrier((arrived, total))
-    running = jnp.sum(arrived, axis=0).astype(jnp.bfloat16).reshape(width // groups, width)
-    hidden = jnp.dot(running, cycle_integral_tiles[0], preferred_element_type=jnp.float32).astype(jnp.bfloat16)
-    hidden = jnp.pad(hidden, ((0, 0), (0, LANES - width)))
-    spread = lax.all_to_all(
-        jnp.broadcast_to(hidden[None], (groups * tiles,) + hidden.shape), ALL, split_axis=0, concat_axis=0, tiled=True
-    )
+    far = mine
     for up in range(half, tiles, across):
-        halves[up], _ = lax.optimization_barrier((halves[up], total))
+        halves[up] = to_tile(far, up)
+    arrived, _ = lax.optimization_barrier((arrived, first))
+    hidden = hide(arrived, cycle_integral_tiles)
+    spread = lax.all_to_all(hidden, ALL, split_axis=0, concat_axis=0, tiled=True)
+    for up in range(half, tiles, across):
+        halves[up], _ = lax.optimization_barrier((halves[up], hidden))
         for side in range(1, across):
             halves[up + side] = to_tile(halves[up], side)
-    total = stage(tuple(range(half, tiles, across)), total, 1)
-    total = stage(tuple(s for s in range(half, tiles) if s % across), total, 1)
+    total = stage(tuple(range(1, half)), total)
+    for slot in range(half, tiles):
+        if slot % across:
+            halves[slot], _ = lax.optimization_barrier((halves[slot], total))
+    total = stage(tuple(range(half, tiles, across)), total)
+    total = stage(tuple(s for s in range(half, tiles) if s % across), total)
     return close(names, blocks, total, spread, tiles, width, amplitudes.shape)
 
 

time: 66.2 us -> 54 us (0.82)
  the two profiles are of different devices: /device:TPU:0 before, /device:TPU:1 now
where the time goes in v5:
time: 54 us; the launch traced here: 53.2 us
  starting transfers between devices  21.6 us (40%)
  Pallas kernels  21.4 us (40%)
  waiting for transfers between devices  8.54 us (16%)
  local copies, waits for them, and re-layouts  1.44 us (3%)
    pallas_call x4, Pallas kernels, ladder(): pl.pallas_call(functools.partial(ladder_kernel, near, tiles, width, len(c...  15 us
    ppermute x7, starting transfers between devices, to_tile(): return lax.ppermute(array, 'tile', [(i, i ^ flip) for i in range(tiles)])  8.67 us
    all_to_all x1, starting transfers between devices, on_device(): lax.all_to_all(shares, ALL, split_axis=0, concat_axis=0, tiled=True)  7.1 us
    all_to_all x1, waiting for transfers between devices, on_device(): lax.all_to_all(shares, ALL, split_axis=0, concat_axis=0, tiled=True)  5.9 us
    ppermute x7, starting transfers between devices, to_core(): return lax.ppermute(array, 'grp', [(i, i ^ 1) for i in range(groups)])  3.15 us
    pallas_call x1, Pallas kernels, prepare(): pl.pallas_call(functools.partial(prepare_kernel, tiles, width), out_shape...  3.03 us
    all_to_all x1, starting transfers between devices, on_device(): lax.all_to_all(hidden, ALL, split_axis=0, concat_axis=0, tiled=True)  2.63 us
    ppermute x7, waiting for transfers between devices, to_tile(): return lax.ppermute(array, 'tile', [(i, i ^ flip) for i in range(tiles)])  2.62 us
  transfers between devices with their start and end apart: 16, of which 3 were waited for; matrix products, arithmetic and copies ran while one was open for 3% of the time, Pallas kernels for 30%

profile of v5, /device:TPU:1, one launch (start us, length us, event | category | flops | bytes accessed | tf_op | source)
XLA Modules:
  0.0 53.2 jit_solution(2698271554697245123)
XLA Ops:
  0.0 3.0 %shard_map.55 = (bf16[32,128,128]{2,1,0:T(8,128)(2,1)}, f32[32,24,128]{2,1,0:T(8,128)}) custom-call(s32[4,8]{1,0:T(4,128)} %bitcast.10, bf16[1,8]{1,0:T(2,128)(2,1)} %bitcast.19, bf16[8,4,9216]{2,1,0:T(4,128)(2,1)} %flat_ref.1), custom_call_target="tpu_custom_call" | custom-call | flops 32 | bytes 32 | tf_op jit(solution)/shard_map/pallas_call | solution.py:219
  3.0 7.1 %all-to-all-start = ((f32[32,24,128]{2,1,0:T(8,128)}), f32[32,24,128]{2,1,0:T(8,128)S(1)}, u32[]{:S(2)}, u32[]{:S(2)}) async-start(f32[32,24,128]{2,1,0:T(8,128)} %get-tuple-element.13), calls=%async_computation | async-start | bytes 786432 | tf_op jit(solution)/shard_map/all_to_all | solution.py:276
  10.1 0.0 copy-done.3
  10.2 0.2 copy.9
  10.4 0.0 copy-start.1
  10.5 0.1 maximum_maximum_fusion
  10.6 0.8 %copy.13 = bf16[1,6,96,128]{3,2,1,0:T(8,128)(2,1)} copy(bf16[1,6,96,128]{2,3,1,0:T(8,128)(2,1)S(1)} %constant_dynamic-slice_fusion) | data formatting | bytes 294912
  11.4 2.3 %collective-permute-start.6 = (bf16[6,96,128]{2,1,0:T(8,128)(2,1)}, bf16[6,96,128]{2,1,0:T(8,128)(2,1)S(1)}, u32[]{:S(2)}, u32[]{:S(2)}) collective-permute-start(bf16[6,96,128]{2,1,0:T(8,128)(2,1)} %bitcast.7), channel_id=1, source_target_pairs={{0,4},{1,5},{2,6},{3,7},{4,0},{5,1},{6,2},{7,3},{8,12},{9,13},{10,... | collective-permute-start | bytes 442376 | tf_op jit(solution)/shard_map/ppermute | solution.py:269
  13.7 1.2 %collective-permute-start = (bf16[6,96,128]{2,1,0:T(8,128)(2,1)}, bf16[6,96,128]{2,1,0:T(8,128)(2,1)}, u32[]{:S(2)}, u32[]{:S(2)}) collective-permute-start(bf16[6,96,128]{2,1,0:T(8,128)(2,1)} %bitcast.7), channel_id=1, source_target_pairs={{0,1},{1,0},{2,3},{3,2},{4,5},{5,4},{6,7},{7,6},{8,9},{9,8},{10,11... | collective-permute-start | bytes 442376 | tf_op jit(solution)/shard_map/ppermute | solution.py:269
  14.9 1.2 %collective-permute-start.2 = (bf16[6,96,128]{2,1,0:T(8,128)(2,1)}, bf16[6,96,128]{2,1,0:T(8,128)(2,1)}, u32[]{:S(2)}, u32[]{:S(2)}) collective-permute-start(bf16[6,96,128]{2,1,0:T(8,128)(2,1)} %bitcast.7), channel_id=1, source_target_pairs={{0,2},{1,3},{2,0},{3,1},{4,6},{5,7},{6,4},{7,5},{8,10},{9,11},{10,... | collective-permute-start | bytes 442376 | tf_op jit(solution)/shard_map/ppermute | solution.py:269
  16.1 0.2 collective-permute-start.4
  16.3 1.2 %collective-permute-start.8 = (bf16[6,96,128]{2,1,0:T(8,128)(2,1)}, bf16[6,96,128]{2,1,0:T(8,128)(2,1)}, u32[]{:S(2)}, u32[]{:S(2)}) collective-permute-start(bf16[6,96,128]{2,1,0:T(8,128)(2,1)} %bitcast.7), channel_id=1, source_target_pairs={{0,6},{1,7},{2,4},{3,5},{4,2},{5,3},{6,0},{7,1},{8,14},{9,15},{10,... | collective-permute-start | bytes 442376 | tf_op jit(solution)/shard_map/ppermute | solution.py:269
  17.5 0.2 copy.10
  17.7 0.0 copy-start.2
  17.7 0.2 copy.11
  17.9 0.0 copy-done
  17.9 2.9 %shard_map.56.rest_0_ = f32[32,96,96]{2,1,0:T(8,128)S(1)} custom-call(s32[4,8]{1,0:T(4,128)S(1)} %bitcast.11, s32[1]{0:T(128)} %bitcast.2.me_ref, bf16[32,128,128]{2,1,0:T(8,128)(2,1)S(1)} %copy-done, bf16[6,96,128]{2,1,0:T(8,128)(2,1)S(1)} %bitcast.8, bf16[6,96,128]{2,1,0:T(8,128)(2,1)S(1)} %bitcast.9), custom_call_target="tpu_custom_call" | custom-call | flops 32 | bytes 32 | tf_op jit(solution)/shard_map/pallas_call | solution.py:111
  20.8 5.9 %all-to-all-done.arrived_ref = f32[32,24,128]{2,1,0:T(8,128)S(1)} async-done(((f32[32,24,128]{2,1,0:T(8,128)}), f32[32,24,128]{2,1,0:T(8,128)S(1)}, u32[]{:S(2)}, u32[]{:S(2)}) %all-to-all-start) | async-done | bytes 393248 | tf_op jit(solution)/shard_map/all_to_all | solution.py:276
  26.7 0.9 %shard_map.58 = bf16[32,24,128]{2,1,0:T(8,128)(2,1)} custom-call(f32[32,24,128]{2,1,0:T(8,128)S(1)} %all-to-all-done.arrived_ref, bf16[1,96,96]{2,1,0:T(8,128)(2,1)S(1)} %copy-done.2), custom_call_target="tpu_custom_call" | custom-call | flops 1000 | bytes 1000 | tf_op jit(solution)/shard_map/pallas_call | solution.py:249
  27.6 2.6 %all-to-all-start.1 = ((bf16[32,24,128]{2,1,0:T(8,128)(2,1)}), bf16[32,24,128]{2,1,0:T(8,128)(2,1)S(1)}, u32[]{:S(2)}, u32[]{:S(2)}) async-start(bf16[32,24,128]{2,1,0:T(8,128)(2,1)} %shard_map.58), calls=%async_computation.1 | async-start | bytes 393216 | tf_op jit(solution)/shard_map/all_to_all | solution.py:296
  30.2 0.0 collective-permute-done.rest_1_
  30.2 0.5 collective-permute-start.1
  30.7 0.0 collective-permute-done.2.rest_3_
  30.7 0.1 collective-permute-start.3
  30.8 0.0 collective-permute-done.4.rest_5_
  30.8 0.4 collective-permute-start.5
  31.2 0.0 collective-permute-done.6.rest_1_
  31.2 1.4 %collective-permute-start.10 = (bf16[6,96,128]{2,1,0:T(8,128)(2,1)S(1)}, bf16[6,96,128]{2,1,0:T(8,128)(2,1)S(1)}, u32[]{:S(2)}, u32[]{:S(2)}) collective-permute-start(bf16[6,96,128]{2,1,0:T(8,128)(2,1)S(1)} %collective-permute-done.6.rest_1_), channel_id=1, source_target_pairs={{0,1},{1,0},{2,3},{3,2},{4,5},{5,4},{6,7},{7,6},{8,9},{9,8},{10,11... | collective-permute-start | bytes 442376 | tf_op jit(solution)/shard_map/ppermute | solution.py:269
  32.6 0.8 %collective-permute-done.8.rest_3_ = bf16[6,96,128]{2,1,0:T(8,128)(2,1)} collective-permute-done((bf16[6,96,128]{2,1,0:T(8,128)(2,1)}, bf16[6,96,128]{2,1,0:T(8,128)(2,1)}, u32[]{:S(2)}, u32[]{:S(2)}) %collective-permute-start.8) | collective-permute-done | bytes 147488 | tf_op jit(solution)/shard_map/ppermute | solution.py:269
  33.3 1.2 %collective-permute-start.12 = (bf16[6,96,128]{2,1,0:T(8,128)(2,1)}, bf16[6,96,128]{2,1,0:T(8,128)(2,1)S(1)}, u32[]{:S(2)}, u32[]{:S(2)}) collective-permute-start(bf16[6,96,128]{2,1,0:T(8,128)(2,1)} %collective-permute-done.8.rest_3_), channel_id=1, source_target_pairs={{0,1},{1,0},{2,3},{3,2},{4,5},{5,4},{6,7},{7,6},{8,9},{9,8},{10,11... | collective-permute-start | bytes 442376 | tf_op jit(solution)/shard_map/ppermute | solution.py:269
  34.5 0.0 collective-permute-done.1.rest_2_
  34.5 1.3 %collective-permute-start.7 = (bf16[6,96,128]{2,1,0:T(8,128)(2,1)S(1)}, bf16[6,96,128]{2,1,0:T(8,128)(2,1)S(1)}, u32[]{:S(2)}, u32[]{:S(2)}) collective-permute-start(bf16[6,96,128]{2,1,0:T(8,128)(2,1)S(1)} %collective-permute-done.6.rest_1_), channel_id=1, source_target_pairs={{0,8},{8,0},{16,24},{24,16},{1,9},{9,1},{17,25},{25,17},{2,10},{10... | collective-permute-start | bytes 442376 | tf_op jit(solution)/shard_map/ppermute | solution.py:272
  35.8 0.0 collective-permute-done.3.rest_4_
  35.8 0.1 collective-permute-start.9
  35.9 0.0 collective-permute-done.5.rest_6_
  35.9 3.7 %shard_map.57.rest_0_ = f32[32,96,96]{2,1,0:T(8,128)S(1)} custom-call(s32[4,8]{1,0:T(4,128)S(1)} %bitcast.12, s32[1]{0:T(128)} %bitcast.2.me_ref, bf16[32,128,128]{2,1,0:T(8,128)(2,1)S(1)} %copy-done, f32[32,96,96]{2,1,0:T(8,128)S(1)} %shard_map.56.rest_0_, bf16[6,96,128]{2,1,0:T(8,128)(2,1)} %collective-permute-done.rest_1_, ...), custom_call_target="tpu_custom_call", output_to_operand_aliasing={{}: (3, {})} | custom-call | flops 32 | bytes 32 | tf_op jit(solution)/shard_map/pallas_call | solution.py:111
  39.6 0.0 collective-permute-done.10.rest_1_
  39.6 1.8 %collective-permute-done.12.rest_3_ = bf16[6,96,128]{2,1,0:T(8,128)(2,1)S(1)} collective-permute-done((bf16[6,96,128]{2,1,0:T(8,128)(2,1)}, bf16[6,96,128]{2,1,0:T(8,128)(2,1)S(1)}, u32[]{:S(2)}, u32[]{:S(2)}) %collective-permute-start.12) | collective-permute-done | bytes 147488 | tf_op jit(solution)/shard_map/ppermute | solution.py:269
  41.4 0.8 %collective-permute-start.11 = (bf16[6,96,128]{2,1,0:T(8,128)(2,1)S(1)}, bf16[6,96,128]{2,1,0:T(8,128)(2,1)S(1)}, u32[]{:S(2)}, u32[]{:S(2)}) collective-permute-start(bf16[6,96,128]{2,1,0:T(8,128)(2,1)S(1)} %collective-permute-done.10.rest_1_), channel_id=1, source_target_pairs={{0,8},{8,0},{16,24},{24,16},{1,9},{9,1},{17,25},{25,17},{2,10},{10... | collective-permute-start | bytes 442376 | tf_op jit(solution)/shard_map/ppermute | solution.py:272
  42.3 0.0 collective-permute-start.13
  42.3 0.0 collective-permute-done.7.rest_2_
  42.3 0.0 collective-permute-done.9.rest_4_
  42.3 4.4 %shard_map.59.rest_0_ = f32[32,96,96]{2,1,0:T(8,128)S(1)} custom-call(s32[4,8]{1,0:T(4,128)S(1)} %bitcast.13, s32[1]{0:T(128)} %bitcast.2.me_ref, bf16[32,128,128]{2,1,0:T(8,128)(2,1)S(1)} %copy-done, f32[32,96,96]{2,1,0:T(8,128)S(1)} %shard_map.57.rest_0_, bf16[6,96,128]{2,1,0:T(8,128)(2,1)S(1)} %collective-permute-done.6.rest_1_, ...), custom_call_target="tpu_custom_call", output_to_operand_aliasing={{}: (3, {})} | custom-call | flops 32 | bytes 32 | tf_op jit(solution)/shard_map/pallas_call | solution.py:111
  46.7 0.0 collective-permute-done.11.rest_2_
  46.7 0.0 collective-permute-done.13.rest_4_
  46.7 4.0 %shard_map.60.total_ref = f32[32,96,96]{2,1,0:T(8,128)S(1)} custom-call(s32[4,8]{1,0:T(4,128)S(1)} %bitcast.14, s32[1]{0:T(128)} %bitcast.2.me_ref, bf16[32,128,128]{2,1,0:T(8,128)(2,1)S(1)} %copy-done, f32[32,96,96]{2,1,0:T(8,128)S(1)} %shard_map.59.rest_0_, ...), custom_call_target="tpu_custom_call", output_to_operand_aliasing={{}: (3, {})} | custom-call | flops 32 | bytes 32 | tf_op jit(solution)/shard_map/pallas_call | solution.py:111
  50.7 0.0 all-to-all-done.1.spread_ref
  50.7 2.5 %shard_map.61 = bf16[8,4,9216]{2,1,0:T(4,128)(2,1)} custom-call(s32[4,8]{1,0:T(4,128)S(1)} %bitcast.15, bf16[32,128,128]{2,1,0:T(8,128)(2,1)S(1)} %copy-done, f32[32,96,96]{2,1,0:T(8,128)S(1)} %shard_map.60.total_ref, bf16[32,24,128]{2,1,0:T(8,128)(2,1)S(1)} %all-to-all-done.1.spread_ref), custom_call_target="tpu_custom_call" | custom-call | flops 32 | bytes 32 | tf_op jit(solution)/shard_map/pallas_call | solution.py:166
  (8 shorter events, 0.1 us)
Async XLA Ops:
  0.0 10.2 %copy-start.3 = (bf16[1,16,96,96]{3,2,1,0:T(8,128)(2,1)S(1)}, bf16[1,16,96,96]{3,2,1,0:T(8,128)(2,1)}, u32[]{:S(2)}) copy-start(bf16[1,16,96,96]{3,2,1,0:T(8,128)(2,1)} %param.8) | copy-start | bytes 884740
  3.0 23.7 %all-to-all-start = ((f32[32,24,128]{2,1,0:T(8,128)}), f32[32,24,128]{2,1,0:T(8,128)S(1)}, u32[]{:S(2)}, u32[]{:S(2)}) async-start(f32[32,24,128]{2,1,0:T(8,128)} %get-tuple-element.13), calls=%async_computation | async-start | bytes 786432 | tf_op jit(solution)/shard_map/all_to_all | solution.py:276
  10.4 7.5 %copy-start = (bf16[32,128,128]{2,1,0:T(8,128)(2,1)S(1)}, bf16[32,128,128]{2,1,0:T(8,128)(2,1)}, u32[]{:S(2)}) copy-start(bf16[32,128,128]{2,1,0:T(8,128)(2,1)} %get-tuple-element.12.blocks_ref) | copy-start | bytes 3145732
  10.4 7.5 %copy-start.1 = (s32[8,4]{0,1:T(4,128)S(1)}, s32[8,4]{0,1:T(4,128)}, u32[]{:S(2)}) copy-start(s32[8,4]{0,1:T(4,128)} %param.6) | copy-start | bytes 388
  11.4 19.8 %collective-permute-start.6 = (bf16[6,96,128]{2,1,0:T(8,128)(2,1)}, bf16[6,96,128]{2,1,0:T(8,128)(2,1)S(1)}, u32[]{:S(2)}, u32[]{:S(2)}) collective-permute-start(bf16[6,96,128]{2,1,0:T(8,128)(2,1)} %bitcast.7), channel_id=1, source_target_pairs={{0,4},{1,5},{2,6},{3,7},{4,0},{5,1},{6,2},{7,3},{8,12},{9,13},{10,... | collective-permute-start | bytes 442376 | tf_op jit(solution)/shard_map/ppermute | solution.py:269
  13.7 16.6 %collective-permute-start = (bf16[6,96,128]{2,1,0:T(8,128)(2,1)}, bf16[6,96,128]{2,1,0:T(8,128)(2,1)}, u32[]{:S(2)}, u32[]{:S(2)}) collective-permute-start(bf16[6,96,128]{2,1,0:T(8,128)(2,1)} %bitcast.7), channel_id=1, source_target_pairs={{0,1},{1,0},{2,3},{3,2},{4,5},{5,4},{6,7},{7,6},{8,9},{9,8},{10,11... | collective-permute-start | bytes 442376 | tf_op jit(solution)/shard_map/ppermute | solution.py:269
  14.9 15.8 %collective-permute-start.2 = (bf16[6,96,128]{2,1,0:T(8,128)(2,1)}, bf16[6,96,128]{2,1,0:T(8,128)(2,1)}, u32[]{:S(2)}, u32[]{:S(2)}) collective-permute-start(bf16[6,96,128]{2,1,0:T(8,128)(2,1)} %bitcast.7), channel_id=1, source_target_pairs={{0,2},{1,3},{2,0},{3,1},{4,6},{5,7},{6,4},{7,5},{8,10},{9,11},{10,... | collective-permute-start | bytes 442376 | tf_op jit(solution)/shard_map/ppermute | solution.py:269
  16.1 14.7 %collective-permute-start.4 = (bf16[6,96,128]{2,1,0:T(8,128)(2,1)}, bf16[6,96,128]{2,1,0:T(8,128)(2,1)}, u32[]{:S(2)}, u32[]{:S(2)}) collective-permute-start(bf16[6,96,128]{2,1,0:T(8,128)(2,1)} %bitcast.7), channel_id=1, source_target_pairs={{0,3},{1,2},{2,1},{3,0},{4,7},{5,6},{6,5},{7,4},{8,11},{9,10},{10,... | collective-permute-start | bytes 442376 | tf_op jit(solution)/shard_map/ppermute | solution.py:269
  16.3 17.0 %collective-permute-start.8 = (bf16[6,96,128]{2,1,0:T(8,128)(2,1)}, bf16[6,96,128]{2,1,0:T(8,128)(2,1)}, u32[]{:S(2)}, u32[]{:S(2)}) collective-permute-start(bf16[6,96,128]{2,1,0:T(8,128)(2,1)} %bitcast.7), channel_id=1, source_target_pairs={{0,6},{1,7},{2,4},{3,5},{4,2},{5,3},{6,0},{7,1},{8,14},{9,15},{10,... | collective-permute-start | bytes 442376 | tf_op jit(solution)/shard_map/ppermute | solution.py:269
  17.7 9.0 %copy-start.2 = (bf16[1,96,96]{2,1,0:T(8,128)(2,1)S(1)}, bf16[1,96,96]{2,1,0:T(8,128)(2,1)}, u32[]{:S(2)}) copy-start(bf16[1,96,96]{2,1,0:T(8,128)(2,1)} %integral_ref.1) | copy-start | bytes 55300
  27.6 23.1 %all-to-all-start.1 = ((bf16[32,24,128]{2,1,0:T(8,128)(2,1)}), bf16[32,24,128]{2,1,0:T(8,128)(2,1)S(1)}, u32[]{:S(2)}, u32[]{:S(2)}) async-start(bf16[32,24,128]{2,1,0:T(8,128)(2,1)} %shard_map.58), calls=%async_computation.1 | async-start | bytes 393216 | tf_op jit(solution)/shard_map/all_to_all | solution.py:296
  30.2 4.3 %collective-permute-start.1 = (bf16[6,96,128]{2,1,0:T(8,128)(2,1)}, bf16[6,96,128]{2,1,0:T(8,128)(2,1)S(1)}, u32[]{:S(2)}, u32[]{:S(2)}) collective-permute-start(bf16[6,96,128]{2,1,0:T(8,128)(2,1)} %collective-permute-done.rest_1_), channel_id=1, source_target_pairs={{0,8},{8,0},{16,24},{24,16},{1,9},{9,1},{17,25},{25,17},{2,10},{10... | collective-permute-start | bytes 442376 | tf_op jit(solution)/shard_map/ppermute | solution.py:272
  30.7 5.1 %collective-permute-start.3 = (bf16[6,96,128]{2,1,0:T(8,128)(2,1)}, bf16[6,96,128]{2,1,0:T(8,128)(2,1)S(1)}, u32[]{:S(2)}, u32[]{:S(2)}) collective-permute-start(bf16[6,96,128]{2,1,0:T(8,128)(2,1)} %collective-permute-done.2.rest_3_), channel_id=1, source_target_pairs={{0,8},{8,0},{16,24},{24,16},{1,9},{9,1},{17,25},{25,17},{2,10},{10... | collective-permute-start | bytes 442376 | tf_op jit(solution)/shard_map/ppermute | solution.py:272
  30.8 5.1 %collective-permute-start.5 = (bf16[6,96,128]{2,1,0:T(8,128)(2,1)}, bf16[6,96,128]{2,1,0:T(8,128)(2,1)S(1)}, u32[]{:S(2)}, u32[]{:S(2)}) collective-permute-start(bf16[6,96,128]{2,1,0:T(8,128)(2,1)} %collective-permute-done.4.rest_5_), channel_id=1, source_target_pairs={{0,8},{8,0},{16,24},{24,16},{1,9},{9,1},{17,25},{25,17},{2,10},{10... | collective-permute-start | bytes 442376 | tf_op jit(solution)/shard_map/ppermute | solution.py:272
  31.2 8.4 %collective-permute-start.10 = (bf16[6,96,128]{2,1,0:T(8,128)(2,1)S(1)}, bf16[6,96,128]{2,1,0:T(8,128)(2,1)S(1)}, u32[]{:S(2)}, u32[]{:S(2)}) collective-permute-start(bf16[6,96,128]{2,1,0:T(8,128)(2,1)S(1)} %collective-permute-done.6.rest_1_), channel_id=1, source_target_pairs={{0,1},{1,0},{2,3},{3,2},{4,5},{5,4},{6,7},{7,6},{8,9},{9,8},{10,11... | collective-permute-start | bytes 442376 | tf_op jit(solution)/shard_map/ppermute | solution.py:269
  33.3 8.1 %collective-permute-start.12 = (bf16[6,96,128]{2,1,0:T(8,128)(2,1)}, bf16[6,96,128]{2,1,0:T(8,128)(2,1)S(1)}, u32[]{:S(2)}, u32[]{:S(2)}) collective-permute-start(bf16[6,96,128]{2,1,0:T(8,128)(2,1)} %collective-permute-done.8.rest_3_), channel_id=1, source_target_pairs={{0,1},{1,0},{2,3},{3,2},{4,5},{5,4},{6,7},{7,6},{8,9},{9,8},{10,11... | collective-permute-start | bytes 442376 | tf_op jit(solution)/shard_map/ppermute | solution.py:269
  34.5 7.7 %collective-permute-start.7 = (bf16[6,96,128]{2,1,0:T(8,128)(2,1)S(1)}, bf16[6,96,128]{2,1,0:T(8,128)(2,1)S(1)}, u32[]{:S(2)}, u32[]{:S(2)}) collective-permute-start(bf16[6,96,128]{2,1,0:T(8,128)(2,1)S(1)} %collective-permute-done.6.rest_1_), channel_id=1, source_target_pairs={{0,8},{8,0},{16,24},{24,16},{1,9},{9,1},{17,25},{25,17},{2,10},{10... | collective-permute-start | bytes 442376 | tf_op jit(solution)/shard_map/ppermute | solution.py:272
  35.8 6.4 %collective-permute-start.9 = (bf16[6,96,128]{2,1,0:T(8,128)(2,1)}, bf16[6,96,128]{2,1,0:T(8,128)(2,1)S(1)}, u32[]{:S(2)}, u32[]{:S(2)}) collective-permute-start(bf16[6,96,128]{2,1,0:T(8,128)(2,1)} %collective-permute-done.8.rest_3_), channel_id=1, source_target_pairs={{0,8},{8,0},{16,24},{24,16},{1,9},{9,1},{17,25},{25,17},{2,10},{10... | collective-permute-start | bytes 442376 | tf_op jit(solution)/shard_map/ppermute | solution.py:272
  41.4 5.2 %collective-permute-start.11 = (bf16[6,96,128]{2,1,0:T(8,128)(2,1)S(1)}, bf16[6,96,128]{2,1,0:T(8,128)(2,1)S(1)}, u32[]{:S(2)}, u32[]{:S(2)}) collective-permute-start(bf16[6,96,128]{2,1,0:T(8,128)(2,1)S(1)} %collective-permute-done.10.rest_1_), channel_id=1, source_target_pairs={{0,8},{8,0},{16,24},{24,16},{1,9},{9,1},{17,25},{25,17},{2,10},{10... | collective-permute-start | bytes 442376 | tf_op jit(solution)/shard_map/ppermute | solution.py:272
  42.3 4.4 %collective-permute-start.13 = (bf16[6,96,128]{2,1,0:T(8,128)(2,1)S(1)}, bf16[6,96,128]{2,1,0:T(8,128)(2,1)S(1)}, u32[]{:S(2)}, u32[]{:S(2)}) collective-permute-start(bf16[6,96,128]{2,1,0:T(8,128)(2,1)S(1)} %collective-permute-done.12.rest_3_), channel_id=1, source_target_pairs={{0,8},{8,0},{16,24},{24,16},{1,9},{9,1},{17,25},{25,17},{2,10},{10... | collective-permute-start | bytes 442376 | tf_op jit(solution)/shard_map/ppermute | solution.py:272

commit v6 on v5

--- a/solution.py
+++ b/solution.py
@@ -122,22 +122,19 @@
             pltpu.VMEM((len(near), width, factor_count * LANES), jnp.bfloat16),
             pltpu.VMEM((2, 2 * width, factor_count * LANES), jnp.bfloat16),
         ],
-        compiler_params=pltpu.CompilerParams(vmem_limit_bytes=(10 << 20) + (len(near) << 21)),
+        compiler_params=pltpu.CompilerParams(vmem_limit_bytes=24 << 20),
         cost_estimate=pl.CostEstimate(flops=cost, bytes_accessed=rows, transcendentals=0),
     )(kept, me, blocks, *carried, *parts)
 
 
-def close_kernel(tiles, width, kept_ref, blocks_ref, total_ref, spread_ref, out_ref, landed, hidden, square, lines, sem):
+def close_kernel(tiles, width, kept_ref, blocks_ref, total_ref, spread_ref, out_ref, hidden, square, lines):
     groups = spread_ref.shape[0] // tiles
     pairs, slots, flat = out_ref.shape
     count = flat // LANES
     parts = width * 4 // LANES
-    copy = pltpu.make_async_copy(spread_ref, landed, sem)
-    copy.start()
     hidden[:, width:, :] = jnp.zeros((tiles, LANES - width, LANES), jnp.bfloat16)
-    copy.wait()
     for tile in range(tiles):
-        pieces = [landed[g * tiles + tile].astype(jnp.float32) for g in range(groups)]
+        pieces = [spread_ref[g * tiles + tile].astype(jnp.float32) for g in range(groups)]
         hidden[tile, :width, :] = jnp.concatenate(pieces, axis=0).astype(jnp.bfloat16)
     spare = LANES - width
     lane = lax.broadcasted_iota(jnp.int32, (width // 4, LANES), 1)
@@ -166,14 +163,12 @@
     return pl.pallas_call(
         functools.partial(close_kernel, tiles, width),
         out_shape=jax.ShapeDtypeStruct(shape, jnp.bfloat16),
-        in_specs=[SMEM] + [VMEM] * 2 + [FREE],
+        in_specs=[SMEM] + [VMEM] * 3,
         out_specs=VMEM,
         scratch_shapes=[
-            pltpu.VMEM(spread.shape, jnp.bfloat16),
             pltpu.VMEM((tiles, LANES, LANES), jnp.bfloat16),
             pltpu.VMEM((rows, width, LANES), jnp.float32),
             pltpu.VMEM((shape[0], shape[1] * shape[2] // LANES, LANES), jnp.float32),
-            pltpu.SemaphoreType.DMA,
         ],
         compiler_params=pltpu.CompilerParams(vmem_limit_bytes=16 << 20),
         cost_estimate=pl.CostEstimate(flops=rows, bytes_accessed=rows, transcendentals=0),

time: 54 us -> 53.5 us (level)
  the two profiles are of different devices: /device:TPU:1 before, /device:TPU:0 now
where the time goes in v6:
time: 53.5 us; the launch traced here: 53.4 us
  starting transfers between devices  22.4 us (42%)
  Pallas kernels  21.1 us (39%)
  waiting for transfers between devices  8.17 us (15%)
  local copies, waits for them, and re-layouts  1.44 us (3%)
    pallas_call x4, Pallas kernels, ladder(): pl.pallas_call(functools.partial(ladder_kernel, near, tiles, width, len(c...  15 us
    ppermute x7, starting transfers between devices, to_tile(): return lax.ppermute(array, 'tile', [(i, i ^ flip) for i in range(tiles)])  10.8 us
    all_to_all x1, starting transfers between devices, on_device(): lax.all_to_all(shares, ALL, split_axis=0, concat_axis=0, tiled=True)  7.3 us
    all_to_all x1, waiting for transfers between devices, on_device(): lax.all_to_all(shares, ALL, split_axis=0, concat_axis=0, tiled=True)  4.58 us
    ppermute x7, waiting for transfers between devices, to_tile(): return lax.ppermute(array, 'tile', [(i, i ^ flip) for i in range(tiles)])  3.58 us
    pallas_call x1, Pallas kernels, prepare(): pl.pallas_call(functools.partial(prepare_kernel, tiles, width), out_shape...  3.03 us
    all_to_all x1, starting transfers between devices, on_device(): lax.all_to_all(hidden, ALL, split_axis=0, concat_axis=0, tiled=True)  2.58 us
    pallas_call x1, Pallas kernels, close(): pl.pallas_call(functools.partial(close_kernel, tiles, width), out_shape=j...  2.22 us
  transfers between devices with their start and end apart: 16, of which 3 were waited for; matrix products, arithmetic and copies ran while one was open for 3% of the time, Pallas kernels for 30%

profile of v6, /device:TPU:0, one launch (start us, length us, event | category | flops | bytes accessed | tf_op | source)
XLA Modules:
  0.0 53.4 jit_solution(10116629276006497721)
XLA Ops:
  0.0 3.0 %shard_map.55 = (bf16[32,128,128]{2,1,0:T(8,128)(2,1)}, f32[32,24,128]{2,1,0:T(8,128)}) custom-call(s32[4,8]{1,0:T(4,128)} %bitcast.10, bf16[1,8]{1,0:T(2,128)(2,1)} %bitcast.19, bf16[8,4,9216]{2,1,0:T(4,128)(2,1)} %flat_ref.1), custom_call_target="tpu_custom_call" | custom-call | flops 32 | bytes 32 | tf_op jit(solution)/shard_map/pallas_call | solution.py:214
  3.0 7.3 %all-to-all-start = ((f32[32,24,128]{2,1,0:T(8,128)}), f32[32,24,128]{2,1,0:T(8,128)S(1)}, u32[]{:S(2)}, u32[]{:S(2)}) async-start(f32[32,24,128]{2,1,0:T(8,128)} %get-tuple-element.13), calls=%async_computation | async-start | bytes 786432 | tf_op jit(solution)/shard_map/all_to_all | solution.py:271
  10.4 0.0 copy-done.3
  10.4 0.2 copy.9
  10.6 0.0 copy-start
  10.6 0.0 copy-start.1
  10.7 0.1 maximum_maximum_fusion
  10.8 0.8 %copy.13 = bf16[1,6,96,128]{3,2,1,0:T(8,128)(2,1)} copy(bf16[1,6,96,128]{2,3,1,0:T(8,128)(2,1)S(1)} %constant_dynamic-slice_fusion) | data formatting | bytes 294912
  11.6 2.7 %collective-permute-start.6 = (bf16[6,96,128]{2,1,0:T(8,128)(2,1)}, bf16[6,96,128]{2,1,0:T(8,128)(2,1)S(1)}, u32[]{:S(2)}, u32[]{:S(2)}) collective-permute-start(bf16[6,96,128]{2,1,0:T(8,128)(2,1)} %bitcast.7), channel_id=1, source_target_pairs={{0,4},{1,5},{2,6},{3,7},{4,0},{5,1},{6,2},{7,3},{8,12},{9,13},{10,... | collective-permute-start | bytes 442376 | tf_op jit(solution)/shard_map/ppermute | solution.py:264
  14.3 1.5 %collective-permute-start = (bf16[6,96,128]{2,1,0:T(8,128)(2,1)}, bf16[6,96,128]{2,1,0:T(8,128)(2,1)}, u32[]{:S(2)}, u32[]{:S(2)}) collective-permute-start(bf16[6,96,128]{2,1,0:T(8,128)(2,1)} %bitcast.7), channel_id=1, source_target_pairs={{0,1},{1,0},{2,3},{3,2},{4,5},{5,4},{6,7},{7,6},{8,9},{9,8},{10,11... | collective-permute-start | bytes 442376 | tf_op jit(solution)/shard_map/ppermute | solution.py:264
  15.7 1.5 %collective-permute-start.2 = (bf16[6,96,128]{2,1,0:T(8,128)(2,1)}, bf16[6,96,128]{2,1,0:T(8,128)(2,1)}, u32[]{:S(2)}, u32[]{:S(2)}) collective-permute-start(bf16[6,96,128]{2,1,0:T(8,128)(2,1)} %bitcast.7), channel_id=1, source_target_pairs={{0,2},{1,3},{2,0},{3,1},{4,6},{5,7},{6,4},{7,5},{8,10},{9,11},{10,... | collective-permute-start | bytes 442376 | tf_op jit(solution)/shard_map/ppermute | solution.py:264
  17.3 0.5 collective-permute-start.4
  17.8 1.5 %collective-permute-start.8 = (bf16[6,96,128]{2,1,0:T(8,128)(2,1)}, bf16[6,96,128]{2,1,0:T(8,128)(2,1)}, u32[]{:S(2)}, u32[]{:S(2)}) collective-permute-start(bf16[6,96,128]{2,1,0:T(8,128)(2,1)} %bitcast.7), channel_id=1, source_target_pairs={{0,6},{1,7},{2,4},{3,5},{4,2},{5,3},{6,0},{7,1},{8,14},{9,15},{10,... | collective-permute-start | bytes 442376 | tf_op jit(solution)/shard_map/ppermute | solution.py:264
  19.2 0.2 copy.10
  19.4 0.0 copy-start.2
  19.4 0.2 copy.11
  19.6 2.9 %shard_map.56.rest_0_ = f32[32,96,96]{2,1,0:T(8,128)S(1)} custom-call(s32[4,8]{1,0:T(4,128)S(1)} %bitcast.11, s32[1]{0:T(128)} %bitcast.2.me_ref, bf16[32,128,128]{2,1,0:T(8,128)(2,1)S(1)} %copy-done, bf16[6,96,128]{2,1,0:T(8,128)(2,1)S(1)} %bitcast.8, bf16[6,96,128]{2,1,0:T(8,128)(2,1)S(1)} %bitcast.9), custom_call_target="tpu_custom_call" | custom-call | flops 32 | bytes 32 | tf_op jit(solution)/shard_map/pallas_call | solution.py:111
  22.5 4.6 %all-to-all-done.arrived_ref = f32[32,24,128]{2,1,0:T(8,128)S(1)} async-done(((f32[32,24,128]{2,1,0:T(8,128)}), f32[32,24,128]{2,1,0:T(8,128)S(1)}, u32[]{:S(2)}, u32[]{:S(2)}) %all-to-all-start) | async-done | bytes 393248 | tf_op jit(solution)/shard_map/all_to_all | solution.py:271
  27.1 0.9 %shard_map.58 = bf16[32,24,128]{2,1,0:T(8,128)(2,1)} custom-call(f32[32,24,128]{2,1,0:T(8,128)S(1)} %all-to-all-done.arrived_ref, bf16[1,96,96]{2,1,0:T(8,128)(2,1)S(1)} %copy-done.2), custom_call_target="tpu_custom_call" | custom-call | flops 1000 | bytes 1000 | tf_op jit(solution)/shard_map/pallas_call | solution.py:244
  28.0 2.6 %all-to-all-start.1 = ((bf16[32,24,128]{2,1,0:T(8,128)(2,1)}), bf16[32,24,128]{2,1,0:T(8,128)(2,1)S(1)}, u32[]{:S(2)}, u32[]{:S(2)}) async-start(bf16[32,24,128]{2,1,0:T(8,128)(2,1)} %shard_map.58), calls=%async_computation.1 | async-start | bytes 393216 | tf_op jit(solution)/shard_map/all_to_all | solution.py:291
  30.6 0.0 collective-permute-done.rest_1_
  30.6 0.2 collective-permute-start.1
  30.8 0.0 collective-permute-done.2.rest_3_
  30.8 0.4 collective-permute-start.3
  31.2 0.0 collective-permute-done.4.rest_5_
  31.2 0.1 collective-permute-start.5
  31.3 0.0 collective-permute-done.6.rest_1_
  31.3 1.7 %collective-permute-start.10 = (bf16[6,96,128]{2,1,0:T(8,128)(2,1)S(1)}, bf16[6,96,128]{2,1,0:T(8,128)(2,1)S(1)}, u32[]{:S(2)}, u32[]{:S(2)}) collective-permute-start(bf16[6,96,128]{2,1,0:T(8,128)(2,1)S(1)} %collective-permute-done.6.rest_1_), channel_id=1, source_target_pairs={{0,1},{1,0},{2,3},{3,2},{4,5},{5,4},{6,7},{7,6},{8,9},{9,8},{10,11... | collective-permute-start | bytes 442376 | tf_op jit(solution)/shard_map/ppermute | solution.py:264
  33.0 1.3 %collective-permute-done.8.rest_3_ = bf16[6,96,128]{2,1,0:T(8,128)(2,1)} collective-permute-done((bf16[6,96,128]{2,1,0:T(8,128)(2,1)}, bf16[6,96,128]{2,1,0:T(8,128)(2,1)}, u32[]{:S(2)}, u32[]{:S(2)}) %collective-permute-start.8) | collective-permute-done | bytes 147488 | tf_op jit(solution)/shard_map/ppermute | solution.py:264
  34.3 1.5 %collective-permute-start.12 = (bf16[6,96,128]{2,1,0:T(8,128)(2,1)}, bf16[6,96,128]{2,1,0:T(8,128)(2,1)S(1)}, u32[]{:S(2)}, u32[]{:S(2)}) collective-permute-start(bf16[6,96,128]{2,1,0:T(8,128)(2,1)} %collective-permute-done.8.rest_3_), channel_id=1, source_target_pairs={{0,1},{1,0},{2,3},{3,2},{4,5},{5,4},{6,7},{7,6},{8,9},{9,8},{10,11... | collective-permute-start | bytes 442376 | tf_op jit(solution)/shard_map/ppermute | solution.py:264
  35.8 0.0 collective-permute-done.1.rest_2_
  35.8 0.0 collective-permute-start.7
  35.8 0.0 collective-permute-done.3.rest_4_
  35.8 0.5 collective-permute-start.9
  36.3 0.0 collective-permute-done.5.rest_6_
  36.3 3.7 %shard_map.57.rest_0_ = f32[32,96,96]{2,1,0:T(8,128)S(1)} custom-call(s32[4,8]{1,0:T(4,128)S(1)} %bitcast.12, s32[1]{0:T(128)} %bitcast.2.me_ref, bf16[32,128,128]{2,1,0:T(8,128)(2,1)S(1)} %copy-done, f32[32,96,96]{2,1,0:T(8,128)S(1)} %shard_map.56.rest_0_, bf16[6,96,128]{2,1,0:T(8,128)(2,1)} %collective-permute-done.rest_1_, ...), custom_call_target="tpu_custom_call", output_to_operand_aliasing={{}: (3, {})} | custom-call | flops 32 | bytes 32 | tf_op jit(solution)/shard_map/pallas_call | solution.py:111
  40.0 0.0 collective-permute-done.10.rest_1_
  40.0 2.2 %collective-permute-done.12.rest_3_ = bf16[6,96,128]{2,1,0:T(8,128)(2,1)S(1)} collective-permute-done((bf16[6,96,128]{2,1,0:T(8,128)(2,1)}, bf16[6,96,128]{2,1,0:T(8,128)(2,1)S(1)}, u32[]{:S(2)}, u32[]{:S(2)}) %collective-permute-start.12) | collective-permute-done | bytes 147488 | tf_op jit(solution)/shard_map/ppermute | solution.py:264
  42.2 0.0 collective-permute-start.11
  42.2 0.5 collective-permute-start.13
  42.7 0.0 collective-permute-done.7.rest_2_
  42.7 0.0 collective-permute-done.9.rest_4_
  42.7 4.4 %shard_map.59.rest_0_ = f32[32,96,96]{2,1,0:T(8,128)S(1)} custom-call(s32[4,8]{1,0:T(4,128)S(1)} %bitcast.13, s32[1]{0:T(128)} %bitcast.2.me_ref, bf16[32,128,128]{2,1,0:T(8,128)(2,1)S(1)} %copy-done, f32[32,96,96]{2,1,0:T(8,128)S(1)} %shard_map.57.rest_0_, bf16[6,96,128]{2,1,0:T(8,128)(2,1)S(1)} %collective-permute-done.6.rest_1_, ...), custom_call_target="tpu_custom_call", output_to_operand_aliasing={{}: (3, {})} | custom-call | flops 32 | bytes 32 | tf_op jit(solution)/shard_map/pallas_call | solution.py:111
  47.1 0.0 collective-permute-done.11.rest_2_
  47.1 0.0 collective-permute-done.13.rest_4_
  47.1 4.0 %shard_map.60.total_ref = f32[32,96,96]{2,1,0:T(8,128)S(1)} custom-call(s32[4,8]{1,0:T(4,128)S(1)} %bitcast.14, s32[1]{0:T(128)} %bitcast.2.me_ref, bf16[32,128,128]{2,1,0:T(8,128)(2,1)S(1)} %copy-done, f32[32,96,96]{2,1,0:T(8,128)S(1)} %shard_map.59.rest_0_, ...), custom_call_target="tpu_custom_call", output_to_operand_aliasing={{}: (3, {})} | custom-call | flops 32 | bytes 32 | tf_op jit(solution)/shard_map/pallas_call | solution.py:111
  51.2 0.0 all-to-all-done.1.spread_ref
  51.2 2.2 %shard_map.61 = bf16[8,4,9216]{2,1,0:T(4,128)(2,1)} custom-call(s32[4,8]{1,0:T(4,128)S(1)} %bitcast.15, bf16[32,128,128]{2,1,0:T(8,128)(2,1)S(1)} %copy-done, f32[32,96,96]{2,1,0:T(8,128)S(1)} %shard_map.60.total_ref, bf16[32,24,128]{2,1,0:T(8,128)(2,1)S(1)} %all-to-all-done.1.spread_ref), custom_call_target="tpu_custom_call" | custom-call | flops 32 | bytes 32 | tf_op jit(solution)/shard_map/pallas_call | solution.py:163
  (8 shorter events, 0.1 us)
Async XLA Ops:
  0.0 10.4 %copy-start.3 = (bf16[1,16,96,96]{3,2,1,0:T(8,128)(2,1)S(1)}, bf16[1,16,96,96]{3,2,1,0:T(8,128)(2,1)}, u32[]{:S(2)}) copy-start(bf16[1,16,96,96]{3,2,1,0:T(8,128)(2,1)} %param.8) | copy-start | bytes 884740
  3.0 24.1 %all-to-all-start = ((f32[32,24,128]{2,1,0:T(8,128)}), f32[32,24,128]{2,1,0:T(8,128)S(1)}, u32[]{:S(2)}, u32[]{:S(2)}) async-start(f32[32,24,128]{2,1,0:T(8,128)} %get-tuple-element.13), calls=%async_computation | async-start | bytes 786432 | tf_op jit(solution)/shard_map/all_to_all | solution.py:271
  10.6 9.0 %copy-start = (bf16[32,128,128]{2,1,0:T(8,128)(2,1)S(1)}, bf16[32,128,128]{2,1,0:T(8,128)(2,1)}, u32[]{:S(2)}) copy-start(bf16[32,128,128]{2,1,0:T(8,128)(2,1)} %get-tuple-element.12.blocks_ref) | copy-start | bytes 3145732
  10.6 9.0 %copy-start.1 = (s32[8,4]{0,1:T(4,128)S(1)}, s32[8,4]{0,1:T(4,128)}, u32[]{:S(2)}) copy-start(s32[8,4]{0,1:T(4,128)} %param.6) | copy-start | bytes 388
  11.6 19.7 %collective-permute-start.6 = (bf16[6,96,128]{2,1,0:T(8,128)(2,1)}, bf16[6,96,128]{2,1,0:T(8,128)(2,1)S(1)}, u32[]{:S(2)}, u32[]{:S(2)}) collective-permute-start(bf16[6,96,128]{2,1,0:T(8,128)(2,1)} %bitcast.7), channel_id=1, source_target_pairs={{0,4},{1,5},{2,6},{3,7},{4,0},{5,1},{6,2},{7,3},{8,12},{9,13},{10,... | collective-permute-start | bytes 442376 | tf_op jit(solution)/shard_map/ppermute | solution.py:264
  14.3 16.3 %collective-permute-start = (bf16[6,96,128]{2,1,0:T(8,128)(2,1)}, bf16[6,96,128]{2,1,0:T(8,128)(2,1)}, u32[]{:S(2)}, u32[]{:S(2)}) collective-permute-start(bf16[6,96,128]{2,1,0:T(8,128)(2,1)} %bitcast.7), channel_id=1, source_target_pairs={{0,1},{1,0},{2,3},{3,2},{4,5},{5,4},{6,7},{7,6},{8,9},{9,8},{10,11... | collective-permute-start | bytes 442376 | tf_op jit(solution)/shard_map/ppermute | solution.py:264
  15.7 15.0 %collective-permute-start.2 = (bf16[6,96,128]{2,1,0:T(8,128)(2,1)}, bf16[6,96,128]{2,1,0:T(8,128)(2,1)}, u32[]{:S(2)}, u32[]{:S(2)}) collective-permute-start(bf16[6,96,128]{2,1,0:T(8,128)(2,1)} %bitcast.7), channel_id=1, source_target_pairs={{0,2},{1,3},{2,0},{3,1},{4,6},{5,7},{6,4},{7,5},{8,10},{9,11},{10,... | collective-permute-start | bytes 442376 | tf_op jit(solution)/shard_map/ppermute | solution.py:264
  17.3 13.9 %collective-permute-start.4 = (bf16[6,96,128]{2,1,0:T(8,128)(2,1)}, bf16[6,96,128]{2,1,0:T(8,128)(2,1)}, u32[]{:S(2)}, u32[]{:S(2)}) collective-permute-start(bf16[6,96,128]{2,1,0:T(8,128)(2,1)} %bitcast.7), channel_id=1, source_target_pairs={{0,3},{1,2},{2,1},{3,0},{4,7},{5,6},{6,5},{7,4},{8,11},{9,10},{10,... | collective-permute-start | bytes 442376 | tf_op jit(solution)/shard_map/ppermute | solution.py:264
  17.8 16.5 %collective-permute-start.8 = (bf16[6,96,128]{2,1,0:T(8,128)(2,1)}, bf16[6,96,128]{2,1,0:T(8,128)(2,1)}, u32[]{:S(2)}, u32[]{:S(2)}) collective-permute-start(bf16[6,96,128]{2,1,0:T(8,128)(2,1)} %bitcast.7), channel_id=1, source_target_pairs={{0,6},{1,7},{2,4},{3,5},{4,2},{5,3},{6,0},{7,1},{8,14},{9,15},{10,... | collective-permute-start | bytes 442376 | tf_op jit(solution)/shard_map/ppermute | solution.py:264
  19.4 7.7 %copy-start.2 = (bf16[1,96,96]{2,1,0:T(8,128)(2,1)S(1)}, bf16[1,96,96]{2,1,0:T(8,128)(2,1)}, u32[]{:S(2)}) copy-start(bf16[1,96,96]{2,1,0:T(8,128)(2,1)} %integral_ref.1) | copy-start | bytes 55300
  28.0 23.2 %all-to-all-start.1 = ((bf16[32,24,128]{2,1,0:T(8,128)(2,1)}), bf16[32,24,128]{2,1,0:T(8,128)(2,1)S(1)}, u32[]{:S(2)}, u32[]{:S(2)}) async-start(bf16[32,24,128]{2,1,0:T(8,128)(2,1)} %shard_map.58), calls=%async_computation.1 | async-start | bytes 393216 | tf_op jit(solution)/shard_map/all_to_all | solution.py:291
  30.6 5.2 %collective-permute-start.1 = (bf16[6,96,128]{2,1,0:T(8,128)(2,1)}, bf16[6,96,128]{2,1,0:T(8,128)(2,1)S(1)}, u32[]{:S(2)}, u32[]{:S(2)}) collective-permute-start(bf16[6,96,128]{2,1,0:T(8,128)(2,1)} %collective-permute-done.rest_1_), channel_id=1, source_target_pairs={{0,8},{8,0},{16,24},{24,16},{1,9},{9,1},{17,25},{25,17},{2,10},{10... | collective-permute-start | bytes 442376 | tf_op jit(solution)/shard_map/ppermute | solution.py:267
  30.8 5.0 %collective-permute-start.3 = (bf16[6,96,128]{2,1,0:T(8,128)(2,1)}, bf16[6,96,128]{2,1,0:T(8,128)(2,1)S(1)}, u32[]{:S(2)}, u32[]{:S(2)}) collective-permute-start(bf16[6,96,128]{2,1,0:T(8,128)(2,1)} %collective-permute-done.2.rest_3_), channel_id=1, source_target_pairs={{0,8},{8,0},{16,24},{24,16},{1,9},{9,1},{17,25},{25,17},{2,10},{10... | collective-permute-start | bytes 442376 | tf_op jit(solution)/shard_map/ppermute | solution.py:267
  31.2 5.1 %collective-permute-start.5 = (bf16[6,96,128]{2,1,0:T(8,128)(2,1)}, bf16[6,96,128]{2,1,0:T(8,128)(2,1)S(1)}, u32[]{:S(2)}, u32[]{:S(2)}) collective-permute-start(bf16[6,96,128]{2,1,0:T(8,128)(2,1)} %collective-permute-done.4.rest_5_), channel_id=1, source_target_pairs={{0,8},{8,0},{16,24},{24,16},{1,9},{9,1},{17,25},{25,17},{2,10},{10... | collective-permute-start | bytes 442376 | tf_op jit(solution)/shard_map/ppermute | solution.py:267
  31.3 8.7 %collective-permute-start.10 = (bf16[6,96,128]{2,1,0:T(8,128)(2,1)S(1)}, bf16[6,96,128]{2,1,0:T(8,128)(2,1)S(1)}, u32[]{:S(2)}, u32[]{:S(2)}) collective-permute-start(bf16[6,96,128]{2,1,0:T(8,128)(2,1)S(1)} %collective-permute-done.6.rest_1_), channel_id=1, source_target_pairs={{0,1},{1,0},{2,3},{3,2},{4,5},{5,4},{6,7},{7,6},{8,9},{9,8},{10,11... | collective-permute-start | bytes 442376 | tf_op jit(solution)/shard_map/ppermute | solution.py:264
  34.3 7.9 %collective-permute-start.12 = (bf16[6,96,128]{2,1,0:T(8,128)(2,1)}, bf16[6,96,128]{2,1,0:T(8,128)(2,1)S(1)}, u32[]{:S(2)}, u32[]{:S(2)}) collective-permute-start(bf16[6,96,128]{2,1,0:T(8,128)(2,1)} %collective-permute-done.8.rest_3_), channel_id=1, source_target_pairs={{0,1},{1,0},{2,3},{3,2},{4,5},{5,4},{6,7},{7,6},{8,9},{9,8},{10,11... | collective-permute-start | bytes 442376 | tf_op jit(solution)/shard_map/ppermute | solution.py:264
  35.8 6.9 %collective-permute-start.7 = (bf16[6,96,128]{2,1,0:T(8,128)(2,1)S(1)}, bf16[6,96,128]{2,1,0:T(8,128)(2,1)S(1)}, u32[]{:S(2)}, u32[]{:S(2)}) collective-permute-start(bf16[6,96,128]{2,1,0:T(8,128)(2,1)S(1)} %collective-permute-done.6.rest_1_), channel_id=1, source_target_pairs={{0,8},{8,0},{16,24},{24,16},{1,9},{9,1},{17,25},{25,17},{2,10},{10... | collective-permute-start | bytes 442376 | tf_op jit(solution)/shard_map/ppermute | solution.py:267
  35.8 6.9 %collective-permute-start.9 = (bf16[6,96,128]{2,1,0:T(8,128)(2,1)}, bf16[6,96,128]{2,1,0:T(8,128)(2,1)S(1)}, u32[]{:S(2)}, u32[]{:S(2)}) collective-permute-start(bf16[6,96,128]{2,1,0:T(8,128)(2,1)} %collective-permute-done.8.rest_3_), channel_id=1, source_target_pairs={{0,8},{8,0},{16,24},{24,16},{1,9},{9,1},{17,25},{25,17},{2,10},{10... | collective-permute-start | bytes 442376 | tf_op jit(solution)/shard_map/ppermute | solution.py:267
  42.2 4.9 %collective-permute-start.11 = (bf16[6,96,128]{2,1,0:T(8,128)(2,1)S(1)}, bf16[6,96,128]{2,1,0:T(8,128)(2,1)S(1)}, u32[]{:S(2)}, u32[]{:S(2)}) collective-permute-start(bf16[6,96,128]{2,1,0:T(8,128)(2,1)S(1)} %collective-permute-done.10.rest_1_), channel_id=1, source_target_pairs={{0,8},{8,0},{16,24},{24,16},{1,9},{9,1},{17,25},{25,17},{2,10},{10... | collective-permute-start | bytes 442376 | tf_op jit(solution)/shard_map/ppermute | solution.py:267
  42.2 4.9 %collective-permute-start.13 = (bf16[6,96,128]{2,1,0:T(8,128)(2,1)S(1)}, bf16[6,96,128]{2,1,0:T(8,128)(2,1)S(1)}, u32[]{:S(2)}, u32[]{:S(2)}) collective-permute-start(bf16[6,96,128]{2,1,0:T(8,128)(2,1)S(1)} %collective-permute-done.12.rest_3_), channel_id=1, source_target_pairs={{0,8},{8,0},{16,24},{24,16},{1,9},{9,1},{17,25},{25,17},{2,10},{10... | collective-permute-start | bytes 442376 | tf_op jit(solution)/shard_map/ppermute | solution.py:267

commit v7 on v6

--- a/solution.py
+++ b/solution.py
@@ -153,9 +153,12 @@
                 jnp.where(lane < spare, third, fourth),
             )
             for i in range(parts):
-                lines[pair, pl.ds(slot * count + i, width // 4, stride=parts), :] = packed[i]
-        for t in range(count):
-            out_ref[pair, :, t * LANES:(t + 1) * LANES] = lines[pair, pl.ds(t, slots, stride=count), :].astype(jnp.bfloat16)
+                lines[pair // 2, pl.ds((pair % 2 * slots + slot) * count + i, width // 4, stride=parts), :] = packed[i]
+        if pair % 2:
+            for t in range(count):
+                both = lines[pair // 2, pl.ds(t, 2 * slots, stride=count), :].astype(jnp.bfloat16)
+                out_ref[pair - 1, :, t * LANES:(t + 1) * LANES] = both[:slots]
+                out_ref[pair, :, t * LANES:(t + 1) * LANES] = both[slots:]
 
 
 def close(kept, blocks, total, spread, tiles, width, shape):
@@ -168,7 +171,7 @@
         scratch_shapes=[
             pltpu.VMEM((tiles, LANES, LANES), jnp.bfloat16),
             pltpu.VMEM((rows, width, LANES), jnp.float32),
-            pltpu.VMEM((shape[0], shape[1] * shape[2] // LANES, LANES), jnp.float32),
+            pltpu.VMEM((shape[0] // 2, 2 * shape[1] * shape[2] // LANES, LANES), jnp.float32),
         ],
         compiler_params=pltpu.CompilerParams(vmem_limit_bytes=16 << 20),
         cost_estimate=pl.CostEstimate(flops=rows, bytes_accessed=rows, transcendentals=0),
@@ -186,11 +189,13 @@
     lane = lax.broadcasted_iota(jnp.int32, (width // 4, LANES), 1)
     foot = jnp.zeros((spare, LANES), jnp.bfloat16)
     for pair in range(pairs):
-        for t in range(length):
-            lines[pair, pl.ds(t, slots, stride=length), :] = flat_ref[pair, :, t * LANES:(t + 1) * LANES].astype(jnp.float32)
+        for t in range(length if pair % 2 == 0 else 0):
+            lanes = slice(t * LANES, (t + 1) * LANES)
+            both = [flat_ref[pair + i, :, lanes].astype(jnp.float32) for i in range(2)]
+            lines[pair // 2, pl.ds(t, 2 * slots, stride=length), :] = jnp.concatenate(both, axis=0)
         for slot in range(slots):
             r = pair * slots + slot
-            first, second, third = (lines[pair, pl.ds(slot * length + i, width // 4, stride=parts), :] for i in range(parts))
+            first, second, third = (lines[pair // 2, pl.ds((pair % 2 * slots + slot) * length + i, width // 4, stride=parts), :] for i in range(parts))
             quarters = (
                 first,
                 jnp.where(lane < spare, pltpu.roll(first, spare, 1), pltpu.roll(second, spare, 1)),
@@ -220,7 +225,7 @@
         in_specs=[SMEM, VMEM, VMEM],
         out_specs=(VMEM, VMEM),
         scratch_shapes=[
-            pltpu.VMEM((pairs, slots * flat // LANES, LANES), jnp.float32),
+            pltpu.VMEM((pairs // 2, 2 * slots * flat // LANES, LANES), jnp.float32),
             pltpu.VMEM((rows, width, LANES), jnp.float32),
             pltpu.VMEM((tiles, width, LANES), jnp.float32),
         ],

time: 53.5 us -> 52.9 us (0.989)
  Pallas kernels: 21.1 us -> 20.2 us
    ppermute x7, waiting for transfers between devices: 3.58 us -> 2.57 us  [to_tile(): return lax.ppermute(array, 'tile', [(i, i ^ flip) for i in range(tiles)])]
    all_to_all x1, waiting for transfers between devices: 4.58 us -> 5.57 us  [on_device(): lax.all_to_all(shares, ALL, split_axis=0, concat_axis=0, tiled=True)]
    pallas_call x4, Pallas kernels: 15 us -> 14 us  [ladder(): pl.pallas_call(functools.partial(ladder_kernel, near, tiles, width, len(c...]
  transfers between devices with their start and end apart: 16 -> 16, of which waited for: 3 -> 3; matrix products, arithmetic and copies ran while one was open for 3% -> 3% of each run, Pallas kernels for 30% -> 28%
where the time goes in v7:
time: 52.9 us; the launch traced here: 52.5 us
  starting transfers between devices  22.4 us (42%)
  Pallas kernels  20.2 us (38%)
  waiting for transfers between devices  8.16 us (15%)
  local copies, waits for them, and re-layouts  1.44 us (3%)
    pallas_call x4, Pallas kernels, ladder(): pl.pallas_call(functools.partial(ladder_kernel, near, tiles, width, len(c...  14 us
    ppermute x7, starting transfers between devices, to_tile(): return lax.ppermute(array, 'tile', [(i, i ^ flip) for i in range(tiles)])  10.8 us
    all_to_all x1, starting transfers between devices, on_device(): lax.all_to_all(shares, ALL, split_axis=0, concat_axis=0, tiled=True)  7.3 us
    all_to_all x1, waiting for transfers between devices, on_device(): lax.all_to_all(shares, ALL, split_axis=0, concat_axis=0, tiled=True)  5.57 us
    pallas_call x1, Pallas kernels, prepare(): pl.pallas_call(functools.partial(prepare_kernel, tiles, width), out_shape...  3.03 us
    all_to_all x1, starting transfers between devices, on_device(): lax.all_to_all(hidden, ALL, split_axis=0, concat_axis=0, tiled=True)  2.58 us
    ppermute x7, waiting for transfers between devices, to_tile(): return lax.ppermute(array, 'tile', [(i, i ^ flip) for i in range(tiles)])  2.57 us
    pallas_call x1, Pallas kernels, close(): pl.pallas_call(functools.partial(close_kernel, tiles, width), out_shape=j...  2.24 us
  transfers between devices with their start and end apart: 16, of which 3 were waited for; matrix products, arithmetic and copies ran while one was open for 3% of the time, Pallas kernels for 28%

profile of v7, /device:TPU:0, one launch (start us, length us, event | category | flops | bytes accessed | tf_op | source)
XLA Modules:
  0.0 52.5 jit_solution(171284403957166264)
XLA Ops:
  0.0 3.0 %shard_map.55 = (bf16[32,128,128]{2,1,0:T(8,128)(2,1)}, f32[32,24,128]{2,1,0:T(8,128)}) custom-call(s32[4,8]{1,0:T(4,128)} %bitcast.10, bf16[1,8]{1,0:T(2,128)(2,1)} %bitcast.19, bf16[8,4,9216]{2,1,0:T(4,128)(2,1)} %flat_ref.1), custom_call_target="tpu_custom_call" | custom-call | flops 32 | bytes 32 | tf_op jit(solution)/shard_map/pallas_call | solution.py:219
  3.0 7.3 %all-to-all-start = ((f32[32,24,128]{2,1,0:T(8,128)}), f32[32,24,128]{2,1,0:T(8,128)S(1)}, u32[]{:S(2)}, u32[]{:S(2)}) async-start(f32[32,24,128]{2,1,0:T(8,128)} %get-tuple-element.13), calls=%async_computation | async-start | bytes 786432 | tf_op jit(solution)/shard_map/all_to_all | solution.py:276
  10.4 0.0 copy-done.3
  10.4 0.2 copy.9
  10.6 0.0 copy-start.1
  10.7 0.1 maximum_maximum_fusion
  10.8 0.8 %copy.13 = bf16[1,6,96,128]{3,2,1,0:T(8,128)(2,1)} copy(bf16[1,6,96,128]{2,3,1,0:T(8,128)(2,1)S(1)} %constant_dynamic-slice_fusion) | data formatting | bytes 294912
  11.6 2.7 %collective-permute-start.6 = (bf16[6,96,128]{2,1,0:T(8,128)(2,1)}, bf16[6,96,128]{2,1,0:T(8,128)(2,1)S(1)}, u32[]{:S(2)}, u32[]{:S(2)}) collective-permute-start(bf16[6,96,128]{2,1,0:T(8,128)(2,1)} %bitcast.7), channel_id=1, source_target_pairs={{0,4},{1,5},{2,6},{3,7},{4,0},{5,1},{6,2},{7,3},{8,12},{9,13},{10,... | collective-permute-start | bytes 442376 | tf_op jit(solution)/shard_map/ppermute | solution.py:269
  14.3 1.5 %collective-permute-start = (bf16[6,96,128]{2,1,0:T(8,128)(2,1)}, bf16[6,96,128]{2,1,0:T(8,128)(2,1)}, u32[]{:S(2)}, u32[]{:S(2)}) collective-permute-start(bf16[6,96,128]{2,1,0:T(8,128)(2,1)} %bitcast.7), channel_id=1, source_target_pairs={{0,1},{1,0},{2,3},{3,2},{4,5},{5,4},{6,7},{7,6},{8,9},{9,8},{10,11... | collective-permute-start | bytes 442376 | tf_op jit(solution)/shard_map/ppermute | solution.py:269
  15.7 1.5 %collective-permute-start.2 = (bf16[6,96,128]{2,1,0:T(8,128)(2,1)}, bf16[6,96,128]{2,1,0:T(8,128)(2,1)}, u32[]{:S(2)}, u32[]{:S(2)}) collective-permute-start(bf16[6,96,128]{2,1,0:T(8,128)(2,1)} %bitcast.7), channel_id=1, source_target_pairs={{0,2},{1,3},{2,0},{3,1},{4,6},{5,7},{6,4},{7,5},{8,10},{9,11},{10,... | collective-permute-start | bytes 442376 | tf_op jit(solution)/shard_map/ppermute | solution.py:269
  17.3 0.5 collective-permute-start.4
  17.8 1.5 %collective-permute-start.8 = (bf16[6,96,128]{2,1,0:T(8,128)(2,1)}, bf16[6,96,128]{2,1,0:T(8,128)(2,1)}, u32[]{:S(2)}, u32[]{:S(2)}) collective-permute-start(bf16[6,96,128]{2,1,0:T(8,128)(2,1)} %bitcast.7), channel_id=1, source_target_pairs={{0,6},{1,7},{2,4},{3,5},{4,2},{5,3},{6,0},{7,1},{8,14},{9,15},{10,... | collective-permute-start | bytes 442376 | tf_op jit(solution)/shard_map/ppermute | solution.py:269
  19.2 0.2 copy.10
  19.4 0.0 copy-start.2
  19.4 0.2 copy.11
  19.6 1.9 %shard_map.56.rest_0_ = f32[32,96,96]{2,1,0:T(8,128)S(1)} custom-call(s32[4,8]{1,0:T(4,128)S(1)} %bitcast.11, s32[1]{0:T(128)} %bitcast.2.me_ref, bf16[32,128,128]{2,1,0:T(8,128)(2,1)S(1)} %copy-done, bf16[6,96,128]{2,1,0:T(8,128)(2,1)S(1)} %bitcast.8, bf16[6,96,128]{2,1,0:T(8,128)(2,1)S(1)} %bitcast.9), custom_call_target="tpu_custom_call" | custom-call | flops 32 | bytes 32 | tf_op jit(solution)/shard_map/pallas_call | solution.py:111
  21.5 5.6 %all-to-all-done.arrived_ref = f32[32,24,128]{2,1,0:T(8,128)S(1)} async-done(((f32[32,24,128]{2,1,0:T(8,128)}), f32[32,24,128]{2,1,0:T(8,128)S(1)}, u32[]{:S(2)}, u32[]{:S(2)}) %all-to-all-start) | async-done | bytes 393248 | tf_op jit(solution)/shard_map/all_to_all | solution.py:276
  27.1 0.0 copy-done.2
  27.1 0.9 %shard_map.58 = bf16[32,24,128]{2,1,0:T(8,128)(2,1)} custom-call(f32[32,24,128]{2,1,0:T(8,128)S(1)} %all-to-all-done.arrived_ref, bf16[1,96,96]{2,1,0:T(8,128)(2,1)S(1)} %copy-done.2), custom_call_target="tpu_custom_call" | custom-call | flops 1000 | bytes 1000 | tf_op jit(solution)/shard_map/pallas_call | solution.py:249
  28.0 2.6 %all-to-all-start.1 = ((bf16[32,24,128]{2,1,0:T(8,128)(2,1)}), bf16[32,24,128]{2,1,0:T(8,128)(2,1)S(1)}, u32[]{:S(2)}, u32[]{:S(2)}) async-start(bf16[32,24,128]{2,1,0:T(8,128)(2,1)} %shard_map.58), calls=%async_computation.1 | async-start | bytes 393216 | tf_op jit(solution)/shard_map/all_to_all | solution.py:296
  30.6 0.0 collective-permute-done.rest_1_
  30.6 0.2 collective-permute-start.1
  30.8 0.0 collective-permute-done.2.rest_3_
  30.8 0.4 collective-permute-start.3
  31.2 0.0 collective-permute-done.4.rest_5_
  31.2 0.1 collective-permute-start.5
  31.3 0.0 collective-permute-done.6.rest_1_
  31.3 1.7 %collective-permute-start.10 = (bf16[6,96,128]{2,1,0:T(8,128)(2,1)S(1)}, bf16[6,96,128]{2,1,0:T(8,128)(2,1)S(1)}, u32[]{:S(2)}, u32[]{:S(2)}) collective-permute-start(bf16[6,96,128]{2,1,0:T(8,128)(2,1)S(1)} %collective-permute-done.6.rest_1_), channel_id=1, source_target_pairs={{0,1},{1,0},{2,3},{3,2},{4,5},{5,4},{6,7},{7,6},{8,9},{9,8},{10,11... | collective-permute-start | bytes 442376 | tf_op jit(solution)/shard_map/ppermute | solution.py:269
  33.0 1.3 %collective-permute-done.8.rest_3_ = bf16[6,96,128]{2,1,0:T(8,128)(2,1)} collective-permute-done((bf16[6,96,128]{2,1,0:T(8,128)(2,1)}, bf16[6,96,128]{2,1,0:T(8,128)(2,1)}, u32[]{:S(2)}, u32[]{:S(2)}) %collective-permute-start.8) | collective-permute-done | bytes 147488 | tf_op jit(solution)/shard_map/ppermute | solution.py:269
  34.3 1.5 %collective-permute-start.12 = (bf16[6,96,128]{2,1,0:T(8,128)(2,1)}, bf16[6,96,128]{2,1,0:T(8,128)(2,1)S(1)}, u32[]{:S(2)}, u32[]{:S(2)}) collective-permute-start(bf16[6,96,128]{2,1,0:T(8,128)(2,1)} %collective-permute-done.8.rest_3_), channel_id=1, source_target_pairs={{0,1},{1,0},{2,3},{3,2},{4,5},{5,4},{6,7},{7,6},{8,9},{9,8},{10,11... | collective-permute-start | bytes 442376 | tf_op jit(solution)/shard_map/ppermute | solution.py:269
  35.8 0.0 collective-permute-done.1.rest_2_
  35.8 0.0 collective-permute-start.7
  35.8 0.0 collective-permute-done.3.rest_4_
  35.8 0.5 collective-permute-start.9
  36.3 0.0 collective-permute-done.5.rest_6_
  36.3 4.7 %shard_map.57.rest_0_ = f32[32,96,96]{2,1,0:T(8,128)S(1)} custom-call(s32[4,8]{1,0:T(4,128)S(1)} %bitcast.12, s32[1]{0:T(128)} %bitcast.2.me_ref, bf16[32,128,128]{2,1,0:T(8,128)(2,1)S(1)} %copy-done, f32[32,96,96]{2,1,0:T(8,128)S(1)} %shard_map.56.rest_0_, bf16[6,96,128]{2,1,0:T(8,128)(2,1)} %collective-permute-done.rest_1_, ...), custom_call_target="tpu_custom_call", output_to_operand_aliasing={{}: (3, {})} | custom-call | flops 32 | bytes 32 | tf_op jit(solution)/shard_map/pallas_call | solution.py:111
  41.0 0.0 collective-permute-done.10.rest_1_
  41.0 1.2 %collective-permute-done.12.rest_3_ = bf16[6,96,128]{2,1,0:T(8,128)(2,1)S(1)} collective-permute-done((bf16[6,96,128]{2,1,0:T(8,128)(2,1)}, bf16[6,96,128]{2,1,0:T(8,128)(2,1)S(1)}, u32[]{:S(2)}, u32[]{:S(2)}) %collective-permute-start.12) | collective-permute-done | bytes 147488 | tf_op jit(solution)/shard_map/ppermute | solution.py:269
  42.2 0.0 collective-permute-start.11
  42.2 0.5 collective-permute-start.13
  42.7 0.0 collective-permute-done.7.rest_2_
  42.7 0.0 collective-permute-done.9.rest_4_
  42.7 3.4 %shard_map.59.rest_0_ = f32[32,96,96]{2,1,0:T(8,128)S(1)} custom-call(s32[4,8]{1,0:T(4,128)S(1)} %bitcast.13, s32[1]{0:T(128)} %bitcast.2.me_ref, bf16[32,128,128]{2,1,0:T(8,128)(2,1)S(1)} %copy-done, f32[32,96,96]{2,1,0:T(8,128)S(1)} %shard_map.57.rest_0_, bf16[6,96,128]{2,1,0:T(8,128)(2,1)S(1)} %collective-permute-done.6.rest_1_, ...), custom_call_target="tpu_custom_call", output_to_operand_aliasing={{}: (3, {})} | custom-call | flops 32 | bytes 32 | tf_op jit(solution)/shard_map/pallas_call | solution.py:111
  46.1 0.0 collective-permute-done.11.rest_2_
  46.1 0.0 collective-permute-done.13.rest_4_
  46.2 4.0 %shard_map.60.total_ref = f32[32,96,96]{2,1,0:T(8,128)S(1)} custom-call(s32[4,8]{1,0:T(4,128)S(1)} %bitcast.14, s32[1]{0:T(128)} %bitcast.2.me_ref, bf16[32,128,128]{2,1,0:T(8,128)(2,1)S(1)} %copy-done, f32[32,96,96]{2,1,0:T(8,128)S(1)} %shard_map.59.rest_0_, ...), custom_call_target="tpu_custom_call", output_to_operand_aliasing={{}: (3, {})} | custom-call | flops 32 | bytes 32 | tf_op jit(solution)/shard_map/pallas_call | solution.py:111
  50.2 0.0 all-to-all-done.1.spread_ref
  50.2 2.2 %shard_map.61 = bf16[8,4,9216]{2,1,0:T(4,128)(2,1)} custom-call(s32[4,8]{1,0:T(4,128)S(1)} %bitcast.15, bf16[32,128,128]{2,1,0:T(8,128)(2,1)S(1)} %copy-done, f32[32,96,96]{2,1,0:T(8,128)S(1)} %shard_map.60.total_ref, bf16[32,24,128]{2,1,0:T(8,128)(2,1)S(1)} %all-to-all-done.1.spread_ref), custom_call_target="tpu_custom_call" | custom-call | flops 32 | bytes 32 | tf_op jit(solution)/shard_map/pallas_call | solution.py:166
  (8 shorter events, 0.1 us)
Async XLA Ops:
  0.0 10.4 %copy-start.3 = (bf16[1,16,96,96]{3,2,1,0:T(8,128)(2,1)S(1)}, bf16[1,16,96,96]{3,2,1,0:T(8,128)(2,1)}, u32[]{:S(2)}) copy-start(bf16[1,16,96,96]{3,2,1,0:T(8,128)(2,1)} %param.8) | copy-start | bytes 884740
  3.0 24.1 %all-to-all-start = ((f32[32,24,128]{2,1,0:T(8,128)}), f32[32,24,128]{2,1,0:T(8,128)S(1)}, u32[]{:S(2)}, u32[]{:S(2)}) async-start(f32[32,24,128]{2,1,0:T(8,128)} %get-tuple-element.13), calls=%async_computation | async-start | bytes 786432 | tf_op jit(solution)/shard_map/all_to_all | solution.py:276
  10.6 9.0 %copy-start = (bf16[32,128,128]{2,1,0:T(8,128)(2,1)S(1)}, bf16[32,128,128]{2,1,0:T(8,128)(2,1)}, u32[]{:S(2)}) copy-start(bf16[32,128,128]{2,1,0:T(8,128)(2,1)} %get-tuple-element.12.blocks_ref) | copy-start | bytes 3145732
  10.6 9.0 %copy-start.1 = (s32[8,4]{0,1:T(4,128)S(1)}, s32[8,4]{0,1:T(4,128)}, u32[]{:S(2)}) copy-start(s32[8,4]{0,1:T(4,128)} %param.6) | copy-start | bytes 388
  11.6 19.7 %collective-permute-start.6 = (bf16[6,96,128]{2,1,0:T(8,128)(2,1)}, bf16[6,96,128]{2,1,0:T(8,128)(2,1)S(1)}, u32[]{:S(2)}, u32[]{:S(2)}) collective-permute-start(bf16[6,96,128]{2,1,0:T(8,128)(2,1)} %bitcast.7), channel_id=1, source_target_pairs={{0,4},{1,5},{2,6},{3,7},{4,0},{5,1},{6,2},{7,3},{8,12},{9,13},{10,... | collective-permute-start | bytes 442376 | tf_op jit(solution)/shard_map/ppermute | solution.py:269
  14.3 16.3 %collective-permute-start = (bf16[6,96,128]{2,1,0:T(8,128)(2,1)}, bf16[6,96,128]{2,1,0:T(8,128)(2,1)}, u32[]{:S(2)}, u32[]{:S(2)}) collective-permute-start(bf16[6,96,128]{2,1,0:T(8,128)(2,1)} %bitcast.7), channel_id=1, source_target_pairs={{0,1},{1,0},{2,3},{3,2},{4,5},{5,4},{6,7},{7,6},{8,9},{9,8},{10,11... | collective-permute-start | bytes 442376 | tf_op jit(solution)/shard_map/ppermute | solution.py:269
  15.7 15.0 %collective-permute-start.2 = (bf16[6,96,128]{2,1,0:T(8,128)(2,1)}, bf16[6,96,128]{2,1,0:T(8,128)(2,1)}, u32[]{:S(2)}, u32[]{:S(2)}) collective-permute-start(bf16[6,96,128]{2,1,0:T(8,128)(2,1)} %bitcast.7), channel_id=1, source_target_pairs={{0,2},{1,3},{2,0},{3,1},{4,6},{5,7},{6,4},{7,5},{8,10},{9,11},{10,... | collective-permute-start | bytes 442376 | tf_op jit(solution)/shard_map/ppermute | solution.py:269
  17.3 13.9 %collective-permute-start.4 = (bf16[6,96,128]{2,1,0:T(8,128)(2,1)}, bf16[6,96,128]{2,1,0:T(8,128)(2,1)}, u32[]{:S(2)}, u32[]{:S(2)}) collective-permute-start(bf16[6,96,128]{2,1,0:T(8,128)(2,1)} %bitcast.7), channel_id=1, source_target_pairs={{0,3},{1,2},{2,1},{3,0},{4,7},{5,6},{6,5},{7,4},{8,11},{9,10},{10,... | collective-permute-start | bytes 442376 | tf_op jit(solution)/shard_map/ppermute | solution.py:269
  17.8 16.5 %collective-permute-start.8 = (bf16[6,96,128]{2,1,0:T(8,128)(2,1)}, bf16[6,96,128]{2,1,0:T(8,128)(2,1)}, u32[]{:S(2)}, u32[]{:S(2)}) collective-permute-start(bf16[6,96,128]{2,1,0:T(8,128)(2,1)} %bitcast.7), channel_id=1, source_target_pairs={{0,6},{1,7},{2,4},{3,5},{4,2},{5,3},{6,0},{7,1},{8,14},{9,15},{10,... | collective-permute-start | bytes 442376 | tf_op jit(solution)/shard_map/ppermute | solution.py:269
  19.4 7.7 %copy-start.2 = (bf16[1,96,96]{2,1,0:T(8,128)(2,1)S(1)}, bf16[1,96,96]{2,1,0:T(8,128)(2,1)}, u32[]{:S(2)}) copy-start(bf16[1,96,96]{2,1,0:T(8,128)(2,1)} %integral_ref.1) | copy-start | bytes 55300
  28.0 22.2 %all-to-all-start.1 = ((bf16[32,24,128]{2,1,0:T(8,128)(2,1)}), bf16[32,24,128]{2,1,0:T(8,128)(2,1)S(1)}, u32[]{:S(2)}, u32[]{:S(2)}) async-start(bf16[32,24,128]{2,1,0:T(8,128)(2,1)} %shard_map.58), calls=%async_computation.1 | async-start | bytes 393216 | tf_op jit(solution)/shard_map/all_to_all | solution.py:296
  30.6 5.2 %collective-permute-start.1 = (bf16[6,96,128]{2,1,0:T(8,128)(2,1)}, bf16[6,96,128]{2,1,0:T(8,128)(2,1)S(1)}, u32[]{:S(2)}, u32[]{:S(2)}) collective-permute-start(bf16[6,96,128]{2,1,0:T(8,128)(2,1)} %collective-permute-done.rest_1_), channel_id=1, source_target_pairs={{0,8},{8,0},{16,24},{24,16},{1,9},{9,1},{17,25},{25,17},{2,10},{10... | collective-permute-start | bytes 442376 | tf_op jit(solution)/shard_map/ppermute | solution.py:272
  30.8 5.0 %collective-permute-start.3 = (bf16[6,96,128]{2,1,0:T(8,128)(2,1)}, bf16[6,96,128]{2,1,0:T(8,128)(2,1)S(1)}, u32[]{:S(2)}, u32[]{:S(2)}) collective-permute-start(bf16[6,96,128]{2,1,0:T(8,128)(2,1)} %collective-permute-done.2.rest_3_), channel_id=1, source_target_pairs={{0,8},{8,0},{16,24},{24,16},{1,9},{9,1},{17,25},{25,17},{2,10},{10... | collective-permute-start | bytes 442376 | tf_op jit(solution)/shard_map/ppermute | solution.py:272
  31.2 5.1 %collective-permute-start.5 = (bf16[6,96,128]{2,1,0:T(8,128)(2,1)}, bf16[6,96,128]{2,1,0:T(8,128)(2,1)S(1)}, u32[]{:S(2)}, u32[]{:S(2)}) collective-permute-start(bf16[6,96,128]{2,1,0:T(8,128)(2,1)} %collective-permute-done.4.rest_5_), channel_id=1, source_target_pairs={{0,8},{8,0},{16,24},{24,16},{1,9},{9,1},{17,25},{25,17},{2,10},{10... | collective-permute-start | bytes 442376 | tf_op jit(solution)/shard_map/ppermute | solution.py:272
  31.3 9.7 %collective-permute-start.10 = (bf16[6,96,128]{2,1,0:T(8,128)(2,1)S(1)}, bf16[6,96,128]{2,1,0:T(8,128)(2,1)S(1)}, u32[]{:S(2)}, u32[]{:S(2)}) collective-permute-start(bf16[6,96,128]{2,1,0:T(8,128)(2,1)S(1)} %collective-permute-done.6.rest_1_), channel_id=1, source_target_pairs={{0,1},{1,0},{2,3},{3,2},{4,5},{5,4},{6,7},{7,6},{8,9},{9,8},{10,11... | collective-permute-start | bytes 442376 | tf_op jit(solution)/shard_map/ppermute | solution.py:269
  34.3 7.9 %collective-permute-start.12 = (bf16[6,96,128]{2,1,0:T(8,128)(2,1)}, bf16[6,96,128]{2,1,0:T(8,128)(2,1)S(1)}, u32[]{:S(2)}, u32[]{:S(2)}) collective-permute-start(bf16[6,96,128]{2,1,0:T(8,128)(2,1)} %collective-permute-done.8.rest_3_), channel_id=1, source_target_pairs={{0,1},{1,0},{2,3},{3,2},{4,5},{5,4},{6,7},{7,6},{8,9},{9,8},{10,11... | collective-permute-start | bytes 442376 | tf_op jit(solution)/shard_map/ppermute | solution.py:269
  35.8 6.9 %collective-permute-start.7 = (bf16[6,96,128]{2,1,0:T(8,128)(2,1)S(1)}, bf16[6,96,128]{2,1,0:T(8,128)(2,1)S(1)}, u32[]{:S(2)}, u32[]{:S(2)}) collective-permute-start(bf16[6,96,128]{2,1,0:T(8,128)(2,1)S(1)} %collective-permute-done.6.rest_1_), channel_id=1, source_target_pairs={{0,8},{8,0},{16,24},{24,16},{1,9},{9,1},{17,25},{25,17},{2,10},{10... | collective-permute-start | bytes 442376 | tf_op jit(solution)/shard_map/ppermute | solution.py:272
  35.8 6.9 %collective-permute-start.9 = (bf16[6,96,128]{2,1,0:T(8,128)(2,1)}, bf16[6,96,128]{2,1,0:T(8,128)(2,1)S(1)}, u32[]{:S(2)}, u32[]{:S(2)}) collective-permute-start(bf16[6,96,128]{2,1,0:T(8,128)(2,1)} %collective-permute-done.8.rest_3_), channel_id=1, source_target_pairs={{0,8},{8,0},{16,24},{24,16},{1,9},{9,1},{17,25},{25,17},{2,10},{10... | collective-permute-start | bytes 442376 | tf_op jit(solution)/shard_map/ppermute | solution.py:272
  42.2 3.9 %collective-permute-start.11 = (bf16[6,96,128]{2,1,0:T(8,128)(2,1)S(1)}, bf16[6,96,128]{2,1,0:T(8,128)(2,1)S(1)}, u32[]{:S(2)}, u32[]{:S(2)}) collective-permute-start(bf16[6,96,128]{2,1,0:T(8,128)(2,1)S(1)} %collective-permute-done.10.rest_1_), channel_id=1, source_target_pairs={{0,8},{8,0},{16,24},{24,16},{1,9},{9,1},{17,25},{25,17},{2,10},{10... | collective-permute-start | bytes 442376 | tf_op jit(solution)/shard_map/ppermute | solution.py:272
  42.2 3.9 %collective-permute-start.13 = (bf16[6,96,128]{2,1,0:T(8,128)(2,1)S(1)}, bf16[6,96,128]{2,1,0:T(8,128)(2,1)S(1)}, u32[]{:S(2)}, u32[]{:S(2)}) collective-permute-start(bf16[6,96,128]{2,1,0:T(8,128)(2,1)S(1)} %collective-permute-done.12.rest_3_), channel_id=1, source_target_pairs={{0,8},{8,0},{16,24},{24,16},{1,9},{9,1},{17,25},{25,17},{2,10},{10... | collective-permute-start | bytes 442376 | tf_op jit(solution)/shard_map/ppermute | solution.py:272

commit v8 on v7

--- a/solution.py
+++ b/solution.py
@@ -288,7 +288,7 @@
 
     total = stage((0,), None)
     first = total
-    far = mine
+    far, _ = lax.optimization_barrier((mine, shares))
     for up in range(half, tiles, across):
         halves[up] = to_tile(far, up)
     arrived, _ = lax.optimization_barrier((arrived, first))

time: 52.9 us -> 53.9 us (1.019)
  Pallas kernels: 20.2 us -> 22.1 us
  waiting for transfers between devices: 8.16 us -> 6.93 us
    all_to_all x1, waiting for transfers between devices: 5.57 us -> 1.38 us  [on_device(): lax.all_to_all(shares, ALL, split_axis=0, concat_axis=0, tiled=True)]
    ppermute x7, waiting for transfers between devices: 2.57 us -> 5.53 us  [to_tile(): return lax.ppermute(array, 'tile', [(i, i ^ flip) for i in range(tiles)])]
    pallas_call x4, Pallas kernels: 14 us -> 16 us  [ladder(): pl.pallas_call(functools.partial(ladder_kernel, near, tiles, width, len(c...]
    ppermute x7, starting transfers between devices: 10.8 us -> 9.69 us  [to_tile(): return lax.ppermute(array, 'tile', [(i, i ^ flip) for i in range(tiles)])]
    all_to_all x1, starting transfers between devices: 2.58 us -> 3.21 us  [on_device(): lax.all_to_all(hidden, ALL, split_axis=0, concat_axis=0, tiled=True)]
    ppermute x7, starting transfers between devices: 1.71 us -> 2.29 us  [to_core(): return lax.ppermute(array, 'grp', [(i, i ^ 1) for i in range(groups)])]
  transfers between devices with their start and end apart: 16 -> 16, of which waited for: 3 -> 3; matrix products, arithmetic and copies ran while one was open for 3% -> 3% of each run, Pallas kernels for 28% -> 32%
where the time goes in v8:
time: 53.9 us; the launch traced here: 53.3 us
  starting transfers between devices  22.5 us (42%)
  Pallas kernels  22.1 us (41%)
  waiting for transfers between devices  6.93 us (13%)
  local copies, waits for them, and re-layouts  1.44 us (3%)
    pallas_call x4, Pallas kernels, ladder(): pl.pallas_call(functools.partial(ladder_kernel, near, tiles, width, len(c...  16 us
    ppermute x7, starting transfers between devices, to_tile(): return lax.ppermute(array, 'tile', [(i, i ^ flip) for i in range(tiles)])  9.69 us
    all_to_all x1, starting transfers between devices, on_device(): lax.all_to_all(shares, ALL, split_axis=0, concat_axis=0, tiled=True)  7.3 us
    ppermute x7, waiting for transfers between devices, to_tile(): return lax.ppermute(array, 'tile', [(i, i ^ flip) for i in range(tiles)])  5.53 us
    all_to_all x1, starting transfers between devices, on_device(): lax.all_to_all(hidden, ALL, split_axis=0, concat_axis=0, tiled=True)  3.21 us
    pallas_call x1, Pallas kernels, prepare(): pl.pallas_call(functools.partial(prepare_kernel, tiles, width), out_shape...  3.03 us
    ppermute x7, starting transfers between devices, to_core(): return lax.ppermute(array, 'grp', [(i, i ^ 1) for i in range(groups)])  2.29 us
    pallas_call x1, Pallas kernels, close(): pl.pallas_call(functools.partial(close_kernel, tiles, width), out_shape=j...  2.24 us
  transfers between devices with their start and end apart: 16, of which 3 were waited for; matrix products, arithmetic and copies ran while one was open for 3% of the time, Pallas kernels for 32%

profile of v8, /device:TPU:0, one launch (start us, length us, event | category | flops | bytes accessed | tf_op | source)
XLA Modules:
  0.0 53.3 jit_solution(9085686521765667440)
XLA Ops:
  0.0 3.0 %shard_map.55 = (bf16[32,128,128]{2,1,0:T(8,128)(2,1)}, f32[32,24,128]{2,1,0:T(8,128)}) custom-call(s32[4,8]{1,0:T(4,128)} %bitcast.10, bf16[1,8]{1,0:T(2,128)(2,1)} %bitcast.19, bf16[8,4,9216]{2,1,0:T(4,128)(2,1)} %flat_ref.1), custom_call_target="tpu_custom_call" | custom-call | flops 32 | bytes 32 | tf_op jit(solution)/shard_map/pallas_call | solution.py:219
  3.0 7.3 %all-to-all-start = ((f32[32,24,128]{2,1,0:T(8,128)}), f32[32,24,128]{2,1,0:T(8,128)S(1)}, u32[]{:S(2)}, u32[]{:S(2)}) async-start(f32[32,24,128]{2,1,0:T(8,128)} %get-tuple-element.14), calls=%async_computation | async-start | bytes 786432 | tf_op jit(solution)/shard_map/all_to_all | solution.py:276
  10.4 0.0 copy-done.3
  10.4 0.2 copy.9
  10.6 0.0 copy-start.1
  10.7 0.1 maximum_maximum_fusion
  10.8 0.8 %copy.13 = bf16[1,6,96,128]{3,2,1,0:T(8,128)(2,1)} copy(bf16[1,6,96,128]{2,3,1,0:T(8,128)(2,1)S(1)} %constant_dynamic-slice_fusion) | data formatting | bytes 294912
  11.6 1.8 %collective-permute-start = (bf16[6,96,128]{2,1,0:T(8,128)(2,1)}, bf16[6,96,128]{2,1,0:T(8,128)(2,1)}, u32[]{:S(2)}, u32[]{:S(2)}) collective-permute-start(bf16[6,96,128]{2,1,0:T(8,128)(2,1)} %bitcast.7), channel_id=1, source_target_pairs={{0,1},{1,0},{2,3},{3,2},{4,5},{5,4},{6,7},{7,6},{8,9},{9,8},{10,11... | collective-permute-start | bytes 442376 | tf_op jit(solution)/shard_map/ppermute | solution.py:269
  13.4 1.5 %collective-permute-start.2 = (bf16[6,96,128]{2,1,0:T(8,128)(2,1)}, bf16[6,96,128]{2,1,0:T(8,128)(2,1)}, u32[]{:S(2)}, u32[]{:S(2)}) collective-permute-start(bf16[6,96,128]{2,1,0:T(8,128)(2,1)} %bitcast.7), channel_id=1, source_target_pairs={{0,2},{1,3},{2,0},{3,1},{4,6},{5,7},{6,4},{7,5},{8,10},{9,11},{10,... | collective-permute-start | bytes 442376 | tf_op jit(solution)/shard_map/ppermute | solution.py:269
  14.8 0.3 collective-permute-start.4
  15.1 2.7 %collective-permute-start.6 = (bf16[6,96,128]{2,1,0:T(8,128)(2,1)}, bf16[6,96,128]{2,1,0:T(8,128)(2,1)S(1)}, u32[]{:S(2)}, u32[]{:S(2)}) collective-permute-start(bf16[6,96,128]{2,1,0:T(8,128)(2,1)} %bitcast.7), channel_id=1, source_target_pairs={{0,4},{1,5},{2,6},{3,7},{4,0},{5,1},{6,2},{7,3},{8,12},{9,13},{10,... | collective-permute-start | bytes 442376 | tf_op jit(solution)/shard_map/ppermute | solution.py:269
  17.8 1.5 %collective-permute-start.8 = (bf16[6,96,128]{2,1,0:T(8,128)(2,1)}, bf16[6,96,128]{2,1,0:T(8,128)(2,1)}, u32[]{:S(2)}, u32[]{:S(2)}) collective-permute-start(bf16[6,96,128]{2,1,0:T(8,128)(2,1)} %bitcast.7), channel_id=1, source_target_pairs={{0,6},{1,7},{2,4},{3,5},{4,2},{5,3},{6,0},{7,1},{8,14},{9,15},{10,... | collective-permute-start | bytes 442376 | tf_op jit(solution)/shard_map/ppermute | solution.py:269
  19.2 0.2 copy.10
  19.4 0.0 copy-start.2
  19.4 0.2 copy.11
  19.6 0.0 copy-done
  19.6 2.9 %shard_map.56.rest_0_ = f32[32,96,96]{2,1,0:T(8,128)S(1)} custom-call(s32[4,8]{1,0:T(4,128)S(1)} %bitcast.11, s32[1]{0:T(128)} %bitcast.2.me_ref, bf16[32,128,128]{2,1,0:T(8,128)(2,1)S(1)} %copy-done, bf16[6,96,128]{2,1,0:T(8,128)(2,1)S(1)} %bitcast.8, bf16[6,96,128]{2,1,0:T(8,128)(2,1)S(1)} %bitcast.9), custom_call_target="tpu_custom_call" | custom-call | flops 32 | bytes 32 | tf_op jit(solution)/shard_map/pallas_call | solution.py:111
  22.5 1.4 %all-to-all-done.arrived_ref = f32[32,24,128]{2,1,0:T(8,128)S(1)} async-done(((f32[32,24,128]{2,1,0:T(8,128)}), f32[32,24,128]{2,1,0:T(8,128)S(1)}, u32[]{:S(2)}, u32[]{:S(2)}) %all-to-all-start) | async-done | bytes 393248 | tf_op jit(solution)/shard_map/all_to_all | solution.py:276
  23.9 0.9 %shard_map.58 = bf16[32,24,128]{2,1,0:T(8,128)(2,1)} custom-call(f32[32,24,128]{2,1,0:T(8,128)S(1)} %all-to-all-done.arrived_ref, bf16[1,96,96]{2,1,0:T(8,128)(2,1)S(1)} %copy-done.2), custom_call_target="tpu_custom_call" | custom-call | flops 1000 | bytes 1000 | tf_op jit(solution)/shard_map/pallas_call | solution.py:249
  24.8 3.2 %all-to-all-start.1 = ((bf16[32,24,128]{2,1,0:T(8,128)(2,1)}), bf16[32,24,128]{2,1,0:T(8,128)(2,1)S(1)}, u32[]{:S(2)}, u32[]{:S(2)}) async-start(bf16[32,24,128]{2,1,0:T(8,128)(2,1)} %shard_map.58), calls=%async_computation.1 | async-start | bytes 393216 | tf_op jit(solution)/shard_map/all_to_all | solution.py:296
  28.0 0.0 collective-permute-done.rest_1_
  28.0 0.3 collective-permute-start.1
  28.3 0.0 collective-permute-done.2.rest_3_
  28.3 0.3 collective-permute-start.3
  28.6 1.4 %collective-permute-done.4.rest_5_ = bf16[6,96,128]{2,1,0:T(8,128)(2,1)} collective-permute-done((bf16[6,96,128]{2,1,0:T(8,128)(2,1)}, bf16[6,96,128]{2,1,0:T(8,128)(2,1)}, u32[]{:S(2)}, u32[]{:S(2)}) %collective-permute-start.4) | collective-permute-done | bytes 147488 | tf_op jit(solution)/shard_map/ppermute | solution.py:269
  30.0 0.0 collective-permute-start.5
  30.0 0.0 collective-permute-done.6.rest_1_
  30.0 0.6 %collective-permute-start.10 = (bf16[6,96,128]{2,1,0:T(8,128)(2,1)S(1)}, bf16[6,96,128]{2,1,0:T(8,128)(2,1)S(1)}, u32[]{:S(2)}, u32[]{:S(2)}) collective-permute-start(bf16[6,96,128]{2,1,0:T(8,128)(2,1)S(1)} %collective-permute-done.6.rest_1_), channel_id=1, source_target_pairs={{0,1},{1,0},{2,3},{3,2},{4,5},{5,4},{6,7},{7,6},{8,9},{9,8},{10,11... | collective-permute-start | bytes 442376 | tf_op jit(solution)/shard_map/ppermute | solution.py:269
  30.6 4.1 %collective-permute-done.8.rest_3_ = bf16[6,96,128]{2,1,0:T(8,128)(2,1)} collective-permute-done((bf16[6,96,128]{2,1,0:T(8,128)(2,1)}, bf16[6,96,128]{2,1,0:T(8,128)(2,1)}, u32[]{:S(2)}, u32[]{:S(2)}) %collective-permute-start.8) | collective-permute-done | bytes 147488 | tf_op jit(solution)/shard_map/ppermute | solution.py:269
  34.7 1.5 %collective-permute-start.12 = (bf16[6,96,128]{2,1,0:T(8,128)(2,1)}, bf16[6,96,128]{2,1,0:T(8,128)(2,1)S(1)}, u32[]{:S(2)}, u32[]{:S(2)}) collective-permute-start(bf16[6,96,128]{2,1,0:T(8,128)(2,1)} %collective-permute-done.8.rest_3_), channel_id=1, source_target_pairs={{0,1},{1,0},{2,3},{3,2},{4,5},{5,4},{6,7},{7,6},{8,9},{9,8},{10,11... | collective-permute-start | bytes 442376 | tf_op jit(solution)/shard_map/ppermute | solution.py:269
  36.2 0.0 collective-permute-done.1.rest_2_
  36.2 0.0 collective-permute-start.7
  36.2 0.0 collective-permute-done.3.rest_4_
  36.2 0.5 collective-permute-start.9
  36.7 0.0 collective-permute-done.5.rest_6_
  36.7 4.6 %shard_map.57.rest_0_ = f32[32,96,96]{2,1,0:T(8,128)S(1)} custom-call(s32[4,8]{1,0:T(4,128)S(1)} %bitcast.12, s32[1]{0:T(128)} %bitcast.2.me_ref, bf16[32,128,128]{2,1,0:T(8,128)(2,1)S(1)} %copy-done, f32[32,96,96]{2,1,0:T(8,128)S(1)} %shard_map.56.rest_0_, bf16[6,96,128]{2,1,0:T(8,128)(2,1)} %collective-permute-done.rest_1_, ...), custom_call_target="tpu_custom_call", output_to_operand_aliasing={{}: (3, {})} | custom-call | flops 32 | bytes 32 | tf_op jit(solution)/shard_map/pallas_call | solution.py:111
  41.4 0.0 collective-permute-done.10.rest_1_
  41.4 0.0 collective-permute-done.12.rest_3_
  41.4 1.1 %collective-permute-start.11 = (bf16[6,96,128]{2,1,0:T(8,128)(2,1)S(1)}, bf16[6,96,128]{2,1,0:T(8,128)(2,1)S(1)}, u32[]{:S(2)}, u32[]{:S(2)}) collective-permute-start(bf16[6,96,128]{2,1,0:T(8,128)(2,1)S(1)} %collective-permute-done.10.rest_1_), channel_id=1, source_target_pairs={{0,8},{8,0},{16,24},{24,16},{1,9},{9,1},{17,25},{25,17},{2,10},{10... | collective-permute-start | bytes 442376 | tf_op jit(solution)/shard_map/ppermute | solution.py:272
  42.5 0.1 collective-permute-start.13
  42.6 0.0 collective-permute-done.7.rest_2_
  42.6 0.0 collective-permute-done.9.rest_4_
  42.6 3.4 %shard_map.59.rest_0_ = f32[32,96,96]{2,1,0:T(8,128)S(1)} custom-call(s32[4,8]{1,0:T(4,128)S(1)} %bitcast.13, s32[1]{0:T(128)} %bitcast.2.me_ref, bf16[32,128,128]{2,1,0:T(8,128)(2,1)S(1)} %copy-done, f32[32,96,96]{2,1,0:T(8,128)S(1)} %shard_map.57.rest_0_, bf16[6,96,128]{2,1,0:T(8,128)(2,1)S(1)} %collective-permute-done.6.rest_1_, ...), custom_call_target="tpu_custom_call", output_to_operand_aliasing={{}: (3, {})} | custom-call | flops 32 | bytes 32 | tf_op jit(solution)/shard_map/pallas_call | solution.py:111
  46.0 0.0 collective-permute-done.11.rest_2_
  46.0 0.0 collective-permute-done.13.rest_4_
  46.0 5.0 %shard_map.60.total_ref = f32[32,96,96]{2,1,0:T(8,128)S(1)} custom-call(s32[4,8]{1,0:T(4,128)S(1)} %bitcast.14, s32[1]{0:T(128)} %bitcast.2.me_ref, bf16[32,128,128]{2,1,0:T(8,128)(2,1)S(1)} %copy-done, f32[32,96,96]{2,1,0:T(8,128)S(1)} %shard_map.59.rest_0_, ...), custom_call_target="tpu_custom_call", output_to_operand_aliasing={{}: (3, {})} | custom-call | flops 32 | bytes 32 | tf_op jit(solution)/shard_map/pallas_call | solution.py:111
  51.0 0.0 all-to-all-done.1.spread_ref
  51.0 2.2 %shard_map.61 = bf16[8,4,9216]{2,1,0:T(4,128)(2,1)} custom-call(s32[4,8]{1,0:T(4,128)S(1)} %bitcast.15, bf16[32,128,128]{2,1,0:T(8,128)(2,1)S(1)} %copy-done, f32[32,96,96]{2,1,0:T(8,128)S(1)} %shard_map.60.total_ref, bf16[32,24,128]{2,1,0:T(8,128)(2,1)S(1)} %all-to-all-done.1.spread_ref), custom_call_target="tpu_custom_call" | custom-call | flops 32 | bytes 32 | tf_op jit(solution)/shard_map/pallas_call | solution.py:166
  (8 shorter events, 0.1 us)
Async XLA Ops:
  0.0 10.4 %copy-start.3 = (bf16[1,16,96,96]{3,2,1,0:T(8,128)(2,1)S(1)}, bf16[1,16,96,96]{3,2,1,0:T(8,128)(2,1)}, u32[]{:S(2)}) copy-start(bf16[1,16,96,96]{3,2,1,0:T(8,128)(2,1)} %param.8) | copy-start | bytes 884740
  3.0 20.9 %all-to-all-start = ((f32[32,24,128]{2,1,0:T(8,128)}), f32[32,24,128]{2,1,0:T(8,128)S(1)}, u32[]{:S(2)}, u32[]{:S(2)}) async-start(f32[32,24,128]{2,1,0:T(8,128)} %get-tuple-element.14), calls=%async_computation | async-start | bytes 786432 | tf_op jit(solution)/shard_map/all_to_all | solution.py:276
  10.6 9.0 %copy-start = (bf16[32,128,128]{2,1,0:T(8,128)(2,1)S(1)}, bf16[32,128,128]{2,1,0:T(8,128)(2,1)}, u32[]{:S(2)}) copy-start(bf16[32,128,128]{2,1,0:T(8,128)(2,1)} %get-tuple-element.13.blocks_ref) | copy-start | bytes 3145732
  10.6 9.0 %copy-start.1 = (s32[8,4]{0,1:T(4,128)S(1)}, s32[8,4]{0,1:T(4,128)}, u32[]{:S(2)}) copy-start(s32[8,4]{0,1:T(4,128)} %param.6) | copy-start | bytes 388
  11.6 16.4 %collective-permute-start = (bf16[6,96,128]{2,1,0:T(8,128)(2,1)}, bf16[6,96,128]{2,1,0:T(8,128)(2,1)}, u32[]{:S(2)}, u32[]{:S(2)}) collective-permute-start(bf16[6,96,128]{2,1,0:T(8,128)(2,1)} %bitcast.7), channel_id=1, source_target_pairs={{0,1},{1,0},{2,3},{3,2},{4,5},{5,4},{6,7},{7,6},{8,9},{9,8},{10,11... | collective-permute-start | bytes 442376 | tf_op jit(solution)/shard_map/ppermute | solution.py:269
  13.4 15.0 %collective-permute-start.2 = (bf16[6,96,128]{2,1,0:T(8,128)(2,1)}, bf16[6,96,128]{2,1,0:T(8,128)(2,1)}, u32[]{:S(2)}, u32[]{:S(2)}) collective-permute-start(bf16[6,96,128]{2,1,0:T(8,128)(2,1)} %bitcast.7), channel_id=1, source_target_pairs={{0,2},{1,3},{2,0},{3,1},{4,6},{5,7},{6,4},{7,5},{8,10},{9,11},{10,... | collective-permute-start | bytes 442376 | tf_op jit(solution)/shard_map/ppermute | solution.py:269
  14.8 15.2 %collective-permute-start.4 = (bf16[6,96,128]{2,1,0:T(8,128)(2,1)}, bf16[6,96,128]{2,1,0:T(8,128)(2,1)}, u32[]{:S(2)}, u32[]{:S(2)}) collective-permute-start(bf16[6,96,128]{2,1,0:T(8,128)(2,1)} %bitcast.7), channel_id=1, source_target_pairs={{0,3},{1,2},{2,1},{3,0},{4,7},{5,6},{6,5},{7,4},{8,11},{9,10},{10,... | collective-permute-start | bytes 442376 | tf_op jit(solution)/shard_map/ppermute | solution.py:269
  15.1 14.9 %collective-permute-start.6 = (bf16[6,96,128]{2,1,0:T(8,128)(2,1)}, bf16[6,96,128]{2,1,0:T(8,128)(2,1)S(1)}, u32[]{:S(2)}, u32[]{:S(2)}) collective-permute-start(bf16[6,96,128]{2,1,0:T(8,128)(2,1)} %bitcast.7), channel_id=1, source_target_pairs={{0,4},{1,5},{2,6},{3,7},{4,0},{5,1},{6,2},{7,3},{8,12},{9,13},{10,... | collective-permute-start | bytes 442376 | tf_op jit(solution)/shard_map/ppermute | solution.py:269
  17.8 16.9 %collective-permute-start.8 = (bf16[6,96,128]{2,1,0:T(8,128)(2,1)}, bf16[6,96,128]{2,1,0:T(8,128)(2,1)}, u32[]{:S(2)}, u32[]{:S(2)}) collective-permute-start(bf16[6,96,128]{2,1,0:T(8,128)(2,1)} %bitcast.7), channel_id=1, source_target_pairs={{0,6},{1,7},{2,4},{3,5},{4,2},{5,3},{6,0},{7,1},{8,14},{9,15},{10,... | collective-permute-start | bytes 442376 | tf_op jit(solution)/shard_map/ppermute | solution.py:269
  19.4 4.5 %copy-start.2 = (bf16[1,96,96]{2,1,0:T(8,128)(2,1)S(1)}, bf16[1,96,96]{2,1,0:T(8,128)(2,1)}, u32[]{:S(2)}) copy-start(bf16[1,96,96]{2,1,0:T(8,128)(2,1)} %integral_ref.1) | copy-start | bytes 55300
  24.8 26.3 %all-to-all-start.1 = ((bf16[32,24,128]{2,1,0:T(8,128)(2,1)}), bf16[32,24,128]{2,1,0:T(8,128)(2,1)S(1)}, u32[]{:S(2)}, u32[]{:S(2)}) async-start(bf16[32,24,128]{2,1,0:T(8,128)(2,1)} %shard_map.58), calls=%async_computation.1 | async-start | bytes 393216 | tf_op jit(solution)/shard_map/all_to_all | solution.py:296
  28.0 8.2 %collective-permute-start.1 = (bf16[6,96,128]{2,1,0:T(8,128)(2,1)}, bf16[6,96,128]{2,1,0:T(8,128)(2,1)S(1)}, u32[]{:S(2)}, u32[]{:S(2)}) collective-permute-start(bf16[6,96,128]{2,1,0:T(8,128)(2,1)} %collective-permute-done.rest_1_), channel_id=1, source_target_pairs={{0,8},{8,0},{16,24},{24,16},{1,9},{9,1},{17,25},{25,17},{2,10},{10... | collective-permute-start | bytes 442376 | tf_op jit(solution)/shard_map/ppermute | solution.py:272
  28.3 7.9 %collective-permute-start.3 = (bf16[6,96,128]{2,1,0:T(8,128)(2,1)}, bf16[6,96,128]{2,1,0:T(8,128)(2,1)S(1)}, u32[]{:S(2)}, u32[]{:S(2)}) collective-permute-start(bf16[6,96,128]{2,1,0:T(8,128)(2,1)} %collective-permute-done.2.rest_3_), channel_id=1, source_target_pairs={{0,8},{8,0},{16,24},{24,16},{1,9},{9,1},{17,25},{25,17},{2,10},{10... | collective-permute-start | bytes 442376 | tf_op jit(solution)/shard_map/ppermute | solution.py:272
  30.0 6.7 %collective-permute-start.5 = (bf16[6,96,128]{2,1,0:T(8,128)(2,1)}, bf16[6,96,128]{2,1,0:T(8,128)(2,1)S(1)}, u32[]{:S(2)}, u32[]{:S(2)}) collective-permute-start(bf16[6,96,128]{2,1,0:T(8,128)(2,1)} %collective-permute-done.4.rest_5_), channel_id=1, source_target_pairs={{0,8},{8,0},{16,24},{24,16},{1,9},{9,1},{17,25},{25,17},{2,10},{10... | collective-permute-start | bytes 442376 | tf_op jit(solution)/shard_map/ppermute | solution.py:272
  30.0 11.3 %collective-permute-start.10 = (bf16[6,96,128]{2,1,0:T(8,128)(2,1)S(1)}, bf16[6,96,128]{2,1,0:T(8,128)(2,1)S(1)}, u32[]{:S(2)}, u32[]{:S(2)}) collective-permute-start(bf16[6,96,128]{2,1,0:T(8,128)(2,1)S(1)} %collective-permute-done.6.rest_1_), channel_id=1, source_target_pairs={{0,1},{1,0},{2,3},{3,2},{4,5},{5,4},{6,7},{7,6},{8,9},{9,8},{10,11... | collective-permute-start | bytes 442376 | tf_op jit(solution)/shard_map/ppermute | solution.py:269
  34.7 6.7 %collective-permute-start.12 = (bf16[6,96,128]{2,1,0:T(8,128)(2,1)}, bf16[6,96,128]{2,1,0:T(8,128)(2,1)S(1)}, u32[]{:S(2)}, u32[]{:S(2)}) collective-permute-start(bf16[6,96,128]{2,1,0:T(8,128)(2,1)} %collective-permute-done.8.rest_3_), channel_id=1, source_target_pairs={{0,1},{1,0},{2,3},{3,2},{4,5},{5,4},{6,7},{7,6},{8,9},{9,8},{10,11... | collective-permute-start | bytes 442376 | tf_op jit(solution)/shard_map/ppermute | solution.py:269
  36.2 6.4 %collective-permute-start.7 = (bf16[6,96,128]{2,1,0:T(8,128)(2,1)S(1)}, bf16[6,96,128]{2,1,0:T(8,128)(2,1)S(1)}, u32[]{:S(2)}, u32[]{:S(2)}) collective-permute-start(bf16[6,96,128]{2,1,0:T(8,128)(2,1)S(1)} %collective-permute-done.6.rest_1_), channel_id=1, source_target_pairs={{0,8},{8,0},{16,24},{24,16},{1,9},{9,1},{17,25},{25,17},{2,10},{10... | collective-permute-start | bytes 442376 | tf_op jit(solution)/shard_map/ppermute | solution.py:272
  36.2 6.4 %collective-permute-start.9 = (bf16[6,96,128]{2,1,0:T(8,128)(2,1)}, bf16[6,96,128]{2,1,0:T(8,128)(2,1)S(1)}, u32[]{:S(2)}, u32[]{:S(2)}) collective-permute-start(bf16[6,96,128]{2,1,0:T(8,128)(2,1)} %collective-permute-done.8.rest_3_), channel_id=1, source_target_pairs={{0,8},{8,0},{16,24},{24,16},{1,9},{9,1},{17,25},{25,17},{2,10},{10... | collective-permute-start | bytes 442376 | tf_op jit(solution)/shard_map/ppermute | solution.py:272
  41.4 4.6 %collective-permute-start.11 = (bf16[6,96,128]{2,1,0:T(8,128)(2,1)S(1)}, bf16[6,96,128]{2,1,0:T(8,128)(2,1)S(1)}, u32[]{:S(2)}, u32[]{:S(2)}) collective-permute-start(bf16[6,96,128]{2,1,0:T(8,128)(2,1)S(1)} %collective-permute-done.10.rest_1_), channel_id=1, source_target_pairs={{0,8},{8,0},{16,24},{24,16},{1,9},{9,1},{17,25},{25,17},{2,10},{10... | collective-permute-start | bytes 442376 | tf_op jit(solution)/shard_map/ppermute | solution.py:272
  42.5 3.5 %collective-permute-start.13 = (bf16[6,96,128]{2,1,0:T(8,128)(2,1)S(1)}, bf16[6,96,128]{2,1,0:T(8,128)(2,1)S(1)}, u32[]{:S(2)}, u32[]{:S(2)}) collective-permute-start(bf16[6,96,128]{2,1,0:T(8,128)(2,1)S(1)} %collective-permute-done.12.rest_3_), channel_id=1, source_target_pairs={{0,8},{8,0},{16,24},{24,16},{1,9},{9,1},{17,25},{25,17},{2,10},{10... | collective-permute-start | bytes 442376 | tf_op jit(solution)/shard_map/ppermute | solution.py:272
